TPU v7x, 512 devices: a whole 4x8x8 slice. The times are simulated.
512 devices in a mesh: pb: 16 (over z, x_hi), ka: 32 (over x_lo, y, core).
Axes of the slice: x: 4 (x_hi: 2, x_lo: 2; x = x_hi * 2 + x_lo), y: 8, z: 8, core: 2. Of those that a mesh axis runs over, the one named last changes fastest.
Arguments:
- queries: float32 [4096, 256], P(('ka', 'pb')), may hold values from -5 to 5
- key_pair: float32 [32768, 256], P(('pb', 'ka')), may hold values from -5 to 5
- values: float32 [32768, 256], P(('pb', 'ka')), may hold values from -6 to 6
- grad_out: float32 [4096, 256], P(('ka', 'pb')), may hold values from -6 to 6
Outputs:
- attended: float32 [4096, 256], P(('ka', 'pb'))
- grad_queries: float32 [4096, 256], P(('ka', 'pb'))
- grad_keys: float32 [32768, 256], P(('pb', 'ka'))
- grad_values: float32 [32768, 256], P(('pb', 'ka'))
All inputs are finite; a program needn't handle non-finite values.
Results may differ from a plain program's by a relative error of at most 0.0003.
Values sent between devices are 32-bit elements; how exact they have to be, the bound alone decides.
No kernel may reach another device: no remote copies, remote signals or barrier semaphores. Data moves between devices by JAX's collectives and lax.ppermute only.
A program may use at most 64 MiB of HBM per device.

v0:
```python
import jax
import jax.numpy as jnp
from jax import lax
from jax.sharding import PartitionSpec as P

LAMBDA = 0.5


def matmul(left, right):
    return jnp.dot(left, right, precision=lax.Precision.HIGHEST, preferred_element_type=jnp.float32)


def inner(left, right):
    return lax.dot_general(
        left,
        right,
        (((0,), (0,)), ((), ())),
        precision=lax.Precision.HIGHEST,
        preferred_element_type=jnp.float32,
    )


def outer(left, right):
    return lax.dot_general(
        left,
        right,
        (((1,), (1,)), ((), ())),
        precision=lax.Precision.HIGHEST,
        preferred_element_type=jnp.float32,
    )


def per_device(queries, key_pair, values, grad_out):
    half = key_pair.shape[1] // 2
    scale = half ** (-0.5)
    own_rows = queries.shape[0]
    q_all, g_all = (
        lax.all_gather(queries, "pb", axis=0, tiled=True),
        lax.all_gather(grad_out, "pb", axis=0, tiled=True),
    )
    k_all, v_all = (
        lax.all_gather(key_pair, "ka", axis=0, tiled=True),
        lax.all_gather(values, "ka", axis=0, tiled=True),
    )
    first_q = q_all[:, :half]
    second_q = q_all[:, half:]
    first_k = k_all[:, :half]
    second_k = k_all[:, half:]
    score_one = outer(first_q, first_k) * scale
    score_two = outer(second_q, second_k) * scale
    top_one = jnp.max(score_one, axis=1)
    top_two = jnp.max(score_two, axis=1)
    weight_one = jnp.exp(score_one - top_one[:, None])
    weight_two = jnp.exp(score_two - top_two[:, None])
    mass_one = jnp.sum(weight_one, axis=1)
    mass_two = jnp.sum(weight_two, axis=1)
    value_one = matmul(weight_one, v_all)
    value_two = matmul(weight_two, v_all)
    peak_one, peak_two = lax.pmax((top_one, top_two), "pb")
    factor_one = jnp.exp(top_one - peak_one)
    factor_two = jnp.exp(top_two - peak_two)
    total_one, summed_one, total_two, summed_two = lax.psum(
        (
            mass_one * factor_one,
            value_one * factor_one[:, None],
            mass_two * factor_two,
            value_two * factor_two[:, None],
        ),
        "pb",
    )
    attend_one = summed_one / total_one[:, None]
    attend_two = summed_two / total_two[:, None]
    result = attend_one - LAMBDA * attend_two
    start = lax.axis_index("pb") * own_rows
    attended = lax.dynamic_slice_in_dim(result, start, own_rows, 0)
    prob_one = weight_one * (factor_one / total_one)[:, None]
    prob_two = weight_two * (factor_two / total_two)[:, None]
    grad_prob = outer(g_all, v_all)
    delta_one = jnp.sum(g_all * attend_one, axis=1)
    delta_two = jnp.sum(g_all * attend_two, axis=1)
    slope_one = prob_one * (grad_prob - delta_one[:, None])
    slope_two = -LAMBDA * prob_two * (grad_prob - delta_two[:, None])
    mixed = prob_one - LAMBDA * prob_two
    query_terms = jnp.concatenate(
        [matmul(slope_one, first_k) * scale, matmul(slope_two, second_k) * scale], axis=1
    )
    query_total = lax.psum(query_terms, "pb")
    grad_queries = lax.dynamic_slice_in_dim(query_total, start, own_rows, 0)
    summed = lax.psum_scatter(
        jnp.concatenate(
            [
                inner(slope_one, first_q) * scale,
                inner(slope_two, second_q) * scale,
                inner(mixed, g_all),
            ],
            axis=1,
        ),
        "ka",
        scatter_dimension=0,
        tiled=True,
    )
    return (attended, grad_queries, summed[:, : 2 * half], summed[:, 2 * half :])


def solution(mesh):
    placed = (
        P(("ka", "pb"), None),
        P(("pb", "ka"), None),
        P(("pb", "ka"), None),
        P(("ka", "pb"), None),
    )
    return jax.shard_map(
        per_device,
        mesh=mesh,
        in_specs=placed,
        out_specs=(
            P(("ka", "pb"), None),
            P(("ka", "pb"), None),
            P(("pb", "ka"), None),
            P(("pb", "ka"), None),
        ),
        check_vma=False,
    )
```

profile of v0, /device:TPU:1, one launch (start us, length us, event | category | flops | bytes accessed | tf_op | source)
XLA Modules:
  0.0 643.2 jit_solution(4281807683046090073)
XLA Ops:
  7.2 0.7 all-gather.3.cloned.1.call-update
  7.9 0.7 all-gather.5.cloned.1.call-update
  8.7 41.6 %all_gather.12 = f32[128,256]{1,0:T(8,128)S(1)} all-gather(f32[8,256]{1,0:T(8,128)} %param.4), channel_id=1, replica_groups=mesh['pb'=16,'ka'=32] {'pb'}, dimensions={0}, use_global_device_ids=true | all-gather | bytes 139264 | tf_op jit(solution)/shard_map/all_gather | solution.py:38
  50.2 29.7 %all_gather.15 = f32[128,256]{1,0:T(8,128)S(1)} all-gather(f32[8,256]{1,0:T(8,128)} %param.7), channel_id=1, replica_groups=mesh['pb'=16,'ka'=32] {'pb'}, dimensions={0}, use_global_device_ids=true | all-gather | bytes 139264 | tf_op jit(solution)/shard_map/all_gather | solution.py:39
  79.9 3.4 all-gather.3.cloned.1.call-done
  83.3 2.5 fusion.27
  85.8 1.1 fusion.26
  86.9 35.3 %all-reduce.2 = (f32[128]{0:T(128)S(1)}, f32[128]{0:T(128)S(1)}) all-reduce(f32[128]{0:T(128)S(1)} %get-tuple-element.28, f32[128]{0:T(128)S(1)} %get-tuple-element.30), channel_id=1, replica_groups=mesh['pb'=16,'ka'=32] {'pb'}, use_global_device_ids=true, to_apply=%region_1.0 | all-reduce | flops 256 | bytes 2048 | tf_op jit(solution)/shard_map/pmax | solution.py:59
  122.3 0.3 fusion.10
  122.6 0.3 fusion.9
  122.9 29.8 %all-reduce = (f32[128]{0:T(128)S(1)}, f32[128]{0:T(128)S(1)}) all-reduce(f32[128]{0:T(128)S(1)} %get-tuple-element.32, f32[128]{0:T(128)S(1)} %get-tuple-element.22), channel_id=1, replica_groups=mesh['pb'=16,'ka'=32] {'pb'}, use_global_device_ids=true, to_apply=%region_4.0 | all-reduce | flops 256 | bytes 2048 | tf_op jit(solution)/shard_map/psum | solution.py:62
  152.7 0.5 copy-done.5
  153.2 3.7 convolution_multiply_fusion.4
  156.9 1.9 convolution_multiply_fusion.5
  158.8 0.2 all-reduce.6.cloned.1.call-start
  159.1 3.5 fusion
  162.6 2.2 fusion.28
  164.8 166.4 %all-reduce.8.cloned.1.call-done = (f32[128,256]{1,0:T(8,128)}, f32[128,256]{1,0:T(8,128)}) async-done(((f32[128,256]{1,0:T(8,128)}, f32[128,256]{1,0:T(8,128)}), (f32[128,256]{1,0:T(8,128)}, f32[128,256]{1,0:T(8,128)})) %all-reduce.8.cloned.1.call-update) | async-done | bytes 262160 | tf_op jit(solution)/shard_map/psum | solution.py:62
  331.3 1.7 multiply_reduce_fusion.1
  333.0 2.4 convolution_multiply_fusion
  335.4 2.4 convolution_multiply_fusion.1
  337.9 2.0 convolution_multiply_fusion.7
  339.9 2.0 convolution_multiply_fusion.6
  341.9 0.7 pad_maximum_fusion.1
  342.6 4.2 pad_maximum_fusion
  346.9 5.3 copy.14
  352.2 1.3 dynamic-slice_subtract_fusion
  353.5 149.5 %all-reduce.6.cloned.1.call-done = f32[128,256]{0,1:T(8,128)} async-done(((f32[128,256]{0,1:T(8,128)}), f32[128,256]{0,1:T(8,128)}) %all-reduce.6.cloned.1.call-update) | async-done | bytes 131088 | tf_op jit(solution)/shard_map/psum | solution.py:87
  503.0 1.0 constant_dynamic-slice_fusion
  504.0 0.7 copy.11
  504.7 130.4 %reduce-scatter.4.cloned.1.call-done = f32[64,512]{1,0:T(8,128)} async-done(((f32[2048,512]{1,0:T(8,128)}), f32[64,512]{1,0:T(8,128)}) %reduce-scatter.4.cloned.1.call-update) | async-done | bytes 131088
  635.1 1.5 fusion.25
  (24 shorter events, 0.3 us)
Async XLA Ops:
  7.2 76.2 %all-gather.3.cloned.1.call-start = ((), (), s32[]{:S(2)}) async-start(), calls=%async_computation.1 | async-start | bytes 2162688 | tf_op jit(solution)/shard_map/all_gather | solution.py:42
  7.9 145.3 %all-gather.5.cloned.1.call-start = ((), (), s32[]{:S(2)}) async-start(), calls=%async_computation.2 | async-start | bytes 2162688 | tf_op jit(solution)/shard_map/all_gather | solution.py:43
  8.7 322.6 %all-reduce.8.cloned.1.call-start = ((), (), s32[]{:S(2)}) async-start(), calls=%async_computation.5 | async-start | bytes 524288 | tf_op jit(solution)/shard_map/psum | solution.py:62
  83.3 2.5 copy-start.2
  152.7 0.5 copy-start.5
  152.7 6.1 copy-start.6
  153.2 3.7 copy-start
  158.8 344.2 %all-reduce.6.cloned.1.call-start = ((), (), s32[]{:S(2)}) async-start(), calls=%async_computation.3 | async-start | bytes 262144 | tf_op jit(solution)/shard_map/psum | solution.py:87
  159.1 3.5 copy-start.1
  335.4 2.5 copy-start.3
  339.8 2.8 copy-start.4
  342.6 292.6 %reduce-scatter.4.cloned.1.call-start = ((), (), s32[]{:S(2)}) async-start(), calls=%async_computation.4 | async-start | bytes 4325376
Sparse Core Ops, SparseCore 0:
  10.1 73.1 all-gather.2
  85.5 67.1 all-gather.4
  158.9 172.2 all-reduce.7
  342.7 160.3 all-reduce.5
  505.7 129.3 reduce-scatter.3
where the time goes:
time: 645 us; the launch traced here: 643 us
  waiting for transfers between devices  451 us (70%)
  blocking collectives  136 us (21%)
  matrix products  23.8 us (4%)
  between operations  13.9 us (2%)
  local copies, waits for them, and re-layouts  9.06 us (1%)
  other arithmetic  8.57 us (1%)
    psum x1, waiting for transfers between devices, per_device(): lax.psum((mass_one * factor_one, value_one * factor_one[:, None], mass_tw...  166 us
    psum x1, waiting for transfers between devices, per_device(): query_total = lax.psum(query_terms, 'pb')  149 us
    unnamed x6, waiting for transfers between devices  132 us
    all_gather x1, blocking collectives, per_device(): lax.all_gather(queries, 'pb', axis=0, tiled=True)  41.6 us
    pmax x1, blocking collectives, per_device(): peak_one, peak_two = lax.pmax((top_one, top_two), 'pb')  35.3 us
    psum x1, blocking collectives, per_device(): lax.psum((mass_one * factor_one, value_one * factor_one[:, None], mass_tw...  29.8 us
    all_gather x1, blocking collectives, per_device(): lax.all_gather(grad_out, 'pb', axis=0, tiled=True)  29.7 us
  transfers between devices with their start and end apart: 5, of which 4 were waited for; matrix products, arithmetic and copies ran while one was open for 4% of the time, Pallas kernels for 0%

commit v1 on v0

v1 whole, which is shorter than its diff:
```python
import jax
import jax.numpy as jnp
from jax import lax
from jax.sharding import Mesh, PartitionSpec as P

LAMBDA = 0.5
PB = ("z2", "z1", "z0", "xh")
KA = ("xl", "y2", "y1", "y0", "c")
KEY_GROUP = ("xh", "xl", "y0")
QUERY_GROUP = ("z2", "z1", "z0", "y2", "y1")
CORE = "c"


def dot(left, right, dims):
    return lax.dot_general(
        left, right, (dims, ((), ())), precision=lax.Precision.HIGHEST, preferred_element_type=jnp.float32
    )


def swap(x):
    return lax.ppermute(x, CORE, [(0, 1), (1, 0)])


def spread(x, axes, count):
    return lax.all_to_all(jnp.broadcast_to(x[None], (count,) + x.shape), axes, 0, 0, tiled=True)


def per_device(queries, key_pair, values, grad_out):
    half = key_pair.shape[1] // 2
    scale = half ** (-0.5)
    keys_in, queries_in = 8, 32
    kv = jnp.concatenate([key_pair, values], axis=1)
    qg = jnp.concatenate([queries, grad_out], axis=1)
    kv_own = spread(kv, KEY_GROUP, keys_in).reshape(-1, kv.shape[1])
    kv_other = swap(kv_own)
    qg_all = spread(qg, QUERY_GROUP, queries_in).reshape(-1, qg.shape[1])
    kv_all = jnp.concatenate([kv_own, kv_other], axis=0)
    q1, q2, g = qg_all[:, :half] * scale, qg_all[:, half : 2 * half] * scale, qg_all[:, 2 * half :]
    k1, k2, v = kv_all[:, :half], kv_all[:, half : 2 * half], kv_all[:, 2 * half :]
    s1 = dot(k1, q1, ((1,), (1,)))
    s2 = dot(k2, q2, ((1,), (1,)))
    dp = dot(v, g, ((1,), (1,)))
    m1, m2 = jnp.max(s1, axis=0), jnp.max(s2, axis=0)
    w1, w2 = jnp.exp(s1 - m1[None]), jnp.exp(s2 - m2[None])
    stats = jnp.stack(
        [m1, m2, jnp.sum(w1, 0), jnp.sum(w2, 0), jnp.sum(w1 * dp, 0), jnp.sum(w2 * dp, 0), m1, m2]
    )
    every = spread(stats, QUERY_GROUP, queries_in).reshape((queries_in,) + stats.shape)
    top = jnp.max(every[:, :2], axis=0)
    factor = jnp.exp(every[:, :2] - top[None])
    total = jnp.sum(every[:, 2:4] * factor, axis=0)
    delta = jnp.sum(every[:, 4:6] * factor, axis=0) / total
    own = jnp.exp(stats[:2] - top) / total
    p1, p2 = w1 * own[0], w2 * own[1]
    mixed = p1 - LAMBDA * p2
    g1 = p1 * (dp - delta[0])
    g2 = -LAMBDA * p2 * (dp - delta[1])
    dkv = jnp.concatenate(
        [dot(g1, q1, ((1,), (0,))), dot(g2, q2, ((1,), (0,))), dot(mixed, g, ((1,), (0,)))], axis=1
    )
    rows = kv_own.shape[0]
    dkv_own = dkv[:rows] + swap(dkv[rows:])
    dkv_parts = lax.all_to_all(
        dkv_own.reshape(keys_in, -1, dkv.shape[1]), KEY_GROUP, 0, 0, tiled=True
    )
    dkv_sum = jnp.sum(dkv_parts, axis=0)
    dq = jnp.concatenate(
        [dot(mixed, v, ((0,), (0,))), dot(g1, k1, ((0,), (0,))) * scale, dot(g2, k2, ((0,), (0,))) * scale],
        axis=1,
    )
    dq_parts = lax.all_to_all(dq.reshape(queries_in, -1, dq.shape[1]), QUERY_GROUP, 0, 0, tiled=True)
    dq_sum = jnp.sum(dq_parts, axis=0)
    wide = 2 * half
    return dq_sum[:, :wide], dq_sum[:, wide:], dkv_sum[:, :wide], dkv_sum[:, wide:]


def solution(mesh):
    fine = Mesh(mesh.devices.reshape((2,) * 9), PB + KA)
    by_query, by_key = P(KA + PB, None), P(PB + KA, None)
    return jax.shard_map(
        per_device,
        mesh=fine,
        in_specs=(by_query, by_key, by_key, by_query),
        out_specs=(by_query, by_query, by_key, by_key),
        check_vma=False,
    )
```

time: 645 us -> 142 us (0.22)
  waiting for transfers between devices: 451 us -> 49.2 us
  blocking collectives: 136 us -> 21.3 us
  starting transfers between devices: 0.38 us -> 44.9 us
  between operations: 13.9 us -> 1.01 us
  matrix products: 23.8 us -> 13.1 us
    psum x2 -> x0, waiting for transfers between devices: 316 us -> none  [the longest x1 166 us: per_device(): lax.psum((mass_one * factor_one, value_one * factor_one[:, None], mass_tw...]
    unnamed x6 -> x0, waiting for transfers between devices: 132 us -> none
    all_gather x2 -> x0, blocking collectives: 71.2 us -> none  [the longest x1 41.6 us: per_device(): lax.all_gather(queries, 'pb', axis=0, tiled=True)]
    all_to_all x0 -> x4, waiting for transfers between devices: none -> 49.2 us  [the longest x2 20.8 us: spread(): lax.all_to_all(jnp.broadcast_to(x[None], (count,) + x.shape), axes, 0, 0,...]
    pmax x1 -> x0, blocking collectives: 35.3 us -> none  [per_device(): peak_one, peak_two = lax.pmax((top_one, top_two), 'pb')]
    all_to_all x0 -> x4, starting transfers between devices: none -> 35 us  [the longest x2 24.1 us: spread(): lax.all_to_all(jnp.broadcast_to(x[None], (count,) + x.shape), axes, 0, 0,...]
    psum x1 -> x0, blocking collectives: 29.8 us -> none  [per_device(): lax.psum((mass_one * factor_one, value_one * factor_one[:, None], mass_tw...]
    all_to_all x0 -> x1, blocking collectives: none -> 21.3 us  [spread(): lax.all_to_all(jnp.broadcast_to(x[None], (count,) + x.shape), axes, 0, 0,...]
  transfers between devices with their start and end apart: 5 -> 6, of which waited for: 4 -> 4; matrix products, arithmetic and copies ran while one was open for 4% -> 5% of each run, Pallas kernels for 0% -> 0%
where the time goes in v1:
time: 142 us; the launch traced here: 141 us
  waiting for transfers between devices  49.2 us (35%)
  starting transfers between devices  44.9 us (32%)
  blocking collectives  21.3 us (15%)
  matrix products  13.1 us (9%)
  local copies, waits for them, and re-layouts  7.79 us (5%)
  other arithmetic  3.98 us (3%)
    all_to_all x2, starting transfers between devices, spread(): lax.all_to_all(jnp.broadcast_to(x[None], (count,) + x.shape), axes, 0, 0,...  24.1 us
    all_to_all x1, blocking collectives, spread(): lax.all_to_all(jnp.broadcast_to(x[None], (count,) + x.shape), axes, 0, 0,...  21.3 us
    all_to_all x2, waiting for transfers between devices, spread(): lax.all_to_all(jnp.broadcast_to(x[None], (count,) + x.shape), axes, 0, 0,...  20.8 us
    all_to_all x1, waiting for transfers between devices, per_device(): lax.all_to_all(dq.reshape(queries_in, -1, dq.shape[1]), QUERY_GROUP, 0, 0...  15.8 us
    dot_general x9, matrix products, dot(): lax.dot_general(left, right, (dims, ((), ())), precision=lax.Precision.HI...  13.1 us
    all_to_all x1, waiting for transfers between devices, per_device(): lax.all_to_all(dkv_own.reshape(keys_in, -1, dkv.shape[1]), KEY_GROUP, 0,...  12.6 us
    ppermute x2, starting transfers between devices, swap(): return lax.ppermute(x, CORE, [(0, 1), (1, 0)])  9.88 us
    all_to_all x1, starting transfers between devices, per_device(): lax.all_to_all(dkv_own.reshape(keys_in, -1, dkv.shape[1]), KEY_GROUP, 0,...  6.28 us
  transfers between devices with their start and end apart: 6, of which 4 were waited for; matrix products, arithmetic and copies ran while one was open for 5% of the time, Pallas kernels for 0%

profile of v1, /device:TPU:1, one launch (start us, length us, event | category | flops | bytes accessed | tf_op | source)
XLA Modules:
  0.0 141.3 jit_solution(1413280763918671639)
XLA Ops:
  0.7 0.9 pad_maximum_fusion.7
  1.5 1.1 broadcast_in_dim.8
  2.6 5.9 %all-to-all-start = ((f32[8,64,512]{2,1,0:T(8,128)}), f32[8,64,512]{2,1,0:T(8,128)S(1)}, u32[]{:S(2)}, u32[]{:S(2)}) async-start(f32[8,64,512]{2,1,0:T(8,128)} %broadcast_in_dim.8), calls=%async_computation | async-start | bytes 2097152 | tf_op jit(solution)/shard_map/all_to_all | solution.py:25
  8.5 11.0 %all-to-all-done = f32[8,64,512]{2,1,0:T(8,128)S(1)} async-done(((f32[8,64,512]{2,1,0:T(8,128)}), f32[8,64,512]{2,1,0:T(8,128)S(1)}, u32[]{:S(2)}, u32[]{:S(2)}) %all-to-all-start) | async-done | bytes 1048608 | tf_op jit(solution)/shard_map/all_to_all | solution.py:25
  19.5 0.9 broadcast_in_dim.9
  20.5 18.3 %all-to-all-start.1 = ((f32[32,8,512]{2,1,0:T(8,128)}), f32[32,8,512]{2,1,0:T(8,128)S(1)}, u32[]{:S(2)}, u32[]{:S(2)}) async-start(f32[32,8,512]{2,1,0:T(8,128)} %broadcast_in_dim.9), calls=%async_computation.1 | async-start | bytes 1048576 | tf_op jit(solution)/shard_map/all_to_all | solution.py:25
  38.7 4.3 %collective-permute-start = (f32[512,512]{1,0:T(8,128)S(1)}, f32[512,512]{1,0:T(8,128)S(1)}, u32[]{:S(2)}, u32[]{:S(2)}) collective-permute-start(f32[512,512]{1,0:T(8,128)S(1)} %bitcast.18), channel_id=1, source_target_pairs={{0,1},{1,0},{2,3},{3,2},{4,5},{5,4},{6,7},{7,6},{8,9},{9,8},{10,11... | collective-permute-start | bytes 3145736 | tf_op jit(solution)/shard_map/ppermute | solution.py:21
  43.1 9.9 %all-to-all-done.1 = f32[32,8,512]{2,1,0:T(8,128)S(1)} async-done(((f32[32,8,512]{2,1,0:T(8,128)}), f32[32,8,512]{2,1,0:T(8,128)S(1)}, u32[]{:S(2)}, u32[]{:S(2)}) %all-to-all-start.1) | async-done | bytes 524320 | tf_op jit(solution)/shard_map/all_to_all | solution.py:25
  53.3 0.5 copy-done.11
  53.8 1.0 fusion.40
  54.8 1.0 fusion.41
  55.8 0.3 copy-done.4
  56.1 1.2 multiply_reduce_fusion
  57.4 21.3 %all_to_all.25 = f32[32,8,256]{2,1,0:T(8,128)S(1)} all-to-all(f32[32,8,256]{2,1,0:T(8,128)S(1)} %broadcast_in_dim.11), channel_id=1, replica_groups=mesh['z2'=2,'z1'=2,'z0'=2,'xh'=2,'xl'=2,'y2'=2,'y1'=2,'y0'=2,'c'=2] {'z2..., dimensions={0} | all-to-all | bytes 524288 | tf_op jit(solution)/shard_map/all_to_all | solution.py:25
  78.9 2.4 %convolution_multiply_fusion = f32[256,128]{0,1:T(8,128)S(1)} fusion(f32[1024,128]{1,0:T(8,128)} %copy-done.10, f32[1024,256]{1,0:T(8,128)S(1)} %get-tuple-element.34, f32[1024,256]{1,0:T(8,128)S(1)} %get-tuple-element.33, f32[256]{0:T(256)S(1)} %bitcast.41, f32[256]{0:T(256)S(1)} %bitcast.35, f32[256]{0:T(256)S(1)} %get-tuple-element.32), kind=kOutput, calls=%fused_computation.1 | convolution fusion | flops 403996672 | bytes 2755584 | tf_op jit(solution)/shard_map/dot_general | solution.py:15
  81.3 1.5 %fusion.8 = f32[1024,128]{0,1:T(8,128)S(1)} fusion(f32[1024,256]{1,0:T(8,128)S(1)} %get-tuple-element.34, f32[1024,256]{1,0:T(8,128)S(1)} %get-tuple-element.33, f32[256]{0:T(256)S(1)} %bitcast.42, f32[256]{0:T(256)S(1)} %bitcast.36, f32[256]{0:T(256)S(1)} %get-tuple-element.32, f32[256,128]{0,1:T(8,128)S(1)} %copy.32), kind=kOutput, calls=%fused_computation.23 | convolution fusion | flops 403996672 | bytes 2755584 | tf_op jit(solution)/shard_map/dot_general | solution.py:15
  82.8 1.2 convolution_multiply_fusion.1
  84.0 1.4 fusion.7
  85.4 1.4 %fusion.4 = f32[1024,256]{0,1:T(8,128)S(1)} fusion(f32[256,512]{1,0:T(8,128)S(1)} %bitcast.24, f32[1024,256]{1,0:T(8,128)S(1)} %get-tuple-element.31, f32[1024,256]{1,0:T(8,128)S(1)} %get-tuple-element.33, f32[256]{0:T(256)S(1)} %bitcast.37, f32[256]{0:T(256)S(1)} %bitcast.33, f32[256]{0:T(256)S(1)} %get-tuple-element.32, f32[256]{0:T(256)S(1)} %get-tuple-element.30), kind=kOutput, calls=%fused_computation.19 | convolution fusion | flops 806879232 | bytes 3411968 | tf_op jit(solution)/shard_map/dot_general | solution.py:15
  87.1 1.1 slice.92
  88.2 5.5 %collective-permute-start.1 = (f32[512,512]{0,1:T(8,128)}, f32[512,512]{0,1:T(8,128)}, u32[]{:S(2)}, u32[]{:S(2)}) collective-permute-start(f32[512,512]{0,1:T(8,128)} %slice.92), channel_id=1, source_target_pairs={{0,1},{1,0},{2,3},{3,2},{4,5},{5,4},{6,7},{7,6},{8,9},{9,8},{10,11... | collective-permute-start | bytes 3145736 | tf_op jit(solution)/shard_map/ppermute | solution.py:21
  93.8 2.0 %fusion.3 = f32[256,256]{0,1:T(8,128)S(1)} fusion(f32[512,512]{1,0:T(8,128)S(1)} %copy-done.5, f32[512,512]{1,0:T(8,128)S(1)} %bitcast.21, f32[1024,256]{1,0:T(8,128)S(1)} %get-tuple-element.31, f32[1024,256]{1,0:T(8,128)S(1)} %get-tuple-element.33, f32[256]{0:T(256)S(1)} %bitcast.38, f32[256]{0:T(256)S(1)} %bitcast.34, f32[256]{0:T(256)S(1)} %get-tuple-element.32, ...), kind=kOutput, calls=%fused_computation.18 | convolution fusion | flops 807141376 | bytes 4460544 | tf_op jit(solution)/shard_map/dot_general | solution.py:15
  95.9 1.0 copy.29
  96.9 4.6 %all-to-all-start.3 = ((f32[32,8,512]{2,1,0:T(8,128)}), f32[32,8,512]{2,1,0:T(8,128)}, u32[]{:S(2)}, u32[]{:S(2)}) async-start(f32[32,8,512]{2,1,0:T(8,128)} %bitcast.12), calls=%async_computation.3 | async-start | bytes 1048576 | tf_op jit(solution)/shard_map/all_to_all | solution.py:71
  101.5 1.4 %slice_add_fusion = f32[512,512]{0,1:T(8,128)S(1)} fusion(f32[512,512]{0,1:T(8,128)} %collective-permute-done.1, f32[1024,512]{0,1:T(8,128)S(1)} %copy-done.7), kind=kLoop, calls=%fused_computation.3 | loop fusion | flops 262144 | bytes 3145728 | tf_op jit(solution)/shard_map/add | solution.py:62
  103.0 1.3 copy.30
  104.3 15.8 %all-to-all-done.3 = f32[32,8,512]{2,1,0:T(8,128)} async-done(((f32[32,8,512]{2,1,0:T(8,128)}), f32[32,8,512]{2,1,0:T(8,128)}, u32[]{:S(2)}, u32[]{:S(2)}) %all-to-all-start.3) | async-done | bytes 524320 | tf_op jit(solution)/shard_map/all_to_all | solution.py:71
  120.0 6.3 %all-to-all-start.4 = ((f32[8,64,512]{2,1,0:T(8,128)}), f32[8,64,512]{2,1,0:T(8,128)S(1)}, u32[]{:S(2)}, u32[]{:S(2)}) async-start(f32[8,64,512]{2,1,0:T(8,128)} %bitcast.13), calls=%async_computation.4 | async-start | bytes 2097152 | tf_op jit(solution)/shard_map/all_to_all | solution.py:63
  126.3 1.1 reduce_sum.78
  127.4 0.6 fusion.37
  128.0 12.6 %all-to-all-done.4 = f32[8,64,512]{2,1,0:T(8,128)S(1)} async-done(((f32[8,64,512]{2,1,0:T(8,128)}), f32[8,64,512]{2,1,0:T(8,128)S(1)}, u32[]{:S(2)}, u32[]{:S(2)}) %all-to-all-start.4) | async-done | bytes 1048608 | tf_op jit(solution)/shard_map/all_to_all | solution.py:63
  140.7 0.7 fusion.36
  (46 shorter events, 0.9 us)
Async XLA Ops:
  0.6 7.9 %copy-start.14 = (f32[8,256]{1,0:T(8,128)S(1)}, f32[8,256]{1,0:T(8,128)}, u32[]{:S(2)}) copy-start(f32[8,256]{1,0:T(8,128)} %param.7) | copy-start | bytes 24580
  0.6 7.9 %copy-start.15 = (f32[8,256]{1,0:T(8,128)S(1)}, f32[8,256]{1,0:T(8,128)}, u32[]{:S(2)}) copy-start(f32[8,256]{1,0:T(8,128)} %param.4) | copy-start | bytes 24580
  2.6 16.9 %all-to-all-start = ((f32[8,64,512]{2,1,0:T(8,128)}), f32[8,64,512]{2,1,0:T(8,128)S(1)}, u32[]{:S(2)}, u32[]{:S(2)}) async-start(f32[8,64,512]{2,1,0:T(8,128)} %broadcast_in_dim.8), calls=%async_computation | async-start | bytes 2097152 | tf_op jit(solution)/shard_map/all_to_all | solution.py:25
  19.5 33.8 %copy-start = (f32[8,64,512]{2,1,0:T(8,128)}, f32[8,64,512]{2,1,0:T(8,128)S(1)}, u32[]{:S(2)}) copy-start(f32[8,64,512]{2,1,0:T(8,128)S(1)} %all-to-all-done) | copy-start | bytes 3145732
  20.5 32.5 %all-to-all-start.1 = ((f32[32,8,512]{2,1,0:T(8,128)}), f32[32,8,512]{2,1,0:T(8,128)S(1)}, u32[]{:S(2)}, u32[]{:S(2)}) async-start(f32[32,8,512]{2,1,0:T(8,128)} %broadcast_in_dim.9), calls=%async_computation.1 | async-start | bytes 1048576 | tf_op jit(solution)/shard_map/all_to_all | solution.py:25
  38.7 14.5 %collective-permute-start = (f32[512,512]{1,0:T(8,128)S(1)}, f32[512,512]{1,0:T(8,128)S(1)}, u32[]{:S(2)}, u32[]{:S(2)}) collective-permute-start(f32[512,512]{1,0:T(8,128)S(1)} %bitcast.18), channel_id=1, source_target_pairs={{0,1},{1,0},{2,3},{3,2},{4,5},{5,4},{6,7},{7,6},{8,9},{9,8},{10,11... | collective-permute-start | bytes 3145736 | tf_op jit(solution)/shard_map/ppermute | solution.py:21
  53.0 0.8 copy-start.11
  53.2 1.6 %copy-start.3 = (f32[512,512]{1,0:T(8,128)}, f32[512,512]{1,0:T(8,128)S(1)}, u32[]{:S(2)}) copy-start(f32[512,512]{1,0:T(8,128)S(1)} %collective-permute-done) | copy-start | bytes 3145732
  53.8 2.0 %copy-start.8 = (f32[1024,128]{1,0:T(8,128)}, f32[1024,128]{1,0:T(8,128)S(1)}, u32[]{:S(2)}) copy-start(f32[1024,128]{1,0:T(8,128)S(1)} %get-tuple-element.12) | copy-start | bytes 1572868
  53.8 2.0 %copy-start.10 = (f32[1024,128]{1,0:T(8,128)}, f32[1024,128]{1,0:T(8,128)S(1)}, u32[]{:S(2)}) copy-start(f32[1024,128]{1,0:T(8,128)S(1)} %get-tuple-element.13) | copy-start | bytes 1572868
  53.8 2.0 %copy-start.1 = (f32[8,64,512]{2,1,0:T(8,128)S(1)}, f32[8,64,512]{2,1,0:T(8,128)}, u32[]{:S(2)}) copy-start(f32[8,64,512]{2,1,0:T(8,128)} %copy-done) | copy-start | bytes 3145732
  53.8 2.0 %copy-start.12 = (f32[32,8,512]{2,1,0:T(8,128)S(1)}, f32[32,8,512]{2,1,0:T(8,128)}, u32[]{:S(2)}) copy-start(f32[32,8,512]{2,1,0:T(8,128)} %copy-done.11) | copy-start | bytes 1572868
  54.8 1.3 copy-start.4
  78.9 3.8 %copy-start.9 = (f32[1024,128]{1,0:T(8,128)S(1)}, f32[1024,128]{1,0:T(8,128)}, u32[]{:S(2)}) copy-start(f32[1024,128]{1,0:T(8,128)} %copy-done.8) | copy-start | bytes 1572868
  82.8 2.6 %copy-start.13 = (f32[32,8,512]{2,1,0:T(8,128)S(1)}, f32[32,8,512]{2,1,0:T(8,128)}, u32[]{:S(2)}) copy-start(f32[32,8,512]{2,1,0:T(8,128)} %copy-done.11) | copy-start | bytes 1572868
  87.1 8.7 %copy-start.6 = (f32[1024,512]{0,1:T(8,128)}, f32[1024,512]{0,1:T(8,128)S(1)}, u32[]{:S(2)}) copy-start(f32[1024,512]{0,1:T(8,128)S(1)} %pad_maximum_fusion) | copy-start | bytes 6291460
  87.1 6.6 %copy-start.2 = (f32[8,64,512]{2,1,0:T(8,128)S(1)}, f32[8,64,512]{2,1,0:T(8,128)}, u32[]{:S(2)}) copy-start(f32[8,64,512]{2,1,0:T(8,128)} %copy-done) | copy-start | bytes 3145732
  87.1 6.6 %copy-start.5 = (f32[512,512]{1,0:T(8,128)S(1)}, f32[512,512]{1,0:T(8,128)}, u32[]{:S(2)}) copy-start(f32[512,512]{1,0:T(8,128)} %copy-done.3) | copy-start | bytes 3145732
  88.2 13.3 %collective-permute-start.1 = (f32[512,512]{0,1:T(8,128)}, f32[512,512]{0,1:T(8,128)}, u32[]{:S(2)}, u32[]{:S(2)}) collective-permute-start(f32[512,512]{0,1:T(8,128)} %slice.92), channel_id=1, source_target_pairs={{0,1},{1,0},{2,3},{3,2},{4,5},{5,4},{6,7},{7,6},{8,9},{9,8},{10,11... | collective-permute-start | bytes 3145736 | tf_op jit(solution)/shard_map/ppermute | solution.py:21
  95.9 5.7 %copy-start.7 = (f32[1024,512]{0,1:T(8,128)S(1)}, f32[1024,512]{0,1:T(8,128)}, u32[]{:S(2)}) copy-start(f32[1024,512]{0,1:T(8,128)} %copy-done.6) | copy-start | bytes 6291460
  96.9 23.2 %all-to-all-start.3 = ((f32[32,8,512]{2,1,0:T(8,128)}), f32[32,8,512]{2,1,0:T(8,128)}, u32[]{:S(2)}, u32[]{:S(2)}) async-start(f32[32,8,512]{2,1,0:T(8,128)} %bitcast.12), calls=%async_computation.3 | async-start | bytes 1048576 | tf_op jit(solution)/shard_map/all_to_all | solution.py:71
  120.0 20.5 %all-to-all-start.4 = ((f32[8,64,512]{2,1,0:T(8,128)}), f32[8,64,512]{2,1,0:T(8,128)S(1)}, u32[]{:S(2)}, u32[]{:S(2)}) async-start(f32[8,64,512]{2,1,0:T(8,128)} %bitcast.13), calls=%async_computation.4 | async-start | bytes 2097152 | tf_op jit(solution)/shard_map/all_to_all | solution.py:63

commit v2 on v1

v2 whole, which is shorter than its diff:
```python
import jax
import jax.numpy as jnp
from jax import lax
from jax.experimental import pallas as pl
from jax.experimental.pallas import tpu as pltpu
from jax.sharding import Mesh, PartitionSpec as P

LAMBDA = 0.5
PB = ("z2", "z1", "z0", "xh")
KA = ("xl", "y2", "y1", "y0", "c")
KEY_GROUP = ("xh", "xl", "y0")
KEYS_IN = 8
QUERY_GROUP = ("z2", "z1", "z0", "y2", "y1")
QUERIES_IN = 32
CORE = "c"
STRIP = 256
F32, BF16 = jnp.float32, jnp.bfloat16
VMEM_LIMIT = 56 * 1024 * 1024


def call(body, out_shape, flops, moved):
    return pl.pallas_call(
        body,
        out_shape=out_shape,
        cost_estimate=pl.CostEstimate(flops=flops, bytes_accessed=moved, transcendentals=0),
        compiler_params=pltpu.CompilerParams(vmem_limit_bytes=VMEM_LIMIT),
    )


def shape(dtype, *dims):
    return jax.ShapeDtypeStruct(dims, dtype)


def parts(x, count):
    out = []
    for _ in range(count):
        out.append(x.astype(BF16))
        x = x - out[-1].astype(F32)
    return out


def dot(left, right, dims=((1,), (0,))):
    return lax.dot_general(left, right, (dims, ((), ())), preferred_element_type=F32)


def beside(*blocks):
    return jnp.concatenate(blocks, axis=1)


def lay_out(queries_ref, grad_ref, key_ref, value_ref, kv_ref, qg_ref):
    wide = key_ref.shape[1]
    for n in range(kv_ref.shape[0]):
        kv_ref[n, :, :wide] = key_ref[...]
        kv_ref[n, :, wide:] = value_ref[...]
    for n in range(qg_ref.shape[0]):
        qg_ref[n, :, :wide] = queries_ref[...]
        qg_ref[n, :, wide:] = grad_ref[...]


def split_keys(kv_ref, key_ref, value_ref, turned_ref):
    wide = kv_ref.shape[1] // 2
    for n, part in enumerate(parts(kv_ref[:, :wide], 3)):
        key_ref[n] = part
    for n, part in enumerate(parts(kv_ref[:, wide:], 2)):
        value_ref[n] = part
    for n, part in enumerate(parts(kv_ref[...].T, 2)):
        turned_ref[n] = part


def forward(own_key, own_value, other_key, other_value, qg_ref, w1_ref, w2_ref, dp_ref, stats_ref):
    half = qg_ref.shape[1] // 4
    scale = half ** (-0.5)
    g_hi, g_lo = parts(qg_ref[:, 2 * half :], 2)
    query = []
    for first in (0, half):
        hi, mid, low = parts(qg_ref[:, first : first + half] * scale, 3)
        query.append((beside(hi, mid), beside(low, hi)))
    rows = own_key.shape[1]
    tops = [None, None]
    for which, (key_ref, value_ref) in enumerate(((own_key, own_value), (other_key, other_value))):
        for start in range(0, rows, STRIP):
            here = pl.ds(start, STRIP)
            there = pl.ds(which * rows + start, STRIP)
            for head, w_ref in enumerate((w1_ref, w2_ref)):
                cols = pl.ds(head * half, half)
                hi, mid, low = (key_ref[n, here, cols] for n in range(3))
                main, rest = query[head]
                across = ((1,), (1,))
                score = (
                    dot(beside(hi, hi), main, across)
                    + dot(beside(mid, mid), main, across)
                    + dot(beside(hi, low), rest, across)
                )
                w_ref[there, :] = score
                top = jnp.max(score, axis=0, keepdims=True)
                tops[head] = top if tops[head] is None else jnp.maximum(tops[head], top)
            v_hi, v_lo = value_ref[0, here, :], value_ref[1, here, :]
            dp_ref[there, :] = (
                dot(v_hi, g_hi, ((1,), (1,))) + dot(v_hi, g_lo, ((1,), (1,))) + dot(v_lo, g_hi, ((1,), (1,)))
            )
    for head, w_ref in enumerate((w1_ref, w2_ref)):
        mass = jnp.zeros_like(tops[head])
        lean = jnp.zeros_like(tops[head])
        for start in range(0, 2 * rows, STRIP):
            here = pl.ds(start, STRIP)
            weight = jnp.exp(w_ref[here, :] - tops[head])
            w_ref[here, :] = weight
            mass = mass + jnp.sum(weight, axis=0, keepdims=True)
            lean = lean + jnp.sum(weight * dp_ref[here, :], axis=0, keepdims=True)
        stats_ref[head : head + 1, :] = tops[head]
        stats_ref[2 + head : 3 + head, :] = mass
        stats_ref[4 + head : 5 + head, :] = lean
    stats_ref[6:8, :] = jnp.zeros_like(stats_ref[6:8, :])


def key_side(w1_ref, w2_ref, dp_ref, qg_ref, stats_ref, every_ref, own_ref, other_ref, slopes_ref):
    half = qg_ref.shape[1] // 4
    scale = half ** (-0.5)
    every = every_ref[...]
    top = jnp.max(every[:, 0:2, :], axis=0)
    factor = jnp.exp(every[:, 0:2, :] - top[None])
    total = jnp.sum(every[:, 2:4, :] * factor, axis=0)
    delta = jnp.sum(every[:, 4:6, :] * factor, axis=0) / total
    rescale = jnp.exp(stats_ref[0:2, :] - top) / total
    g_hi, g_lo = parts(qg_ref[:, 2 * half :], 2)
    query = [parts(qg_ref[:, first : first + half] * scale, 2) for first in (0, half)]
    rows = own_ref.shape[0]
    for which, out_ref in enumerate((own_ref, other_ref)):
        for start in range(0, rows, STRIP):
            here = pl.ds(start, STRIP)
            there = pl.ds(which * rows + start, STRIP)
            dp = dp_ref[there, :]
            p1 = w1_ref[there, :] * rescale[0:1]
            p2 = w2_ref[there, :] * (-LAMBDA * rescale[1:2])
            slopes = (p1 * (dp - delta[0:1]), p2 * (dp - delta[1:2]))
            mix_hi, mix_lo = parts(p1 + p2, 2)
            slopes_ref[0, there, :] = mix_hi
            slopes_ref[1, there, :] = mix_lo
            for head in range(2):
                hi, lo = parts(slopes[head], 2)
                slopes_ref[2 + 2 * head, there, :] = hi
                slopes_ref[3 + 2 * head, there, :] = lo
                q_hi, q_lo = query[head]
                both = dot(hi, beside(q_hi, q_lo))
                out_ref[here, head * half : (head + 1) * half] = both[:, :half] + both[:, half:] + dot(lo, q_hi)
            out_ref[here, 2 * half :] = dot(mix_hi, g_hi) + dot(mix_hi, g_lo) + dot(mix_lo, g_hi)


def query_side(slopes_ref, own_ref, other_ref, out_ref):
    rows = own_ref.shape[2]
    wide = own_ref.shape[1] // 2
    half = wide // 2
    scale = half ** (-0.5)

    def product(first, count, at):
        total = None
        for which, turned in enumerate((own_ref, other_ref)):
            there = pl.ds(which * rows, rows)
            hi, lo = turned[0, first : first + count, :], turned[1, first : first + count, :]
            s_hi, s_lo = slopes_ref[at, there, :], slopes_ref[at + 1, there, :]
            term = dot(hi, s_hi) + dot(hi, s_lo) + dot(lo, s_hi)
            total = term if total is None else total + term
        return total.T

    out_ref[:, :wide] = product(wide, wide, 0)
    out_ref[:, wide : wide + half] = product(0, half, 2) * scale
    out_ref[:, wide + half :] = product(half, half, 4) * scale


def swap(x):
    return lax.ppermute(x, CORE, [(0, 1), (1, 0)])


def exchange(x, axes):
    return lax.all_to_all(x, axes, 0, 0, tiled=True)


def per_device(queries, key_pair, values, grad_out):
    wide = values.shape[1]
    own_keys, own_rows = key_pair.shape[0], queries.shape[0]
    rows, columns = KEYS_IN * own_keys, QUERIES_IN * own_rows
    kv, qg = call(
        lay_out,
        (shape(F32, KEYS_IN, own_keys, 2 * wide), shape(F32, QUERIES_IN, own_rows, 2 * wide)),
        0,
        4 * 2 * wide * (rows + columns),
    )(queries, grad_out, key_pair, values)
    kv_own = exchange(kv, KEY_GROUP).reshape(rows, 2 * wide)
    kv_other = swap(kv_own)
    qg_all = exchange(qg, QUERY_GROUP).reshape(columns, 2 * wide)
    split = call(
        split_keys,
        (shape(BF16, 3, rows, wide), shape(BF16, 2, rows, wide), shape(BF16, 2, 2 * wide, rows)),
        0,
        4 * 2 * wide * rows * 3,
    )
    own_key, own_value, own_turned = split(kv_own)
    other_key, other_value, other_turned = split(kv_other)
    big = shape(F32, 2 * rows, columns)
    pairs = 2 * rows * columns
    w1, w2, dp, stats = call(
        forward, (big, big, big, shape(F32, 8, columns)), 2 * pairs * wide * 9, 4 * pairs * 3
    )(own_key, own_value, other_key, other_value, qg_all)
    every = exchange(
        jnp.broadcast_to(stats[None], (QUERIES_IN,) + stats.shape), QUERY_GROUP
    ).reshape((QUERIES_IN,) + stats.shape)
    half_grad = shape(F32, rows, 2 * wide)
    dkv_own, dkv_other, slopes = call(
        key_side, (half_grad, half_grad, shape(BF16, 6, 2 * rows, columns)), 2 * pairs * wide * 6, 4 * pairs * 6
    )(w1, w2, dp, qg_all, stats, every)
    moved = swap(dkv_other)
    dq = call(query_side, shape(F32, columns, 2 * wide), 2 * pairs * wide * 6, 4 * pairs * 4)(
        slopes, own_turned, other_turned
    )
    dq_sum = jnp.sum(exchange(dq.reshape(QUERIES_IN, own_rows, 2 * wide), QUERY_GROUP), axis=0)
    dkv = (dkv_own + moved).reshape(KEYS_IN, own_keys, 2 * wide)
    dkv_sum = jnp.sum(exchange(dkv, KEY_GROUP), axis=0)
    return dq_sum[:, :wide], dq_sum[:, wide:], dkv_sum[:, :wide], dkv_sum[:, wide:]


def solution(mesh):
    fine = Mesh(mesh.devices.reshape((2,) * 9), PB + KA)
    by_query, by_key = P(KA + PB, None), P(PB + KA, None)
    return jax.shard_map(
        per_device,
        mesh=fine,
        in_specs=(by_query, by_key, by_key, by_query),
        out_specs=(by_query, by_query, by_key, by_key),
        check_vma=False,
    )
```

time: 142 us -> 145 us (1.021)
  Pallas kernels: 0 us -> 23.4 us
  blocking collectives: 21.3 us -> 36.1 us
  matrix products: 13.1 us -> 0 us
  starting transfers between devices: 44.9 us -> 34.4 us
  waiting for transfers between devices: 49.2 us -> 44.3 us
  local copies, waits for them, and re-layouts: 7.79 us -> 3.76 us
  other arithmetic: 3.98 us -> 1.3 us
    pallas_call x0 -> x6, Pallas kernels: none -> 23.4 us  [the longest x1 5.46 us: per_device(): call(key_side, (half_grad, half_grad, shape(BF16, 6, 2 * rows, columns)),...]
    all_to_all x1 -> x2, blocking collectives: 21.3 us -> 36.1 us  [exchange(): return lax.all_to_all(x, axes, 0, 0, tiled=True)]
    dot_general x9 -> x0, matrix products: 13.1 us -> none  [dot(): lax.dot_general(left, right, (dims, ((), ())), precision=lax.Precision.HI...]
    all_to_all x4 -> x3, starting transfers between devices: 35 us -> 22.9 us  [exchange(): return lax.all_to_all(x, axes, 0, 0, tiled=True)]
    all_to_all x4 -> x3, waiting for transfers between devices: 49.2 us -> 44.3 us  [exchange(): return lax.all_to_all(x, axes, 0, 0, tiled=True)]
    ppermute x2, starting transfers between devices: 9.88 us -> 11.5 us  [swap(): return lax.ppermute(x, CORE, [(0, 1), (1, 0)])]
  transfers between devices with their start and end apart: 6 -> 5, of which waited for: 4 -> 3; matrix products, arithmetic and copies ran while one was open for 5% -> 1% of each run, Pallas kernels for 0% -> 7%
where the time goes in v2:
time: 145 us; the launch traced here: 144 us
  waiting for transfers between devices  44.3 us (31%)
  blocking collectives  36.1 us (25%)
  starting transfers between devices  34.4 us (24%)
  Pallas kernels  23.4 us (16%)
  local copies, waits for them, and re-layouts  3.76 us (3%)
    all_to_all x3, waiting for transfers between devices, exchange(): return lax.all_to_all(x, axes, 0, 0, tiled=True)  44.3 us
    all_to_all x2, blocking collectives, exchange(): return lax.all_to_all(x, axes, 0, 0, tiled=True)  36.1 us
    all_to_all x3, starting transfers between devices, exchange(): return lax.all_to_all(x, axes, 0, 0, tiled=True)  22.9 us
    ppermute x2, starting transfers between devices, swap(): return lax.ppermute(x, CORE, [(0, 1), (1, 0)])  11.5 us
    pallas_call x1, Pallas kernels, per_device(): call(key_side, (half_grad, half_grad, shape(BF16, 6, 2 * rows, columns)),...  5.46 us
    pallas_call x1, Pallas kernels, per_device(): call(forward, (big, big, big, shape(F32, 8, columns)), 2 * pairs * wide *...  5.02 us
    pallas_call x1, Pallas kernels, per_device(): call(query_side, shape(F32, columns, 2 * wide), 2 * pairs * wide * 6, 4 *...  4.5 us
    pallas_call x1, Pallas kernels, per_device(): other_key, other_value, other_turned = split(kv_other)  3.12 us
  transfers between devices with their start and end apart: 5, of which 3 were waited for; matrix products, arithmetic and copies ran while one was open for 1% of the time, Pallas kernels for 7%

profile of v2, /device:TPU:1, one launch (start us, length us, event | category | flops | bytes accessed | tf_op | source)
XLA Modules:
  0.0 144.0 jit_solution(6239813641809297130)
XLA Ops:
  0.6 2.2 %shard_map.75 = (f32[8,64,512]{2,1,0:T(8,128)}, f32[32,8,512]{2,1,0:T(8,128)}) custom-call(f32[8,256]{1,0:T(8,128)} %queries_ref.1, f32[8,256]{1,0:T(8,128)} %grad_ref.1, f32[64,256]{1,0:T(8,128)} %key_ref.1, f32[64,256]{1,0:T(8,128)} %value_ref.1), custom_call_target="tpu_custom_call" | custom-call | bytes 1572864 | tf_op jit(solution)/shard_map/pallas_call | solution.py:182
  2.8 17.1 %all_to_all.25 = f32[8,64,512]{2,1,0:T(8,128)S(1)} all-to-all(f32[8,64,512]{2,1,0:T(8,128)} %get-tuple-element.19), channel_id=1, replica_groups=mesh['z2'=2,'z1'=2,'z0'=2,'xh'=2,'xl'=2,'y2'=2,'y1'=2,'y0'=2,'c'=2] {'xh..., dimensions={0} | all-to-all | bytes 2097152 | tf_op jit(solution)/shard_map/all_to_all | solution.py:175
  19.9 0.0 copy-start
  19.9 7.3 %collective-permute-start = (f32[512,512]{1,0:T(8,128)S(1)}, f32[512,512]{1,0:T(8,128)S(1)}, u32[]{:S(2)}, u32[]{:S(2)}) collective-permute-start(f32[512,512]{1,0:T(8,128)S(1)} %bitcast.4), channel_id=1, source_target_pairs={{0,1},{1,0},{2,3},{3,2},{4,5},{5,4},{6,7},{7,6},{8,9},{9,8},{10,11... | collective-permute-start | bytes 3145736 | tf_op jit(solution)/shard_map/ppermute | solution.py:171
  27.2 14.9 %all-to-all-start.1 = ((f32[32,8,512]{2,1,0:T(8,128)}), f32[32,8,512]{2,1,0:T(8,128)S(1)}, u32[]{:S(2)}, u32[]{:S(2)}) async-start(f32[32,8,512]{2,1,0:T(8,128)} %get-tuple-element.24), calls=%async_computation.1 | async-start | bytes 1048576 | tf_op jit(solution)/shard_map/all_to_all | solution.py:175
  42.2 0.0 copy-done
  42.2 3.1 %shard_map.76 = (bf16[3,512,256]{2,1,0:T(8,128)(2,1)}, bf16[2,512,256]{2,1,0:T(8,128)(2,1)}, bf16[2,512,512]{2,1,0:T(8,128)(2,1)}) custom-call(f32[512,512]{1,0:T(8,128)} %bitcast.5), custom_call_target="tpu_custom_call" | custom-call | bytes 3145728 | tf_op jit(solution)/shard_map/pallas_call | solution.py:197
  45.3 0.0 collective-permute-done.kv_ref
  45.3 0.0 copy-start.3
  45.3 1.0 copy-done.3
  46.3 3.1 %shard_map.77 = (bf16[3,512,256]{2,1,0:T(8,128)(2,1)}, bf16[2,512,256]{2,1,0:T(8,128)(2,1)}, bf16[2,512,512]{2,1,0:T(8,128)(2,1)}) custom-call(f32[512,512]{1,0:T(8,128)} %copy-done.3), custom_call_target="tpu_custom_call" | custom-call | bytes 3145728 | tf_op jit(solution)/shard_map/pallas_call | solution.py:198
  49.4 11.7 %all-to-all-done.1 = f32[32,8,512]{2,1,0:T(8,128)S(1)} async-done(((f32[32,8,512]{2,1,0:T(8,128)}), f32[32,8,512]{2,1,0:T(8,128)S(1)}, u32[]{:S(2)}, u32[]{:S(2)}) %all-to-all-start.1) | async-done | bytes 524320 | tf_op jit(solution)/shard_map/all_to_all | solution.py:175
  61.1 0.0 copy-start.1
  61.1 0.8 copy-done.1
  61.9 5.0 %shard_map.78 = (f32[1024,256]{1,0:T(8,128)}, f32[1024,256]{1,0:T(8,128)}, f32[1024,256]{1,0:T(8,128)}, f32[8,256]{1,0:T(8,128)}) custom-call(bf16[3,512,256]{2,1,0:T(8,128)(2,1)} %get-tuple-element.20.own_key, bf16[2,512,256]{2,1,0:T(8,128)(2,1)} %get-tuple-element.21.own_value, bf16[3,512,256]{2,1,0:T(8,128)(2,1)} %get-tuple-element.22.other_key, ...), custom_call_target="tpu_custom_call" | custom-call | flops 1207959552 | bytes 3145728 | tf_op jit(solution)/shard_map/pallas_call | solution.py:201
  66.9 0.7 broadcast_in_dim.2
  67.7 19.0 %all_to_all.26.every_ref = f32[32,8,256]{2,1,0:T(8,128)} all-to-all(f32[32,8,256]{2,1,0:T(8,128)S(1)} %broadcast_in_dim.2), channel_id=1, replica_groups=mesh['z2'=2,'z1'=2,'z0'=2,'xh'=2,'xl'=2,'y2'=2,'y1'=2,'y0'=2,'c'=2] {'z2..., dimensions={0} | all-to-all | bytes 524288 | tf_op jit(solution)/shard_map/all_to_all | solution.py:175
  86.6 5.5 %shard_map.79 = (f32[512,512]{1,0:T(8,128)}, f32[512,512]{1,0:T(8,128)}, bf16[6,1024,256]{2,1,0:T(8,128)(2,1)}) custom-call(f32[1024,256]{1,0:T(8,128)} %get-tuple-element.25.w1_ref, f32[1024,256]{1,0:T(8,128)} %get-tuple-element.26.w2_ref, f32[1024,256]{1,0:T(8,128)} %get-tuple-element.27.dp_ref, f32[256,512]{1,0:T(8,128)} %bitcast.7, ...), custom_call_target="tpu_custom_call" | custom-call | flops 805306368 | bytes 6291456 | tf_op jit(solution)/shard_map/pallas_call | solution.py:208
  92.1 4.2 %collective-permute-start.1 = (f32[512,512]{1,0:T(8,128)}, f32[512,512]{1,0:T(8,128)S(1)}, u32[]{:S(2)}, u32[]{:S(2)}) collective-permute-start(f32[512,512]{1,0:T(8,128)} %get-tuple-element.33), channel_id=1, source_target_pairs={{0,1},{1,0},{2,3},{3,2},{4,5},{5,4},{6,7},{7,6},{8,9},{9,8},{10,11... | collective-permute-start | bytes 3145736 | tf_op jit(solution)/shard_map/ppermute | solution.py:171
  96.3 0.0 copy-start.2
  96.3 4.5 %shard_map.80 = f32[256,512]{1,0:T(8,128)} custom-call(bf16[6,1024,256]{2,1,0:T(8,128)(2,1)} %get-tuple-element.29.slopes_ref, bf16[2,512,512]{2,1,0:T(8,128)(2,1)} %get-tuple-element.30.own_ref, bf16[2,512,512]{2,1,0:T(8,128)(2,1)} %get-tuple-element.31.other_ref), custom_call_target="tpu_custom_call" | custom-call | flops 805306368 | bytes 4194304 | tf_op jit(solution)/shard_map/pallas_call | solution.py:212
  100.8 4.4 %all-to-all-start.3 = ((f32[32,8,512]{2,1,0:T(8,128)}), f32[32,8,512]{2,1,0:T(8,128)S(1)}, u32[]{:S(2)}, u32[]{:S(2)}) async-start(f32[32,8,512]{2,1,0:T(8,128)} %bitcast.8), calls=%async_computation.3 | async-start | bytes 1048576 | tf_op jit(solution)/shard_map/all_to_all | solution.py:175
  105.2 0.0 collective-permute-done.1
  105.2 0.0 copy-done.2
  105.2 1.2 add.3
  106.4 18.8 %all-to-all-done.3 = f32[32,8,512]{2,1,0:T(8,128)S(1)} async-done(((f32[32,8,512]{2,1,0:T(8,128)}), f32[32,8,512]{2,1,0:T(8,128)S(1)}, u32[]{:S(2)}, u32[]{:S(2)}) %all-to-all-start.3) | async-done | bytes 524320 | tf_op jit(solution)/shard_map/all_to_all | solution.py:175
  125.2 3.6 %all-to-all-start.4 = ((f32[8,64,512]{2,1,0:T(8,128)}), f32[8,64,512]{2,1,0:T(8,128)S(1)}, u32[]{:S(2)}, u32[]{:S(2)}) async-start(f32[8,64,512]{2,1,0:T(8,128)} %bitcast.3), calls=%async_computation.4 | async-start | bytes 2097152 | tf_op jit(solution)/shard_map/all_to_all | solution.py:175
  128.8 0.6 fusion.1
  129.4 13.8 %all-to-all-done.4 = f32[8,64,512]{2,1,0:T(8,128)S(1)} async-done(((f32[8,64,512]{2,1,0:T(8,128)}), f32[8,64,512]{2,1,0:T(8,128)S(1)}, u32[]{:S(2)}, u32[]{:S(2)}) %all-to-all-start.4) | async-done | bytes 1048608 | tf_op jit(solution)/shard_map/all_to_all | solution.py:175
  143.3 0.1 reduce_sum.19
  143.3 0.7 fusion
  (1 shorter events, 0.0 us)
Async XLA Ops:
  19.9 22.3 %copy-start = (f32[8,64,512]{2,1,0:T(8,128)}, f32[8,64,512]{2,1,0:T(8,128)S(1)}, u32[]{:S(2)}) copy-start(f32[8,64,512]{2,1,0:T(8,128)S(1)} %all_to_all.25) | copy-start | bytes 3145732
  19.9 25.4 %collective-permute-start = (f32[512,512]{1,0:T(8,128)S(1)}, f32[512,512]{1,0:T(8,128)S(1)}, u32[]{:S(2)}, u32[]{:S(2)}) collective-permute-start(f32[512,512]{1,0:T(8,128)S(1)} %bitcast.4), channel_id=1, source_target_pairs={{0,1},{1,0},{2,3},{3,2},{4,5},{5,4},{6,7},{7,6},{8,9},{9,8},{10,11... | collective-permute-start | bytes 3145736 | tf_op jit(solution)/shard_map/ppermute | solution.py:171
  27.2 33.9 %all-to-all-start.1 = ((f32[32,8,512]{2,1,0:T(8,128)}), f32[32,8,512]{2,1,0:T(8,128)S(1)}, u32[]{:S(2)}, u32[]{:S(2)}) async-start(f32[32,8,512]{2,1,0:T(8,128)} %get-tuple-element.24), calls=%async_computation.1 | async-start | bytes 1048576 | tf_op jit(solution)/shard_map/all_to_all | solution.py:175
  45.3 1.0 copy-start.3
  61.1 0.8 copy-start.1
  92.1 13.1 %collective-permute-start.1 = (f32[512,512]{1,0:T(8,128)}, f32[512,512]{1,0:T(8,128)S(1)}, u32[]{:S(2)}, u32[]{:S(2)}) collective-permute-start(f32[512,512]{1,0:T(8,128)} %get-tuple-element.33), channel_id=1, source_target_pairs={{0,1},{1,0},{2,3},{3,2},{4,5},{5,4},{6,7},{7,6},{8,9},{9,8},{10,11... | collective-permute-start | bytes 3145736 | tf_op jit(solution)/shard_map/ppermute | solution.py:171
  96.3 8.9 %copy-start.2 = (f32[512,512]{1,0:T(8,128)S(1)}, f32[512,512]{1,0:T(8,128)}, u32[]{:S(2)}) copy-start(f32[512,512]{1,0:T(8,128)} %get-tuple-element.32) | copy-start | bytes 3145732
  100.8 24.4 %all-to-all-start.3 = ((f32[32,8,512]{2,1,0:T(8,128)}), f32[32,8,512]{2,1,0:T(8,128)S(1)}, u32[]{:S(2)}, u32[]{:S(2)}) async-start(f32[32,8,512]{2,1,0:T(8,128)} %bitcast.8), calls=%async_computation.3 | async-start | bytes 1048576 | tf_op jit(solution)/shard_map/all_to_all | solution.py:175
  125.2 18.1 %all-to-all-start.4 = ((f32[8,64,512]{2,1,0:T(8,128)}), f32[8,64,512]{2,1,0:T(8,128)S(1)}, u32[]{:S(2)}, u32[]{:S(2)}) async-start(f32[8,64,512]{2,1,0:T(8,128)} %bitcast.3), calls=%async_computation.4 | async-start | bytes 2097152 | tf_op jit(solution)/shard_map/all_to_all | solution.py:175

commit v3 on v2

--- a/solution.py
+++ b/solution.py
@@ -8,22 +8,26 @@
 LAMBDA = 0.5
 PB = ("z2", "z1", "z0", "xh")
 KA = ("xl", "y2", "y1", "y0", "c")
-KEY_GROUP = ("xh", "xl", "y0")
-KEYS_IN = 8
+RING = ("xh", "xl")
+PAIR = "y0"
+AROUND = 4
+NEAR = 2
+KEYS_IN = NEAR * AROUND
 QUERY_GROUP = ("z2", "z1", "z0", "y2", "y1")
 QUERIES_IN = 32
 CORE = "c"
 STRIP = 256
 F32, BF16 = jnp.float32, jnp.bfloat16
-VMEM_LIMIT = 56 * 1024 * 1024
-
-
-def call(body, out_shape, flops, moved):
+VMEM_LIMIT = 16 * 1024 * 1024
+
+
+def call(body, out_shape, flops, moved, **given):
     return pl.pallas_call(
         body,
         out_shape=out_shape,
         cost_estimate=pl.CostEstimate(flops=flops, bytes_accessed=moved, transcendentals=0),
         compiler_params=pltpu.CompilerParams(vmem_limit_bytes=VMEM_LIMIT),
+        **given,
     )
 
 
@@ -47,24 +51,37 @@
     return jnp.concatenate(blocks, axis=1)
 
 
-def lay_out(queries_ref, grad_ref, key_ref, value_ref, kv_ref, qg_ref):
-    wide = key_ref.shape[1]
-    for n in range(kv_ref.shape[0]):
-        kv_ref[n, :, :wide] = key_ref[...]
-        kv_ref[n, :, wide:] = value_ref[...]
-    for n in range(qg_ref.shape[0]):
-        qg_ref[n, :, :wide] = queries_ref[...]
-        qg_ref[n, :, wide:] = grad_ref[...]
-
-
-def split_keys(kv_ref, key_ref, value_ref, turned_ref):
-    wide = kv_ref.shape[1] // 2
-    for n, part in enumerate(parts(kv_ref[:, :wide], 3)):
-        key_ref[n] = part
-    for n, part in enumerate(parts(kv_ref[:, wide:], 2)):
-        value_ref[n] = part
-    for n, part in enumerate(parts(kv_ref[...].T, 2)):
-        turned_ref[n] = part
+def lay_out(left_ref, right_ref, out_ref):
+    wide = left_ref.shape[1]
+    for n in range(out_ref.shape[0]):
+        out_ref[n, :, :wide] = left_ref[...]
+        out_ref[n, :, wide:] = right_ref[...]
+
+
+def lay_once(left_ref, right_ref, out_ref):
+    wide = left_ref.shape[1]
+    out_ref[:, :wide] = left_ref[...]
+    out_ref[:, wide:] = right_ref[...]
+
+
+def stack(*refs):
+    *in_refs, out_ref = refs
+    rows = in_refs[0].shape[0]
+    for n, ref in enumerate(in_refs):
+        out_ref[pl.ds(n * rows, rows), :] = ref[...]
+
+
+def split_keys(*refs):
+    *in_refs, key_ref, value_ref, turned_ref = refs
+    rows, wide = in_refs[0].shape[0], in_refs[0].shape[1] // 2
+    for at, ref in enumerate(in_refs):
+        here = pl.ds(at * rows, rows)
+        for n, part in enumerate(parts(ref[:, :wide], 3)):
+            key_ref[n, here, :] = part
+        for n, part in enumerate(parts(ref[:, wide:], 2)):
+            value_ref[n, here, :] = part
+        for n, part in enumerate(parts(ref[...].T, 2)):
+            turned_ref[n, :, here] = part
 
 
 def forward(own_key, own_value, other_key, other_value, qg_ref, w1_ref, w2_ref, dp_ref, stats_ref):
@@ -98,6 +115,8 @@
             dp_ref[there, :] = (
                 dot(v_hi, g_hi, ((1,), (1,))) + dot(v_hi, g_lo, ((1,), (1,))) + dot(v_lo, g_hi, ((1,), (1,)))
             )
+    numbers = []
+    columns = qg_ref.shape[0]
     for head, w_ref in enumerate((w1_ref, w2_ref)):
         mass = jnp.zeros_like(tops[head])
         lean = jnp.zeros_like(tops[head])
@@ -107,10 +126,11 @@
             w_ref[here, :] = weight
             mass = mass + jnp.sum(weight, axis=0, keepdims=True)
             lean = lean + jnp.sum(weight * dp_ref[here, :], axis=0, keepdims=True)
-        stats_ref[head : head + 1, :] = tops[head]
-        stats_ref[2 + head : 3 + head, :] = mass
-        stats_ref[4 + head : 5 + head, :] = lean
-    stats_ref[6:8, :] = jnp.zeros_like(stats_ref[6:8, :])
+        numbers.append((tops[head], mass, lean))
+    blank = jnp.zeros((2, columns), F32)
+    stats = jnp.concatenate([pair[n] for n in range(3) for pair in numbers] + [blank], axis=0)
+    for n in range(stats_ref.shape[0]):
+        stats_ref[n] = stats
 
 
 def key_side(w1_ref, w2_ref, dp_ref, qg_ref, stats_ref, every_ref, own_ref, other_ref, slopes_ref):
@@ -121,14 +141,15 @@
     factor = jnp.exp(every[:, 0:2, :] - top[None])
     total = jnp.sum(every[:, 2:4, :] * factor, axis=0)
     delta = jnp.sum(every[:, 4:6, :] * factor, axis=0) / total
-    rescale = jnp.exp(stats_ref[0:2, :] - top) / total
+    rescale = jnp.exp(stats_ref[0, 0:2, :] - top) / total
     g_hi, g_lo = parts(qg_ref[:, 2 * half :], 2)
-    query = [parts(qg_ref[:, first : first + half] * scale, 2) for first in (0, half)]
-    rows = own_ref.shape[0]
-    for which, out_ref in enumerate((own_ref, other_ref)):
-        for start in range(0, rows, STRIP):
+    query = [parts(qg_ref[:, at : at + half] * scale, 2) for at in (0, half)]
+    first = 0
+    for out_ref in (own_ref, other_ref):
+        for start in range(0, out_ref.shape[0], STRIP):
             here = pl.ds(start, STRIP)
-            there = pl.ds(which * rows + start, STRIP)
+            there = pl.ds(first, STRIP)
+            first += STRIP
             dp = dp_ref[there, :]
             p1 = w1_ref[there, :] * rescale[0:1]
             p2 = w2_ref[there, :] * (-LAMBDA * rescale[1:2])
@@ -167,8 +188,43 @@
     out_ref[:, wide + half :] = product(half, half, 4) * scale
 
 
-def swap(x):
-    return lax.ppermute(x, CORE, [(0, 1), (1, 0)])
+def add_moved(own_ref, moved_ref, *out_refs):
+    rows = out_refs[0].shape[0]
+    for n, out_ref in enumerate(out_refs):
+        here = pl.ds(n * rows, rows)
+        out_ref[...] = own_ref[here, :] + moved_ref[here, :]
+
+
+def add_ring(*refs):
+    *in_refs, near_ref, far_ref = refs
+    total = in_refs[0][...]
+    for ref in in_refs[1:]:
+        total = total + ref[...]
+    rows = near_ref.shape[0]
+    near_ref[...] = total[:rows]
+    far_ref[...] = total[rows:]
+
+
+def add_pair(near_ref, came_ref, left_ref, right_ref):
+    wide = left_ref.shape[1]
+    total = near_ref[...] + came_ref[...]
+    left_ref[...] = total[:, :wide]
+    right_ref[...] = total[:, wide:]
+
+
+def add_blocks(parts_ref, left_ref, right_ref):
+    wide = left_ref.shape[1]
+    total = jnp.sum(parts_ref[...], axis=0)
+    left_ref[...] = total[:, :wide]
+    right_ref[...] = total[:, wide:]
+
+
+def swap(x, axis):
+    return lax.ppermute(x, axis, [(0, 1), (1, 0)])
+
+
+def around(x, step):
+    return lax.ppermute(x, RING, [(n, (n + step) % AROUND) for n in range(AROUND)])
 
 
 def exchange(x, axes):
@@ -179,43 +235,47 @@
     wide = values.shape[1]
     own_keys, own_rows = key_pair.shape[0], queries.shape[0]
     rows, columns = KEYS_IN * own_keys, QUERIES_IN * own_rows
-    kv, qg = call(
-        lay_out,
-        (shape(F32, KEYS_IN, own_keys, 2 * wide), shape(F32, QUERIES_IN, own_rows, 2 * wide)),
-        0,
-        4 * 2 * wide * (rows + columns),
-    )(queries, grad_out, key_pair, values)
-    kv_own = exchange(kv, KEY_GROUP).reshape(rows, 2 * wide)
-    kv_other = swap(kv_own)
+    block = 4 * 2 * wide * rows
+    kv = call(lay_once, shape(F32, own_keys, 2 * wide), 0, block // 4)(key_pair, values)
+    qg = call(lay_out, shape(F32, QUERIES_IN, own_rows, 2 * wide), 0, block // 2)(queries, grad_out)
+    kv_pair = call(stack, shape(F32, NEAR * own_keys, 2 * wide), 10**10, block // 2)(kv, swap(kv, PAIR))
+    kv_own = [kv_pair] + [around(kv_pair, -n) for n in range(1, AROUND)]
+    kv_other = [swap(x, CORE) for x in kv_own]
     qg_all = exchange(qg, QUERY_GROUP).reshape(columns, 2 * wide)
     split = call(
         split_keys,
         (shape(BF16, 3, rows, wide), shape(BF16, 2, rows, wide), shape(BF16, 2, 2 * wide, rows)),
         0,
-        4 * 2 * wide * rows * 3,
-    )
-    own_key, own_value, own_turned = split(kv_own)
-    other_key, other_value, other_turned = split(kv_other)
+        3 * block,
+    )
+    own_key, own_value, own_turned = split(*kv_own)
+    other_key, other_value, other_turned = split(*kv_other)
     big = shape(F32, 2 * rows, columns)
     pairs = 2 * rows * columns
     w1, w2, dp, stats = call(
-        forward, (big, big, big, shape(F32, 8, columns)), 2 * pairs * wide * 9, 4 * pairs * 3
+        forward, (big, big, big, shape(F32, QUERIES_IN, 8, columns)), 2 * pairs * wide * 9, 4 * pairs * 3
     )(own_key, own_value, other_key, other_value, qg_all)
-    every = exchange(
-        jnp.broadcast_to(stats[None], (QUERIES_IN,) + stats.shape), QUERY_GROUP
-    ).reshape((QUERIES_IN,) + stats.shape)
+    every = exchange(stats, QUERY_GROUP)
     half_grad = shape(F32, rows, 2 * wide)
-    dkv_own, dkv_other, slopes = call(
-        key_side, (half_grad, half_grad, shape(BF16, 6, 2 * rows, columns)), 2 * pairs * wide * 6, 4 * pairs * 6
+    own, other, slopes = call(
+        key_side,
+        (half_grad, half_grad, shape(BF16, 6, 2 * rows, columns)),
+        2 * pairs * wide * 6,
+        4 * pairs * 6,
     )(w1, w2, dp, qg_all, stats, every)
-    moved = swap(dkv_other)
+    moved = swap(other, CORE)
     dq = call(query_side, shape(F32, columns, 2 * wide), 2 * pairs * wide * 6, 4 * pairs * 4)(
         slopes, own_turned, other_turned
     )
-    dq_sum = jnp.sum(exchange(dq.reshape(QUERIES_IN, own_rows, 2 * wide), QUERY_GROUP), axis=0)
-    dkv = (dkv_own + moved).reshape(KEYS_IN, own_keys, 2 * wide)
-    dkv_sum = jnp.sum(exchange(dkv, KEY_GROUP), axis=0)
-    return dq_sum[:, :wide], dq_sum[:, wide:], dkv_sum[:, :wide], dkv_sum[:, wide:]
+    dq_parts = exchange(dq.reshape(QUERIES_IN, own_rows, 2 * wide), QUERY_GROUP)
+    attended, grad_queries = call(
+        add_blocks, (shape(F32, own_rows, wide),) * 2, 0, block // 2
+    )(dq_parts)
+    mine, *away = call(add_moved, (shape(F32, NEAR * own_keys, 2 * wide),) * AROUND, 0, block)(own, moved)
+    landed = [around(x, n + 1) for n, x in enumerate(away)]
+    near, far = call(add_ring, (shape(F32, own_keys, 2 * wide),) * NEAR, 0, block)(mine, *landed)
+    grad_keys, grad_values = call(add_pair, (shape(F32, own_keys, wide),) * 2, 0, block // 4)(near, swap(far, PAIR))
+    return attended, grad_queries, grad_keys, grad_values
 
 
 def solution(mesh):

time: 145 us -> 116 us (0.80)
  the two profiles are of different devices: /device:TPU:1 before, /device:TPU:42 now
where the time goes in v3:
time: 116 us; the launch traced here: 115 us
  starting transfers between devices  59.4 us (51%)
  blocking collectives  23.8 us (21%)
  waiting for transfers between devices  16.5 us (14%)
  Pallas kernels  9.62 us (8%)
  local copies, waits for them, and re-layouts  5.02 us (4%)
    all_to_all x1, blocking collectives, exchange(): return lax.all_to_all(x, axes, 0, 0, tiled=True)  23.8 us
    all_to_all x2, starting transfers between devices, exchange(): return lax.all_to_all(x, axes, 0, 0, tiled=True)  23.6 us
    ppermute x6, starting transfers between devices, around(): lax.ppermute(x, RING, [(n, (n + step) % AROUND) for n in range(AROUND)])  20 us
    ppermute x7, starting transfers between devices, swap(): return lax.ppermute(x, axis, [(0, 1), (1, 0)])  15.9 us
    ppermute x6, waiting for transfers between devices, around(): lax.ppermute(x, RING, [(n, (n + step) % AROUND) for n in range(AROUND)])  12.5 us
    unnamed x16, local copies, waits for them, and re-layouts  5.02 us
    ppermute x7, waiting for transfers between devices, swap(): return lax.ppermute(x, axis, [(0, 1), (1, 0)])  4.05 us
    pallas_call x1, Pallas kernels, per_device(): call(key_side, (half_grad, half_grad, shape(BF16, 6, 2 * rows, columns)),...  2.42 us
  transfers between devices with their start and end apart: 15, of which 6 were waited for; matrix products, arithmetic and copies ran while one was open for 0% of the time, Pallas kernels for 4%

profile of v3, /device:TPU:42, one launch (start us, length us, event | category | flops | bytes accessed | tf_op | source)
XLA Modules:
  0.0 115.3 jit_solution(939386012202295661)
XLA Ops:
  0.6 0.8 copy-done.4
  1.5 0.8 copy-done.5
  2.3 3.3 %collective-permute-start = (f32[64,512]{1,0:T(8,128)S(1)}, f32[64,512]{1,0:T(8,128)S(1)}, u32[]{:S(2)}, u32[]{:S(2)}) collective-permute-start(f32[64,512]{1,0:T(8,128)S(1)} %shard_map.75.refs_0_), channel_id=1, source_target_pairs={{0,2},{2,0},{1,3},{3,1},{4,6},{6,4},{5,7},{7,5},{8,10},{10,8},{9,1... | collective-permute-start | bytes 393224 | tf_op jit(solution)/shard_map/ppermute | solution.py:223
  5.6 0.7 copy-done.6
  6.3 0.7 copy-done.7
  7.0 0.8 shard_map.79
  7.8 15.8 %all-to-all-start = ((f32[32,8,512]{2,1,0:T(8,128)}), f32[32,8,512]{2,1,0:T(8,128)S(1)}, u32[]{:S(2)}, u32[]{:S(2)}) async-start(f32[32,8,512]{2,1,0:T(8,128)} %shard_map.79), calls=%async_computation | async-start | bytes 1048576 | tf_op jit(solution)/shard_map/all_to_all | solution.py:231
  23.7 3.4 %collective-permute-start.3 = (f32[128,512]{1,0:T(8,128)S(1)}, f32[128,512]{1,0:T(8,128)S(1)}, u32[]{:S(2)}, u32[]{:S(2)}) collective-permute-start(f32[128,512]{1,0:T(8,128)S(1)} %shard_map.76.refs_0_), channel_id=1, source_target_pairs={{0,16},{16,32},{32,48},{48,0},{1,17},{17,33},{33,49},{49,1},{2,18}... | collective-permute-start | bytes 786440 | tf_op jit(solution)/shard_map/ppermute | solution.py:227
  27.1 3.0 %collective-permute-start.2 = (f32[128,512]{1,0:T(8,128)S(1)}, f32[128,512]{1,0:T(8,128)S(1)}, u32[]{:S(2)}, u32[]{:S(2)}) collective-permute-start(f32[128,512]{1,0:T(8,128)S(1)} %shard_map.76.refs_0_), channel_id=1, source_target_pairs={{0,32},{16,48},{32,0},{48,16},{1,33},{17,49},{33,1},{49,17},{2,34}... | collective-permute-start | bytes 786440 | tf_op jit(solution)/shard_map/ppermute | solution.py:227
  30.2 4.1 %collective-permute-start.1 = (f32[128,512]{1,0:T(8,128)S(1)}, f32[128,512]{1,0:T(8,128)S(1)}, u32[]{:S(2)}, u32[]{:S(2)}) collective-permute-start(f32[128,512]{1,0:T(8,128)S(1)} %shard_map.76.refs_0_), channel_id=1, source_target_pairs={{0,48},{16,0},{32,16},{48,32},{1,49},{17,1},{33,17},{49,33},{2,50}... | collective-permute-start | bytes 786440 | tf_op jit(solution)/shard_map/ppermute | solution.py:227
  34.2 1.9 %collective-permute-start.4 = (f32[128,512]{1,0:T(8,128)S(1)}, f32[128,512]{1,0:T(8,128)S(1)}, u32[]{:S(2)}, u32[]{:S(2)}) collective-permute-start(f32[128,512]{1,0:T(8,128)S(1)} %shard_map.76.refs_0_), channel_id=1, source_target_pairs={{0,1},{1,0},{2,3},{3,2},{4,5},{5,4},{6,7},{7,6},{8,9},{9,8},{10,11... | collective-permute-start | bytes 786440 | tf_op jit(solution)/shard_map/ppermute | solution.py:223
  36.2 2.4 %collective-permute-start.7 = (f32[128,512]{1,0:T(8,128)S(1)}, f32[128,512]{1,0:T(8,128)S(1)}, u32[]{:S(2)}, u32[]{:S(2)}) collective-permute-start(f32[128,512]{1,0:T(8,128)S(1)} %collective-permute-done.3.refs_3_), channel_id=1, source_target_pairs={{0,1},{1,0},{2,3},{3,2},{4,5},{5,4},{6,7},{7,6},{8,9},{9,8},{10,11... | collective-permute-start | bytes 786440 | tf_op jit(solution)/shard_map/ppermute | solution.py:223
  38.6 1.2 %collective-permute-done.2.refs_2_ = f32[128,512]{1,0:T(8,128)S(1)} collective-permute-done((f32[128,512]{1,0:T(8,128)S(1)}, f32[128,512]{1,0:T(8,128)S(1)}, u32[]{:S(2)}, u32[]{:S(2)}) %collective-permute-start.2) | collective-permute-done | bytes 262176 | tf_op jit(solution)/shard_map/ppermute | solution.py:227
  39.8 1.9 %collective-permute-start.6 = (f32[128,512]{1,0:T(8,128)S(1)}, f32[128,512]{1,0:T(8,128)S(1)}, u32[]{:S(2)}, u32[]{:S(2)}) collective-permute-start(f32[128,512]{1,0:T(8,128)S(1)} %collective-permute-done.2.refs_2_), channel_id=1, source_target_pairs={{0,1},{1,0},{2,3},{3,2},{4,5},{5,4},{6,7},{7,6},{8,9},{9,8},{10,11... | collective-permute-start | bytes 786440 | tf_op jit(solution)/shard_map/ppermute | solution.py:223
  41.7 1.3 %collective-permute-done.1.refs_1_ = f32[128,512]{1,0:T(8,128)S(1)} collective-permute-done((f32[128,512]{1,0:T(8,128)S(1)}, f32[128,512]{1,0:T(8,128)S(1)}, u32[]{:S(2)}, u32[]{:S(2)}) %collective-permute-start.1) | collective-permute-done | bytes 262176 | tf_op jit(solution)/shard_map/ppermute | solution.py:227
  43.1 1.9 %collective-permute-start.5 = (f32[128,512]{1,0:T(8,128)S(1)}, f32[128,512]{1,0:T(8,128)S(1)}, u32[]{:S(2)}, u32[]{:S(2)}) collective-permute-start(f32[128,512]{1,0:T(8,128)S(1)} %collective-permute-done.1.refs_1_), channel_id=1, source_target_pairs={{0,1},{1,0},{2,3},{3,2},{4,5},{5,4},{6,7},{7,6},{8,9},{9,8},{10,11... | collective-permute-start | bytes 786440 | tf_op jit(solution)/shard_map/ppermute | solution.py:223
  45.6 1.0 copy-done
  47.1 1.0 copy-done.2
  48.1 1.8 %shard_map.80 = (f32[1024,256]{1,0:T(8,128)S(1)}, f32[1024,256]{1,0:T(8,128)S(1)}, f32[1024,256]{1,0:T(8,128)S(1)}, f32[32,8,256]{2,1,0:T(8,128)S(1)}) custom-call(bf16[3,512,256]{2,1,0:T(8,128)(2,1)S(1)} %get-tuple-element.27.own_key, bf16[2,512,256]{2,1,0:T(8,128)(2,1)S(1)} %get-tuple-element.28.own_value, ...), custom_call_target="tpu_custom_call" | custom-call | flops 1207959552 | bytes 3145728 | tf_op jit(solution)/shard_map/pallas_call | solution.py:255
  50.0 23.8 %all_to_all.15.every_ref = f32[32,8,256]{2,1,0:T(8,128)S(1)} all-to-all(f32[32,8,256]{2,1,0:T(8,128)S(1)} %get-tuple-element.34.stats_ref), channel_id=1, replica_groups=mesh['z2'=2,'z1'=2,'z0'=2,'xh'=2,'xl'=2,'y2'=2,'y1'=2,'y0'=2,'c'=2] {'z2..., dimensions={0} | all-to-all | bytes 524288 | tf_op jit(solution)/shard_map/all_to_all | solution.py:231
  73.8 2.4 %shard_map.81 = (f32[512,512]{1,0:T(8,128)S(1)}, f32[512,512]{1,0:T(8,128)}, bf16[6,1024,256]{2,1,0:T(8,128)(2,1)S(1)}) custom-call(f32[1024,256]{1,0:T(8,128)S(1)} %get-tuple-element.31.w1_ref, f32[1024,256]{1,0:T(8,128)S(1)} %get-tuple-element.32.w2_ref, f32[1024,256]{1,0:T(8,128)S(1)} %get-tuple-element.33.dp_ref, f32[256,512]{1,0:T(8,128)S(1)} %bitcast.3, ...), custom_call_target="tpu_custom_call" | custom-call | flops 805306368 | bytes 6291456 | tf_op jit(solution)/shard_map/pallas_call | solution.py:260
  76.2 1.9 %collective-permute-start.8 = (f32[512,512]{1,0:T(8,128)}, f32[512,512]{1,0:T(8,128)S(1)}, u32[]{:S(2)}, u32[]{:S(2)}) collective-permute-start(f32[512,512]{1,0:T(8,128)} %get-tuple-element.41), channel_id=1, source_target_pairs={{0,1},{1,0},{2,3},{3,2},{4,5},{5,4},{6,7},{7,6},{8,9},{9,8},{10,11... | collective-permute-start | bytes 3145736 | tf_op jit(solution)/shard_map/ppermute | solution.py:223
  78.1 1.9 %shard_map.82 = f32[256,512]{1,0:T(8,128)} custom-call(bf16[6,1024,256]{2,1,0:T(8,128)(2,1)S(1)} %get-tuple-element.35.slopes_ref, bf16[2,512,512]{2,1,0:T(8,128)(2,1)S(1)} %copy-done.1, bf16[2,512,512]{2,1,0:T(8,128)(2,1)S(1)} %copy-done.3), custom_call_target="tpu_custom_call" | custom-call | flops 805306368 | bytes 4194304 | tf_op jit(solution)/shard_map/pallas_call | solution.py:267
  80.0 7.7 %all-to-all-start.2 = ((f32[32,8,512]{2,1,0:T(8,128)}), f32[32,8,512]{2,1,0:T(8,128)S(1)}, u32[]{:S(2)}, u32[]{:S(2)}) async-start(f32[32,8,512]{2,1,0:T(8,128)} %bitcast.1), calls=%async_computation.2 | async-start | bytes 1048576 | tf_op jit(solution)/shard_map/all_to_all | solution.py:231
  87.9 2.5 %collective-permute-start.9 = (f32[128,512]{1,0:T(8,128)S(1)}, f32[128,512]{1,0:T(8,128)S(1)}, u32[]{:S(2)}, u32[]{:S(2)}) collective-permute-start(f32[128,512]{1,0:T(8,128)S(1)} %get-tuple-element.43), channel_id=1, source_target_pairs={{0,16},{16,32},{32,48},{48,0},{1,17},{17,33},{33,49},{49,1},{2,18}... | collective-permute-start | bytes 786440 | tf_op jit(solution)/shard_map/ppermute | solution.py:227
  90.4 3.3 %collective-permute-start.10 = (f32[128,512]{1,0:T(8,128)S(1)}, f32[128,512]{1,0:T(8,128)S(1)}, u32[]{:S(2)}, u32[]{:S(2)}) collective-permute-start(f32[128,512]{1,0:T(8,128)S(1)} %get-tuple-element.44), channel_id=1, source_target_pairs={{0,32},{16,48},{32,0},{48,16},{1,33},{17,49},{33,1},{49,17},{2,34}... | collective-permute-start | bytes 786440 | tf_op jit(solution)/shard_map/ppermute | solution.py:227
  93.7 3.6 %collective-permute-start.11 = (f32[128,512]{1,0:T(8,128)S(1)}, f32[128,512]{1,0:T(8,128)S(1)}, u32[]{:S(2)}, u32[]{:S(2)}) collective-permute-start(f32[128,512]{1,0:T(8,128)S(1)} %get-tuple-element.45), channel_id=1, source_target_pairs={{0,48},{16,0},{32,16},{48,32},{1,49},{17,1},{33,17},{49,33},{2,50}... | collective-permute-start | bytes 786440 | tf_op jit(solution)/shard_map/ppermute | solution.py:227
  97.4 1.6 %collective-permute-done.9.refs_1_ = f32[128,512]{1,0:T(8,128)S(1)} collective-permute-done((f32[128,512]{1,0:T(8,128)S(1)}, f32[128,512]{1,0:T(8,128)S(1)}, u32[]{:S(2)}, u32[]{:S(2)}) %collective-permute-start.9) | collective-permute-done | bytes 262176 | tf_op jit(solution)/shard_map/ppermute | solution.py:227
  99.0 4.1 %collective-permute-done.10.refs_2_ = f32[128,512]{1,0:T(8,128)S(1)} collective-permute-done((f32[128,512]{1,0:T(8,128)S(1)}, f32[128,512]{1,0:T(8,128)S(1)}, u32[]{:S(2)}, u32[]{:S(2)}) %collective-permute-start.10) | collective-permute-done | bytes 262176 | tf_op jit(solution)/shard_map/ppermute | solution.py:227
  103.1 4.2 %collective-permute-done.11.refs_3_ = f32[128,512]{1,0:T(8,128)S(1)} collective-permute-done((f32[128,512]{1,0:T(8,128)S(1)}, f32[128,512]{1,0:T(8,128)S(1)}, u32[]{:S(2)}, u32[]{:S(2)}) %collective-permute-start.11) | collective-permute-done | bytes 262176 | tf_op jit(solution)/shard_map/ppermute | solution.py:227
  107.3 2.6 %collective-permute-start.12 = (f32[64,512]{1,0:T(8,128)S(1)}, f32[64,512]{1,0:T(8,128)S(1)}, u32[]{:S(2)}, u32[]{:S(2)}) collective-permute-start(f32[64,512]{1,0:T(8,128)S(1)} %get-tuple-element.47), channel_id=1, source_target_pairs={{0,2},{2,0},{1,3},{3,1},{4,6},{6,4},{5,7},{7,5},{8,10},{10,8},{9,1... | collective-permute-start | bytes 393224 | tf_op jit(solution)/shard_map/ppermute | solution.py:223
  110.6 4.0 %collective-permute-done.12.came_ref = f32[64,512]{1,0:T(8,128)S(1)} collective-permute-done((f32[64,512]{1,0:T(8,128)S(1)}, f32[64,512]{1,0:T(8,128)S(1)}, u32[]{:S(2)}, u32[]{:S(2)}) %collective-permute-start.12) | collective-permute-done | bytes 131104 | tf_op jit(solution)/shard_map/ppermute | solution.py:223
  (27 shorter events, 2.7 us)
Async XLA Ops:
  0.6 0.8 copy-start.4
  1.5 0.8 copy-start.5
  2.3 21.4 %collective-permute-start = (f32[64,512]{1,0:T(8,128)S(1)}, f32[64,512]{1,0:T(8,128)S(1)}, u32[]{:S(2)}, u32[]{:S(2)}) collective-permute-start(f32[64,512]{1,0:T(8,128)S(1)} %shard_map.75.refs_0_), channel_id=1, source_target_pairs={{0,2},{2,0},{1,3},{3,1},{4,6},{6,4},{5,7},{7,5},{8,10},{10,8},{9,1... | collective-permute-start | bytes 393224 | tf_op jit(solution)/shard_map/ppermute | solution.py:223
  5.6 0.7 copy-start.6
  6.3 0.7 copy-start.7
  7.8 40.3 %all-to-all-start = ((f32[32,8,512]{2,1,0:T(8,128)}), f32[32,8,512]{2,1,0:T(8,128)S(1)}, u32[]{:S(2)}, u32[]{:S(2)}) async-start(f32[32,8,512]{2,1,0:T(8,128)} %shard_map.79), calls=%async_computation | async-start | bytes 1048576 | tf_op jit(solution)/shard_map/all_to_all | solution.py:231
  23.7 12.4 %collective-permute-start.3 = (f32[128,512]{1,0:T(8,128)S(1)}, f32[128,512]{1,0:T(8,128)S(1)}, u32[]{:S(2)}, u32[]{:S(2)}) collective-permute-start(f32[128,512]{1,0:T(8,128)S(1)} %shard_map.76.refs_0_), channel_id=1, source_target_pairs={{0,16},{16,32},{32,48},{48,0},{1,17},{17,33},{33,49},{49,1},{2,18}... | collective-permute-start | bytes 786440 | tf_op jit(solution)/shard_map/ppermute | solution.py:227
  27.1 12.7 %collective-permute-start.2 = (f32[128,512]{1,0:T(8,128)S(1)}, f32[128,512]{1,0:T(8,128)S(1)}, u32[]{:S(2)}, u32[]{:S(2)}) collective-permute-start(f32[128,512]{1,0:T(8,128)S(1)} %shard_map.76.refs_0_), channel_id=1, source_target_pairs={{0,32},{16,48},{32,0},{48,16},{1,33},{17,49},{33,1},{49,17},{2,34}... | collective-permute-start | bytes 786440 | tf_op jit(solution)/shard_map/ppermute | solution.py:227
  30.2 12.9 %collective-permute-start.1 = (f32[128,512]{1,0:T(8,128)S(1)}, f32[128,512]{1,0:T(8,128)S(1)}, u32[]{:S(2)}, u32[]{:S(2)}) collective-permute-start(f32[128,512]{1,0:T(8,128)S(1)} %shard_map.76.refs_0_), channel_id=1, source_target_pairs={{0,48},{16,0},{32,16},{48,32},{1,49},{17,1},{33,17},{49,33},{2,50}... | collective-permute-start | bytes 786440 | tf_op jit(solution)/shard_map/ppermute | solution.py:227
  34.2 12.3 %collective-permute-start.4 = (f32[128,512]{1,0:T(8,128)S(1)}, f32[128,512]{1,0:T(8,128)S(1)}, u32[]{:S(2)}, u32[]{:S(2)}) collective-permute-start(f32[128,512]{1,0:T(8,128)S(1)} %shard_map.76.refs_0_), channel_id=1, source_target_pairs={{0,1},{1,0},{2,3},{3,2},{4,5},{5,4},{6,7},{7,6},{8,9},{9,8},{10,11... | collective-permute-start | bytes 786440 | tf_op jit(solution)/shard_map/ppermute | solution.py:223
  36.2 10.4 %collective-permute-start.7 = (f32[128,512]{1,0:T(8,128)S(1)}, f32[128,512]{1,0:T(8,128)S(1)}, u32[]{:S(2)}, u32[]{:S(2)}) collective-permute-start(f32[128,512]{1,0:T(8,128)S(1)} %collective-permute-done.3.refs_3_), channel_id=1, source_target_pairs={{0,1},{1,0},{2,3},{3,2},{4,5},{5,4},{6,7},{7,6},{8,9},{9,8},{10,11... | collective-permute-start | bytes 786440 | tf_op jit(solution)/shard_map/ppermute | solution.py:223
  39.8 6.7 %collective-permute-start.6 = (f32[128,512]{1,0:T(8,128)S(1)}, f32[128,512]{1,0:T(8,128)S(1)}, u32[]{:S(2)}, u32[]{:S(2)}) collective-permute-start(f32[128,512]{1,0:T(8,128)S(1)} %collective-permute-done.2.refs_2_), channel_id=1, source_target_pairs={{0,1},{1,0},{2,3},{3,2},{4,5},{5,4},{6,7},{7,6},{8,9},{9,8},{10,11... | collective-permute-start | bytes 786440 | tf_op jit(solution)/shard_map/ppermute | solution.py:223
  43.1 3.5 %collective-permute-start.5 = (f32[128,512]{1,0:T(8,128)S(1)}, f32[128,512]{1,0:T(8,128)S(1)}, u32[]{:S(2)}, u32[]{:S(2)}) collective-permute-start(f32[128,512]{1,0:T(8,128)S(1)} %collective-permute-done.1.refs_1_), channel_id=1, source_target_pairs={{0,1},{1,0},{2,3},{3,2},{4,5},{5,4},{6,7},{7,6},{8,9},{9,8},{10,11... | collective-permute-start | bytes 786440 | tf_op jit(solution)/shard_map/ppermute | solution.py:223
  45.5 1.0 copy-start
  47.1 1.0 copy-start.2
  49.9 28.2 %copy-start.1 = (bf16[2,512,512]{2,1,0:T(8,128)(2,1)S(1)}, bf16[2,512,512]{2,1,0:T(8,128)(2,1)}, u32[]{:S(2)}) copy-start(bf16[2,512,512]{2,1,0:T(8,128)(2,1)} %copy-done) | copy-start | bytes 3145732
  50.0 28.2 %copy-start.3 = (bf16[2,512,512]{2,1,0:T(8,128)(2,1)S(1)}, bf16[2,512,512]{2,1,0:T(8,128)(2,1)}, u32[]{:S(2)}) copy-start(bf16[2,512,512]{2,1,0:T(8,128)(2,1)} %copy-done.2) | copy-start | bytes 3145732
  76.2 11.6 %collective-permute-start.8 = (f32[512,512]{1,0:T(8,128)}, f32[512,512]{1,0:T(8,128)S(1)}, u32[]{:S(2)}, u32[]{:S(2)}) collective-permute-start(f32[512,512]{1,0:T(8,128)} %get-tuple-element.41), channel_id=1, source_target_pairs={{0,1},{1,0},{2,3},{3,2},{4,5},{5,4},{6,7},{7,6},{8,9},{9,8},{10,11... | collective-permute-start | bytes 3145736 | tf_op jit(solution)/shard_map/ppermute | solution.py:223
  80.0 29.9 %all-to-all-start.2 = ((f32[32,8,512]{2,1,0:T(8,128)}), f32[32,8,512]{2,1,0:T(8,128)S(1)}, u32[]{:S(2)}, u32[]{:S(2)}) async-start(f32[32,8,512]{2,1,0:T(8,128)} %bitcast.1), calls=%async_computation.2 | async-start | bytes 1048576 | tf_op jit(solution)/shard_map/all_to_all | solution.py:231
  87.9 11.1 %collective-permute-start.9 = (f32[128,512]{1,0:T(8,128)S(1)}, f32[128,512]{1,0:T(8,128)S(1)}, u32[]{:S(2)}, u32[]{:S(2)}) collective-permute-start(f32[128,512]{1,0:T(8,128)S(1)} %get-tuple-element.43), channel_id=1, source_target_pairs={{0,16},{16,32},{32,48},{48,0},{1,17},{17,33},{33,49},{49,1},{2,18}... | collective-permute-start | bytes 786440 | tf_op jit(solution)/shard_map/ppermute | solution.py:227
  90.4 12.7 %collective-permute-start.10 = (f32[128,512]{1,0:T(8,128)S(1)}, f32[128,512]{1,0:T(8,128)S(1)}, u32[]{:S(2)}, u32[]{:S(2)}) collective-permute-start(f32[128,512]{1,0:T(8,128)S(1)} %get-tuple-element.44), channel_id=1, source_target_pairs={{0,32},{16,48},{32,0},{48,16},{1,33},{17,49},{33,1},{49,17},{2,34}... | collective-permute-start | bytes 786440 | tf_op jit(solution)/shard_map/ppermute | solution.py:227
  93.7 13.6 %collective-permute-start.11 = (f32[128,512]{1,0:T(8,128)S(1)}, f32[128,512]{1,0:T(8,128)S(1)}, u32[]{:S(2)}, u32[]{:S(2)}) collective-permute-start(f32[128,512]{1,0:T(8,128)S(1)} %get-tuple-element.45), channel_id=1, source_target_pairs={{0,48},{16,0},{32,16},{48,32},{1,49},{17,1},{33,17},{49,33},{2,50}... | collective-permute-start | bytes 786440 | tf_op jit(solution)/shard_map/ppermute | solution.py:227
  107.3 7.3 %collective-permute-start.12 = (f32[64,512]{1,0:T(8,128)S(1)}, f32[64,512]{1,0:T(8,128)S(1)}, u32[]{:S(2)}, u32[]{:S(2)}) collective-permute-start(f32[64,512]{1,0:T(8,128)S(1)} %get-tuple-element.47), channel_id=1, source_target_pairs={{0,2},{2,0},{1,3},{3,1},{4,6},{6,4},{5,7},{7,5},{8,10},{10,8},{9,1... | collective-permute-start | bytes 393224 | tf_op jit(solution)/shard_map/ppermute | solution.py:223

commit v4 on v3

v4 whole, which is shorter than its diff:
```python
import functools

import jax
import jax.numpy as jnp
from jax import lax
from jax.experimental import pallas as pl
from jax.experimental.pallas import tpu as pltpu
from jax.sharding import Mesh, PartitionSpec as P

LAMBDA = 0.5
PB = ("z2", "z1", "z0", "xh")
KA = ("xl", "y2", "y1", "y0", "c")
RING = ("xh", "xl")
PAIR = "y0"
AROUND = 4
NEAR = 2
KEYS_IN = NEAR * AROUND
QUERY_GROUP = ("z2", "z1", "z0", "y2", "y1")
QUERIES_IN = 32
CORE = "c"
STRIP = 256
F32, BF16 = jnp.float32, jnp.bfloat16
VMEM_LIMIT = 16 * 1024 * 1024


def call(body, out_shape, flops, moved, **given):
    return pl.pallas_call(
        body,
        out_shape=out_shape,
        cost_estimate=pl.CostEstimate(flops=flops, bytes_accessed=moved, transcendentals=0),
        compiler_params=pltpu.CompilerParams(vmem_limit_bytes=VMEM_LIMIT),
        **given,
    )


def shape(dtype, *dims):
    return jax.ShapeDtypeStruct(dims, dtype)


def parts(x, count):
    out = []
    for _ in range(count):
        out.append(x.astype(BF16))
        x = x - out[-1].astype(F32)
    return out


def dot(left, right, dims=((1,), (0,))):
    return lax.dot_general(left, right, (dims, ((), ())), preferred_element_type=F32)


def beside(*blocks):
    return jnp.concatenate(blocks, axis=1)


def lay_out(queries_ref, grad_ref, key_ref, value_ref, kv_ref, qg_ref, row_ref, sems):
    wide = key_ref.shape[1]
    copies = [
        pltpu.make_async_copy(source, target.at[:, pl.ds(first, wide)], sems.at[n])
        for n, (source, target, first) in enumerate(
            (
                (queries_ref, row_ref, 0),
                (grad_ref, row_ref, wide),
                (key_ref, kv_ref, 0),
                (value_ref, kv_ref, wide),
            )
        )
    ]
    for copy in copies:
        copy.start()
    for copy in copies[:2]:
        copy.wait()
    rows = row_ref[...]
    for n in range(qg_ref.shape[0]):
        qg_ref[n] = rows
    for copy in copies[2:]:
        copy.wait()


def stack(*refs):
    *in_refs, out_ref = refs
    rows = in_refs[0].shape[0]
    for n, ref in enumerate(in_refs):
        out_ref[pl.ds(n * rows, rows), :] = ref[...]


def halves(row):
    middle = row.shape[1] // 2
    return [row[:, :middle], row[:, middle:]]


def turn(*refs):
    *in_refs, out_ref = refs
    rows = in_refs[0].shape[0]
    for at, ref in enumerate(in_refs):
        for n, part in enumerate(parts(ref[...].T, 2)):
            out_ref[n, :, pl.ds(at * rows, rows)] = part


def forward(*refs):
    *in_refs, qg_ref, w1_ref, w2_ref, dp_ref, stats_ref, top_ref = refs
    half = qg_ref.shape[1] // 4
    scale = half ** (-0.5)
    g_hi, g_lo = parts(qg_ref[:, 2 * half :], 2)
    query = []
    for first in (0, half):
        hi, mid, low = parts(qg_ref[:, first : first + half] * scale, 3)
        query.append((beside(hi, mid), beside(low, hi)))
    rows = 2 * in_refs[0].shape[0]
    across = ((1,), (1,))
    tops = [None, None]
    for at in range(len(in_refs) // 2):
        both = jnp.concatenate([in_refs[2 * at][...], in_refs[2 * at + 1][...]], axis=0)
        there = pl.ds(at * rows, rows)
        for head, w_ref in enumerate((w1_ref, w2_ref)):
            hi, mid, low = parts(both[:, head * half : (head + 1) * half], 3)
            main, rest = query[head]
            score = (
                dot(beside(hi, hi), main, across)
                + dot(beside(mid, mid), main, across)
                + dot(beside(hi, low), rest, across)
            )
            w_ref[there, :] = score
            top = jnp.max(score, axis=0, keepdims=True)
            tops[head] = top if tops[head] is None else jnp.maximum(tops[head], top)
        v_hi, v_lo = parts(both[:, 2 * half :], 2)
        dp_ref[there, :] = dot(v_hi, g_hi, across) + dot(v_hi, g_lo, across) + dot(v_lo, g_hi, across)
    numbers = []
    for head, w_ref in enumerate((w1_ref, w2_ref)):
        mass = jnp.zeros_like(tops[head])
        lean = jnp.zeros_like(tops[head])
        for start in range(0, w_ref.shape[0], STRIP):
            here = pl.ds(start, STRIP)
            weight = jnp.exp(w_ref[here, :] - tops[head])
            w_ref[here, :] = weight
            mass = mass + jnp.sum(weight, axis=0, keepdims=True)
            lean = lean + jnp.sum(weight * dp_ref[here, :], axis=0, keepdims=True)
        numbers += halves(tops[head] + jnp.log(mass)) + halves(lean / mass)
    stats = jnp.concatenate(numbers, axis=0)
    for n in range(stats_ref.shape[0]):
        stats_ref[n] = stats
    top_ref[...] = jnp.concatenate(tops, axis=0)


def key_side(first, w1_ref, w2_ref, dp_ref, qg_ref, top_ref, every_ref, out_ref, slopes_ref):
    half = qg_ref.shape[1] // 4
    scale = half ** (-0.5)
    rescale, delta = [], []
    for head in range(2):
        logs = beside(every_ref[:, 4 * head, :], every_ref[:, 4 * head + 1, :])
        means = beside(every_ref[:, 4 * head + 2, :], every_ref[:, 4 * head + 3, :])
        top = jnp.max(logs, axis=0, keepdims=True)
        share = jnp.exp(logs - top)
        total = jnp.sum(share, axis=0, keepdims=True)
        delta.append(jnp.sum(share * means, axis=0, keepdims=True) / total)
        rescale.append(jnp.exp(top_ref[head : head + 1, :] - top) / total)
    g_hi, g_lo = parts(qg_ref[:, 2 * half :], 2)
    query = [parts(qg_ref[:, at : at + half] * scale, 2) for at in (0, half)]
    for start in range(0, out_ref.shape[0], STRIP):
        here = pl.ds(start, STRIP)
        there = pl.ds(first + start, STRIP)
        dp = dp_ref[there, :]
        p1 = w1_ref[there, :] * rescale[0]
        p2 = w2_ref[there, :] * (-LAMBDA * rescale[1])
        slopes = (p1 * (dp - delta[0]), p2 * (dp - delta[1]))
        mix_hi, mix_lo = parts(p1 + p2, 2)
        slopes_ref[0, here, :] = mix_hi
        slopes_ref[1, here, :] = mix_lo
        for head in range(2):
            hi, lo = parts(slopes[head], 2)
            slopes_ref[2 + 2 * head, here, :] = hi
            slopes_ref[3 + 2 * head, here, :] = lo
            q_hi, q_lo = query[head]
            both = dot(hi, beside(q_hi, q_lo))
            out_ref[here, head * half : (head + 1) * half] = both[:, :half] + both[:, half:] + dot(lo, q_hi)
        out_ref[here, 2 * half :] = dot(mix_hi, g_hi) + dot(mix_hi, g_lo) + dot(mix_lo, g_hi)


def key_side_and_turn(first, count, *refs):
    blocks, rest = refs[:count], refs[count:]
    turn(*blocks, rest[-1])
    key_side(first, *rest[:-1])


def query_side(own_ref, other_ref, turned_ref, out_ref):
    rows = own_ref.shape[1]
    wide = turned_ref.shape[1] // 2
    half = wide // 2
    scale = half ** (-0.5)

    def product(first, count, at):
        total = None
        for which, slopes_ref in enumerate((own_ref, other_ref)):
            there = pl.ds(which * rows, rows)
            hi, lo = turned_ref[0, first : first + count, there], turned_ref[1, first : first + count, there]
            s_hi, s_lo = slopes_ref[at], slopes_ref[at + 1]
            term = dot(hi, s_hi) + dot(hi, s_lo) + dot(lo, s_hi)
            total = term if total is None else total + term
        return total.T

    out_ref[:, :wide] = product(wide, wide, 0)
    out_ref[:, wide : wide + half] = product(0, half, 2) * scale
    out_ref[:, wide + half :] = product(half, half, 4) * scale


def add_moved(own_ref, moved_ref, *out_refs):
    rows = out_refs[0].shape[0]
    for n, out_ref in enumerate(out_refs):
        here = pl.ds(n * rows, rows)
        out_ref[...] = own_ref[here, :] + moved_ref[here, :]


def add_two(left_ref, right_ref, out_ref):
    out_ref[...] = left_ref[...] + right_ref[...]


def add_ring(*refs):
    *in_refs, near_ref, far_ref = refs
    total = in_refs[0][...]
    for ref in in_refs[1:]:
        total = total + ref[...]
    rows = near_ref.shape[0]
    near_ref[...] = total[:rows]
    far_ref[...] = total[rows:]


def add_pair(near_ref, came_ref, left_ref, right_ref):
    wide = left_ref.shape[1]
    total = near_ref[...] + came_ref[...]
    left_ref[...] = total[:, :wide]
    right_ref[...] = total[:, wide:]


def add_blocks(parts_ref, left_ref, right_ref):
    wide = left_ref.shape[1]
    total = jnp.sum(parts_ref[...], axis=0)
    left_ref[...] = total[:, :wide]
    right_ref[...] = total[:, wide:]


def in_hbm(x):
    return pltpu.with_memory_space_constraint(x, pltpu.HBM)


def swap(x, axis):
    return lax.ppermute(x, axis, [(0, 1), (1, 0)])


def around(x, step):
    return lax.ppermute(x, RING, [(n, (n + step) % AROUND) for n in range(AROUND)])


def exchange(x, axes):
    return lax.all_to_all(x, axes, 0, 0, tiled=True)


def per_device(queries, key_pair, values, grad_out):
    wide = values.shape[1]
    own_keys, own_rows = key_pair.shape[0], queries.shape[0]
    rows, columns = KEYS_IN * own_keys, QUERIES_IN * own_rows
    block = 4 * 2 * wide * rows
    kv, qg = call(
        lay_out,
        (shape(F32, own_keys, 2 * wide), shape(F32, QUERIES_IN, own_rows, 2 * wide)),
        0,
        block // 2,
        in_specs=[pl.BlockSpec(memory_space=pltpu.HBM)] * 4,
        scratch_shapes=[pltpu.VMEM((own_rows, 2 * wide), F32), pltpu.SemaphoreType.DMA((4,))],
    )(*(in_hbm(x) for x in (queries, grad_out, key_pair, values)))
    kv_pair = call(stack, shape(F32, NEAR * own_keys, 2 * wide), 10**10, block // 2)(kv, swap(kv, PAIR))
    kv_own = [kv_pair] + [around(kv_pair, -n) for n in range(1, AROUND)]
    kv_other = [swap(x, CORE) for x in kv_own]
    qg_all = exchange(qg, QUERY_GROUP).reshape(columns, 2 * wide)
    big = shape(F32, 2 * rows, columns)
    pairs = 2 * rows * columns
    stats_shape = shape(F32, QUERIES_IN, 8, columns // 2)
    w1, w2, dp, stats, tops = call(
        forward, (big, big, big, stats_shape, shape(F32, 2, columns)), 2 * pairs * wide * 9, 4 * pairs * 3
    )(*kv_own, *kv_other, qg_all)
    every = exchange(stats, QUERY_GROUP)
    half_out = (shape(F32, rows, 2 * wide), shape(BF16, 6, rows, columns))
    other, other_slopes = call(
        functools.partial(key_side, rows), half_out, pairs * wide * 6, 4 * pairs * 3
    )(w1, w2, dp, qg_all, tops, every)
    moved = swap(other, CORE)
    own, own_slopes, turned = call(
        functools.partial(key_side_and_turn, 0, 2 * AROUND),
        half_out + (shape(BF16, 2, 2 * wide, 2 * rows),),
        pairs * wide * 6,
        4 * pairs * 3,
    )(*kv_own, *kv_other, w1, w2, dp, qg_all, tops, every)
    dq = call(query_side, shape(F32, columns, 2 * wide), 2 * pairs * wide * 6, 4 * pairs * 4)(
        own_slopes, other_slopes, turned
    )
    dq_parts = exchange(dq.reshape(QUERIES_IN, own_rows, 2 * wide), QUERY_GROUP)
    attended, grad_queries = call(
        add_blocks, (shape(F32, own_rows, wide),) * 2, 0, block // 2
    )(dq_parts)
    mine, *away = call(add_moved, (shape(F32, NEAR * own_keys, 2 * wide),) * AROUND, 0, block)(own, moved)
    right, across, left = (around(x, n + 1) for n, x in enumerate(away))
    mine = call(add_two, shape(F32, NEAR * own_keys, 2 * wide), 10**10, block)(mine, across)
    near, far = call(add_ring, (shape(F32, own_keys, 2 * wide),) * NEAR, 0, block)(mine, right, left)
    grad_keys, grad_values = call(add_pair, (shape(F32, own_keys, wide),) * 2, 0, block // 4)(near, swap(far, PAIR))
    return attended, grad_queries, grad_keys, grad_values


def solution(mesh):
    fine = Mesh(mesh.devices.reshape((2,) * 9), PB + KA)
    by_query, by_key = P(KA + PB, None), P(PB + KA, None)
    return jax.shard_map(
        per_device,
        mesh=fine,
        in_specs=(by_query, by_key, by_key, by_query),
        out_specs=(by_query, by_query, by_key, by_key),
        check_vma=False,
    )
```

time: 116 us -> 109 us (0.940)
  the two profiles are of different devices: /device:TPU:42 before, /device:TPU:8 now
where the time goes in v4:
time: 109 us; the launch traced here: 108 us
  starting transfers between devices  58 us (53%)
  blocking collectives  24.5 us (22%)
  waiting for transfers between devices  15.2 us (14%)
  Pallas kernels  9.17 us (8%)
    all_to_all x1, blocking collectives, exchange(): return lax.all_to_all(x, axes, 0, 0, tiled=True)  24.5 us
    ppermute x6, starting transfers between devices, around(): lax.ppermute(x, RING, [(n, (n + step) % AROUND) for n in range(AROUND)])  22.7 us
    ppermute x7, starting transfers between devices, swap(): return lax.ppermute(x, axis, [(0, 1), (1, 0)])  20.8 us
    all_to_all x2, starting transfers between devices, exchange(): return lax.all_to_all(x, axes, 0, 0, tiled=True)  14.5 us
    ppermute x6, waiting for transfers between devices, around(): lax.ppermute(x, RING, [(n, (n + step) % AROUND) for n in range(AROUND)])  6.68 us
    all_to_all x2, waiting for transfers between devices, exchange(): return lax.all_to_all(x, axes, 0, 0, tiled=True)  5.99 us
    ppermute x7, waiting for transfers between devices, swap(): return lax.ppermute(x, axis, [(0, 1), (1, 0)])  2.49 us
  transfers between devices with their start and end apart: 15, of which 6 were waited for; matrix products, arithmetic and copies ran while one was open for 0% of the time, Pallas kernels for 4%

profile of v4, /device:TPU:8, one launch (start us, length us, event | category | flops | bytes accessed | tf_op | source)
XLA Modules:
  0.0 107.7 jit_solution(18359732553108596203)
XLA Ops:
  0.6 1.7 %shard_map.75 = (f32[64,512]{1,0:T(8,128)S(1)}, f32[32,8,512]{2,1,0:T(8,128)}) custom-call(f32[8,256]{1,0:T(8,128)} %queries_ref.1, f32[8,256]{1,0:T(8,128)} %grad_ref.1, f32[64,256]{1,0:T(8,128)} %key_ref.1, f32[64,256]{1,0:T(8,128)} %value_ref.1), custom_call_target="tpu_custom_call" | custom-call | bytes 524288 | tf_op jit(solution)/shard_map/pallas_call | solution.py:262
  2.4 7.7 %collective-permute-start = (f32[64,512]{1,0:T(8,128)S(1)}, f32[64,512]{1,0:T(8,128)S(1)}, u32[]{:S(2)}, u32[]{:S(2)}) collective-permute-start(f32[64,512]{1,0:T(8,128)S(1)} %get-tuple-element.26.refs_0_), channel_id=1, source_target_pairs={{0,2},{2,0},{1,3},{3,1},{4,6},{6,4},{5,7},{7,5},{8,10},{10,8},{9,1... | collective-permute-start | bytes 393224 | tf_op jit(solution)/shard_map/ppermute | solution.py:246
  10.1 10.6 %all-to-all-start = ((f32[32,8,512]{2,1,0:T(8,128)}), f32[32,8,512]{2,1,0:T(8,128)S(1)}, u32[]{:S(2)}, u32[]{:S(2)}) async-start(f32[32,8,512]{2,1,0:T(8,128)} %get-tuple-element.27), calls=%async_computation | async-start | bytes 1048576 | tf_op jit(solution)/shard_map/all_to_all | solution.py:254
  20.7 0.0 collective-permute-done.refs_1_
  20.8 3.4 %collective-permute-start.3 = (f32[128,512]{1,0:T(8,128)S(1)}, f32[128,512]{1,0:T(8,128)S(1)}, u32[]{:S(2)}, u32[]{:S(2)}) collective-permute-start(f32[128,512]{1,0:T(8,128)S(1)} %shard_map.76.refs_0_), channel_id=1, source_target_pairs={{0,16},{16,32},{32,48},{48,0},{1,17},{17,33},{33,49},{49,1},{2,18}... | collective-permute-start | bytes 786440 | tf_op jit(solution)/shard_map/ppermute | solution.py:250
  24.2 4.6 %collective-permute-start.2 = (f32[128,512]{1,0:T(8,128)S(1)}, f32[128,512]{1,0:T(8,128)S(1)}, u32[]{:S(2)}, u32[]{:S(2)}) collective-permute-start(f32[128,512]{1,0:T(8,128)S(1)} %shard_map.76.refs_0_), channel_id=1, source_target_pairs={{0,32},{16,48},{32,0},{48,16},{1,33},{17,49},{33,1},{49,17},{2,34}... | collective-permute-start | bytes 786440 | tf_op jit(solution)/shard_map/ppermute | solution.py:250
  28.8 3.3 %collective-permute-start.1 = (f32[128,512]{1,0:T(8,128)S(1)}, f32[128,512]{1,0:T(8,128)S(1)}, u32[]{:S(2)}, u32[]{:S(2)}) collective-permute-start(f32[128,512]{1,0:T(8,128)S(1)} %shard_map.76.refs_0_), channel_id=1, source_target_pairs={{0,48},{16,0},{32,16},{48,32},{1,49},{17,1},{33,17},{49,33},{2,50}... | collective-permute-start | bytes 786440 | tf_op jit(solution)/shard_map/ppermute | solution.py:250
  32.2 1.9 %collective-permute-start.4 = (f32[128,512]{1,0:T(8,128)S(1)}, f32[128,512]{1,0:T(8,128)S(1)}, u32[]{:S(2)}, u32[]{:S(2)}) collective-permute-start(f32[128,512]{1,0:T(8,128)S(1)} %shard_map.76.refs_0_), channel_id=1, source_target_pairs={{0,1},{1,0},{2,3},{3,2},{4,5},{5,4},{6,7},{7,6},{8,9},{9,8},{10,11... | collective-permute-start | bytes 786440 | tf_op jit(solution)/shard_map/ppermute | solution.py:246
  34.1 0.0 collective-permute-done.3.refs_3_
  34.1 2.4 %collective-permute-start.7 = (f32[128,512]{1,0:T(8,128)S(1)}, f32[128,512]{1,0:T(8,128)S(1)}, u32[]{:S(2)}, u32[]{:S(2)}) collective-permute-start(f32[128,512]{1,0:T(8,128)S(1)} %collective-permute-done.3.refs_3_), channel_id=1, source_target_pairs={{0,1},{1,0},{2,3},{3,2},{4,5},{5,4},{6,7},{7,6},{8,9},{9,8},{10,11... | collective-permute-start | bytes 786440 | tf_op jit(solution)/shard_map/ppermute | solution.py:246
  36.5 1.4 %collective-permute-done.2.refs_2_ = f32[128,512]{1,0:T(8,128)S(1)} collective-permute-done((f32[128,512]{1,0:T(8,128)S(1)}, f32[128,512]{1,0:T(8,128)S(1)}, u32[]{:S(2)}, u32[]{:S(2)}) %collective-permute-start.2) | collective-permute-done | bytes 262176 | tf_op jit(solution)/shard_map/ppermute | solution.py:250
  38.0 1.9 %collective-permute-start.6 = (f32[128,512]{1,0:T(8,128)S(1)}, f32[128,512]{1,0:T(8,128)S(1)}, u32[]{:S(2)}, u32[]{:S(2)}) collective-permute-start(f32[128,512]{1,0:T(8,128)S(1)} %collective-permute-done.2.refs_2_), channel_id=1, source_target_pairs={{0,1},{1,0},{2,3},{3,2},{4,5},{5,4},{6,7},{7,6},{8,9},{9,8},{10,11... | collective-permute-start | bytes 786440 | tf_op jit(solution)/shard_map/ppermute | solution.py:246
  39.9 2.4 %collective-permute-start.5 = (f32[128,512]{1,0:T(8,128)S(1)}, f32[128,512]{1,0:T(8,128)S(1)}, u32[]{:S(2)}, u32[]{:S(2)}) collective-permute-start(f32[128,512]{1,0:T(8,128)S(1)} %collective-permute-done.1.refs_1_), channel_id=1, source_target_pairs={{0,1},{1,0},{2,3},{3,2},{4,5},{5,4},{6,7},{7,6},{8,9},{9,8},{10,11... | collective-permute-start | bytes 786440 | tf_op jit(solution)/shard_map/ppermute | solution.py:246
  42.3 1.1 %collective-permute-done.5.refs_5_ = f32[128,512]{1,0:T(8,128)S(1)} collective-permute-done((f32[128,512]{1,0:T(8,128)S(1)}, f32[128,512]{1,0:T(8,128)S(1)}, u32[]{:S(2)}, u32[]{:S(2)}) %collective-permute-start.5) | collective-permute-done | bytes 262176 | tf_op jit(solution)/shard_map/ppermute | solution.py:246
  43.5 1.9 %shard_map.77 = (f32[1024,256]{1,0:T(8,128)S(1)}, f32[1024,256]{1,0:T(8,128)S(1)}, f32[1024,256]{1,0:T(8,128)S(1)}, f32[32,8,128]{2,1,0:T(8,128)S(1)}, f32[2,256]{1,0:T(2,128)S(1)}) custom-call(f32[128,512]{1,0:T(8,128)S(1)} %shard_map.76.refs_0_, f32[128,512]{1,0:T(8,128)S(1)} %collective-permute-done.1.refs_1_, ...), custom_call_target="tpu_custom_call" | custom-call | flops 1207959552 | bytes 3145728 | tf_op jit(solution)/shard_map/pallas_call | solution.py:277
  45.4 24.5 %all_to_all.15.refs_13_.every_ref = f32[32,8,128]{2,1,0:T(8,128)S(1)} all-to-all(f32[32,8,128]{2,1,0:T(8,128)S(1)} %get-tuple-element.32), channel_id=1, replica_groups=mesh['z2'=2,'z1'=2,'z0'=2,'xh'=2,'xl'=2,'y2'=2,'y1'=2,'y0'=2,'c'=2] {'z2..., dimensions={0} | all-to-all | bytes 262144 | tf_op jit(solution)/shard_map/all_to_all | solution.py:254
  69.9 0.8 shard_map.79
  70.8 1.9 %collective-permute-start.8 = (f32[512,512]{1,0:T(8,128)S(1)}, f32[512,512]{1,0:T(8,128)S(1)}, u32[]{:S(2)}, u32[]{:S(2)}) collective-permute-start(f32[512,512]{1,0:T(8,128)S(1)} %get-tuple-element.39), channel_id=1, source_target_pairs={{0,1},{1,0},{2,3},{3,2},{4,5},{5,4},{6,7},{7,6},{8,9},{9,8},{10,11... | collective-permute-start | bytes 3145736 | tf_op jit(solution)/shard_map/ppermute | solution.py:246
  72.7 1.2 %shard_map.78 = (f32[512,512]{1,0:T(8,128)S(1)}, bf16[6,512,256]{2,1,0:T(8,128)(2,1)S(1)}, bf16[2,512,1024]{2,1,0:T(8,128)(2,1)S(1)}) custom-call(f32[128,512]{1,0:T(8,128)S(1)} %shard_map.76.refs_0_, f32[128,512]{1,0:T(8,128)S(1)} %collective-permute-done.1.refs_1_, f32[128,512]{1,0:T(8,128)S(1)} %collective-permute-done.2.refs_2_, ...), custom_call_target="tpu_custom_call" | custom-call | flops 402653184 | bytes 3145728 | tf_op jit(solution)/shard_map/pallas_call | solution.py:286
  73.9 1.4 %collective-permute-done.8.moved_ref = f32[512,512]{1,0:T(8,128)S(1)} collective-permute-done((f32[512,512]{1,0:T(8,128)S(1)}, f32[512,512]{1,0:T(8,128)S(1)}, u32[]{:S(2)}, u32[]{:S(2)}) %collective-permute-start.8) | collective-permute-done | bytes 1048608 | tf_op jit(solution)/shard_map/ppermute | solution.py:246
  75.3 0.1 shard_map.82
  75.4 4.3 %collective-permute-start.9 = (f32[128,512]{1,0:T(8,128)S(1)}, f32[128,512]{1,0:T(8,128)S(1)}, u32[]{:S(2)}, u32[]{:S(2)}) collective-permute-start(f32[128,512]{1,0:T(8,128)S(1)} %get-tuple-element.41), channel_id=1, source_target_pairs={{0,32},{16,48},{32,0},{48,16},{1,33},{17,49},{33,1},{49,17},{2,34}... | collective-permute-start | bytes 786440 | tf_op jit(solution)/shard_map/ppermute | solution.py:250
  79.7 1.9 %shard_map.80 = f32[256,512]{1,0:T(8,128)} custom-call(bf16[6,512,256]{2,1,0:T(8,128)(2,1)S(1)} %get-tuple-element.33.own_ref, bf16[6,512,256]{2,1,0:T(8,128)(2,1)S(1)} %get-tuple-element.34.other_ref, bf16[2,512,1024]{2,1,0:T(8,128)(2,1)S(1)} %get-tuple-element.35.turned_ref), custom_call_target="tpu_custom_call" | custom-call | flops 805306368 | bytes 4194304 | tf_op jit(solution)/shard_map/pallas_call | solution.py:292
  81.6 3.9 %all-to-all-start.2 = ((f32[32,8,512]{2,1,0:T(8,128)}), f32[32,8,512]{2,1,0:T(8,128)S(1)}, u32[]{:S(2)}, u32[]{:S(2)}) async-start(f32[32,8,512]{2,1,0:T(8,128)} %bitcast.1), calls=%async_computation.2 | async-start | bytes 1048576 | tf_op jit(solution)/shard_map/all_to_all | solution.py:254
  85.5 2.4 %collective-permute-start.10 = (f32[128,512]{1,0:T(8,128)S(1)}, f32[128,512]{1,0:T(8,128)S(1)}, u32[]{:S(2)}, u32[]{:S(2)}) collective-permute-start(f32[128,512]{1,0:T(8,128)S(1)} %get-tuple-element.42), channel_id=1, source_target_pairs={{0,16},{16,32},{32,48},{48,0},{1,17},{17,33},{33,49},{49,1},{2,18}... | collective-permute-start | bytes 786440 | tf_op jit(solution)/shard_map/ppermute | solution.py:250
  87.9 4.7 %collective-permute-start.11 = (f32[128,512]{1,0:T(8,128)S(1)}, f32[128,512]{1,0:T(8,128)S(1)}, u32[]{:S(2)}, u32[]{:S(2)}) collective-permute-start(f32[128,512]{1,0:T(8,128)S(1)} %get-tuple-element.43), channel_id=1, source_target_pairs={{0,48},{16,0},{32,16},{48,32},{1,49},{17,1},{33,17},{49,33},{2,50}... | collective-permute-start | bytes 786440 | tf_op jit(solution)/shard_map/ppermute | solution.py:250
  92.6 4.1 %collective-permute-done.10.refs_1_ = f32[128,512]{1,0:T(8,128)S(1)} collective-permute-done((f32[128,512]{1,0:T(8,128)S(1)}, f32[128,512]{1,0:T(8,128)S(1)}, u32[]{:S(2)}, u32[]{:S(2)}) %collective-permute-start.10) | collective-permute-done | bytes 262176 | tf_op jit(solution)/shard_map/ppermute | solution.py:250
  96.7 1.2 %collective-permute-done.11.refs_2_ = f32[128,512]{1,0:T(8,128)S(1)} collective-permute-done((f32[128,512]{1,0:T(8,128)S(1)}, f32[128,512]{1,0:T(8,128)S(1)}, u32[]{:S(2)}, u32[]{:S(2)}) %collective-permute-start.11) | collective-permute-done | bytes 262176 | tf_op jit(solution)/shard_map/ppermute | solution.py:250
  97.9 2.5 %collective-permute-start.12 = (f32[64,512]{1,0:T(8,128)S(1)}, f32[64,512]{1,0:T(8,128)S(1)}, u32[]{:S(2)}, u32[]{:S(2)}) collective-permute-start(f32[64,512]{1,0:T(8,128)S(1)} %get-tuple-element.45), channel_id=1, source_target_pairs={{0,2},{2,0},{1,3},{3,1},{4,6},{6,4},{5,7},{7,5},{8,10},{10,8},{9,1... | collective-permute-start | bytes 393224 | tf_op jit(solution)/shard_map/ppermute | solution.py:246
  100.4 6.0 %all-to-all-done.2.parts_ref = f32[32,8,512]{2,1,0:T(8,128)S(1)} async-done(((f32[32,8,512]{2,1,0:T(8,128)}), f32[32,8,512]{2,1,0:T(8,128)S(1)}, u32[]{:S(2)}, u32[]{:S(2)}) %all-to-all-start.2) | async-done | bytes 524320 | tf_op jit(solution)/shard_map/all_to_all | solution.py:254
  106.4 0.6 shard_map.81
  107.1 0.7 shard_map.85
  (10 shorter events, 0.1 us)
Async XLA Ops:
  2.4 18.4 %collective-permute-start = (f32[64,512]{1,0:T(8,128)S(1)}, f32[64,512]{1,0:T(8,128)S(1)}, u32[]{:S(2)}, u32[]{:S(2)}) collective-permute-start(f32[64,512]{1,0:T(8,128)S(1)} %get-tuple-element.26.refs_0_), channel_id=1, source_target_pairs={{0,2},{2,0},{1,3},{3,1},{4,6},{6,4},{5,7},{7,5},{8,10},{10,8},{9,1... | collective-permute-start | bytes 393224 | tf_op jit(solution)/shard_map/ppermute | solution.py:246
  10.1 33.3 %all-to-all-start = ((f32[32,8,512]{2,1,0:T(8,128)}), f32[32,8,512]{2,1,0:T(8,128)S(1)}, u32[]{:S(2)}, u32[]{:S(2)}) async-start(f32[32,8,512]{2,1,0:T(8,128)} %get-tuple-element.27), calls=%async_computation | async-start | bytes 1048576 | tf_op jit(solution)/shard_map/all_to_all | solution.py:254
  20.8 13.3 %collective-permute-start.3 = (f32[128,512]{1,0:T(8,128)S(1)}, f32[128,512]{1,0:T(8,128)S(1)}, u32[]{:S(2)}, u32[]{:S(2)}) collective-permute-start(f32[128,512]{1,0:T(8,128)S(1)} %shard_map.76.refs_0_), channel_id=1, source_target_pairs={{0,16},{16,32},{32,48},{48,0},{1,17},{17,33},{33,49},{49,1},{2,18}... | collective-permute-start | bytes 786440 | tf_op jit(solution)/shard_map/ppermute | solution.py:250
  24.2 13.8 %collective-permute-start.2 = (f32[128,512]{1,0:T(8,128)S(1)}, f32[128,512]{1,0:T(8,128)S(1)}, u32[]{:S(2)}, u32[]{:S(2)}) collective-permute-start(f32[128,512]{1,0:T(8,128)S(1)} %shard_map.76.refs_0_), channel_id=1, source_target_pairs={{0,32},{16,48},{32,0},{48,16},{1,33},{17,49},{33,1},{49,17},{2,34}... | collective-permute-start | bytes 786440 | tf_op jit(solution)/shard_map/ppermute | solution.py:250
  28.8 11.1 %collective-permute-start.1 = (f32[128,512]{1,0:T(8,128)S(1)}, f32[128,512]{1,0:T(8,128)S(1)}, u32[]{:S(2)}, u32[]{:S(2)}) collective-permute-start(f32[128,512]{1,0:T(8,128)S(1)} %shard_map.76.refs_0_), channel_id=1, source_target_pairs={{0,48},{16,0},{32,16},{48,32},{1,49},{17,1},{33,17},{49,33},{2,50}... | collective-permute-start | bytes 786440 | tf_op jit(solution)/shard_map/ppermute | solution.py:250
  32.2 10.1 %collective-permute-start.4 = (f32[128,512]{1,0:T(8,128)S(1)}, f32[128,512]{1,0:T(8,128)S(1)}, u32[]{:S(2)}, u32[]{:S(2)}) collective-permute-start(f32[128,512]{1,0:T(8,128)S(1)} %shard_map.76.refs_0_), channel_id=1, source_target_pairs={{0,1},{1,0},{2,3},{3,2},{4,5},{5,4},{6,7},{7,6},{8,9},{9,8},{10,11... | collective-permute-start | bytes 786440 | tf_op jit(solution)/shard_map/ppermute | solution.py:246
  34.1 8.2 %collective-permute-start.7 = (f32[128,512]{1,0:T(8,128)S(1)}, f32[128,512]{1,0:T(8,128)S(1)}, u32[]{:S(2)}, u32[]{:S(2)}) collective-permute-start(f32[128,512]{1,0:T(8,128)S(1)} %collective-permute-done.3.refs_3_), channel_id=1, source_target_pairs={{0,1},{1,0},{2,3},{3,2},{4,5},{5,4},{6,7},{7,6},{8,9},{9,8},{10,11... | collective-permute-start | bytes 786440 | tf_op jit(solution)/shard_map/ppermute | solution.py:246
  38.0 4.4 %collective-permute-start.6 = (f32[128,512]{1,0:T(8,128)S(1)}, f32[128,512]{1,0:T(8,128)S(1)}, u32[]{:S(2)}, u32[]{:S(2)}) collective-permute-start(f32[128,512]{1,0:T(8,128)S(1)} %collective-permute-done.2.refs_2_), channel_id=1, source_target_pairs={{0,1},{1,0},{2,3},{3,2},{4,5},{5,4},{6,7},{7,6},{8,9},{9,8},{10,11... | collective-permute-start | bytes 786440 | tf_op jit(solution)/shard_map/ppermute | solution.py:246
  39.9 3.6 %collective-permute-start.5 = (f32[128,512]{1,0:T(8,128)S(1)}, f32[128,512]{1,0:T(8,128)S(1)}, u32[]{:S(2)}, u32[]{:S(2)}) collective-permute-start(f32[128,512]{1,0:T(8,128)S(1)} %collective-permute-done.1.refs_1_), channel_id=1, source_target_pairs={{0,1},{1,0},{2,3},{3,2},{4,5},{5,4},{6,7},{7,6},{8,9},{9,8},{10,11... | collective-permute-start | bytes 786440 | tf_op jit(solution)/shard_map/ppermute | solution.py:246
  70.8 4.6 %collective-permute-start.8 = (f32[512,512]{1,0:T(8,128)S(1)}, f32[512,512]{1,0:T(8,128)S(1)}, u32[]{:S(2)}, u32[]{:S(2)}) collective-permute-start(f32[512,512]{1,0:T(8,128)S(1)} %get-tuple-element.39), channel_id=1, source_target_pairs={{0,1},{1,0},{2,3},{3,2},{4,5},{5,4},{6,7},{7,6},{8,9},{9,8},{10,11... | collective-permute-start | bytes 3145736 | tf_op jit(solution)/shard_map/ppermute | solution.py:246
  75.4 17.2 %collective-permute-start.9 = (f32[128,512]{1,0:T(8,128)S(1)}, f32[128,512]{1,0:T(8,128)S(1)}, u32[]{:S(2)}, u32[]{:S(2)}) collective-permute-start(f32[128,512]{1,0:T(8,128)S(1)} %get-tuple-element.41), channel_id=1, source_target_pairs={{0,32},{16,48},{32,0},{48,16},{1,33},{17,49},{33,1},{49,17},{2,34}... | collective-permute-start | bytes 786440 | tf_op jit(solution)/shard_map/ppermute | solution.py:250
  81.6 24.8 %all-to-all-start.2 = ((f32[32,8,512]{2,1,0:T(8,128)}), f32[32,8,512]{2,1,0:T(8,128)S(1)}, u32[]{:S(2)}, u32[]{:S(2)}) async-start(f32[32,8,512]{2,1,0:T(8,128)} %bitcast.1), calls=%async_computation.2 | async-start | bytes 1048576 | tf_op jit(solution)/shard_map/all_to_all | solution.py:254
  85.5 11.2 %collective-permute-start.10 = (f32[128,512]{1,0:T(8,128)S(1)}, f32[128,512]{1,0:T(8,128)S(1)}, u32[]{:S(2)}, u32[]{:S(2)}) collective-permute-start(f32[128,512]{1,0:T(8,128)S(1)} %get-tuple-element.42), channel_id=1, source_target_pairs={{0,16},{16,32},{32,48},{48,0},{1,17},{17,33},{33,49},{49,1},{2,18}... | collective-permute-start | bytes 786440 | tf_op jit(solution)/shard_map/ppermute | solution.py:250
  87.9 10.0 %collective-permute-start.11 = (f32[128,512]{1,0:T(8,128)S(1)}, f32[128,512]{1,0:T(8,128)S(1)}, u32[]{:S(2)}, u32[]{:S(2)}) collective-permute-start(f32[128,512]{1,0:T(8,128)S(1)} %get-tuple-element.43), channel_id=1, source_target_pairs={{0,48},{16,0},{32,16},{48,32},{1,49},{17,1},{33,17},{49,33},{2,50}... | collective-permute-start | bytes 786440 | tf_op jit(solution)/shard_map/ppermute | solution.py:250
  97.9 9.2 %collective-permute-start.12 = (f32[64,512]{1,0:T(8,128)S(1)}, f32[64,512]{1,0:T(8,128)S(1)}, u32[]{:S(2)}, u32[]{:S(2)}) collective-permute-start(f32[64,512]{1,0:T(8,128)S(1)} %get-tuple-element.45), channel_id=1, source_target_pairs={{0,2},{2,0},{1,3},{3,1},{4,6},{6,4},{5,7},{7,5},{8,10},{10,8},{9,1... | collective-permute-start | bytes 393224 | tf_op jit(solution)/shard_map/ppermute | solution.py:246

commit v5 on v4

--- a/solution.py
+++ b/solution.py
@@ -91,10 +91,12 @@
 
 def turn(*refs):
     *in_refs, out_ref = refs
-    rows = in_refs[0].shape[0]
-    for at, ref in enumerate(in_refs):
+    at = 0
+    for ref in in_refs:
+        rows = ref.shape[0]
         for n, part in enumerate(parts(ref[...].T, 2)):
-            out_ref[n, :, pl.ds(at * rows, rows)] = part
+            out_ref[n, :, pl.ds(at, rows)] = part
+        at += rows
 
 
 def forward(*refs):
@@ -106,12 +108,13 @@
     for first in (0, half):
         hi, mid, low = parts(qg_ref[:, first : first + half] * scale, 3)
         query.append((beside(hi, mid), beside(low, hi)))
-    rows = 2 * in_refs[0].shape[0]
     across = ((1,), (1,))
     tops = [None, None]
-    for at in range(len(in_refs) // 2):
-        both = jnp.concatenate([in_refs[2 * at][...], in_refs[2 * at + 1][...]], axis=0)
-        there = pl.ds(at * rows, rows)
+    at = 0
+    for some in (in_refs[0:1], in_refs[1:3], in_refs[3:4], in_refs[4:6]):
+        both = jnp.concatenate([ref[...] for ref in some], axis=0)
+        there = pl.ds(at, both.shape[0])
+        at += both.shape[0]
         for head, w_ref in enumerate((w1_ref, w2_ref)):
             hi, mid, low = parts(both[:, head * half : (head + 1) * half], 3)
             main, rest = query[head]
@@ -176,12 +179,6 @@
         out_ref[here, 2 * half :] = dot(mix_hi, g_hi) + dot(mix_hi, g_lo) + dot(mix_lo, g_hi)
 
 
-def key_side_and_turn(first, count, *refs):
-    blocks, rest = refs[:count], refs[count:]
-    turn(*blocks, rest[-1])
-    key_side(first, *rest[:-1])
-
-
 def query_side(own_ref, other_ref, turned_ref, out_ref):
     rows = own_ref.shape[1]
     wide = turned_ref.shape[1] // 2
@@ -203,11 +200,20 @@
     out_ref[:, wide + half :] = product(half, half, 4) * scale
 
 
-def add_moved(own_ref, moved_ref, *out_refs):
+def add_moved(own_ref, moved_ref, _, *refs):
+    *out_refs, _ = refs
     rows = out_refs[0].shape[0]
     for n, out_ref in enumerate(out_refs):
         here = pl.ds(n * rows, rows)
         out_ref[...] = own_ref[here, :] + moved_ref[here, :]
+
+
+def own_half(count, *refs):
+    blocks = refs[:count]
+    *given, other_slopes, out_ref, dq_ref, slopes, turned = refs[count:]
+    key_side(0, *given, out_ref, slopes)
+    turn(*blocks, turned)
+    query_side(slopes, other_slopes, turned, dq_ref)
 
 
 def add_two(left_ref, right_ref, out_ref):
@@ -224,18 +230,14 @@
     far_ref[...] = total[rows:]
 
 
-def add_pair(near_ref, came_ref, left_ref, right_ref):
-    wide = left_ref.shape[1]
+def finish(near_ref, came_ref, parts_ref, keys_ref, values_ref, attended_ref, queries_ref):
+    wide = keys_ref.shape[1]
     total = near_ref[...] + came_ref[...]
-    left_ref[...] = total[:, :wide]
-    right_ref[...] = total[:, wide:]
-
-
-def add_blocks(parts_ref, left_ref, right_ref):
-    wide = left_ref.shape[1]
+    keys_ref[...] = total[:, :wide]
+    values_ref[...] = total[:, wide:]
     total = jnp.sum(parts_ref[...], axis=0)
-    left_ref[...] = total[:, :wide]
-    right_ref[...] = total[:, wide:]
+    attended_ref[...] = total[:, :wide]
+    queries_ref[...] = total[:, wide:]
 
 
 def in_hbm(x):
@@ -268,7 +270,9 @@
         scratch_shapes=[pltpu.VMEM((own_rows, 2 * wide), F32), pltpu.SemaphoreType.DMA((4,))],
     )(*(in_hbm(x) for x in (queries, grad_out, key_pair, values)))
     kv_pair = call(stack, shape(F32, NEAR * own_keys, 2 * wide), 10**10, block // 2)(kv, swap(kv, PAIR))
-    kv_own = [kv_pair] + [around(kv_pair, -n) for n in range(1, AROUND)]
+    right, across, left = (around(kv_pair, -n) for n in range(1, AROUND))
+    first = call(stack, shape(F32, 2 * NEAR * own_keys, 2 * wide), 10**9, block)(kv_pair, across)
+    kv_own = [first, right, left]
     kv_other = [swap(x, CORE) for x in kv_own]
     qg_all = exchange(qg, QUERY_GROUP).reshape(columns, 2 * wide)
     big = shape(F32, 2 * rows, columns)
@@ -283,24 +287,30 @@
         functools.partial(key_side, rows), half_out, pairs * wide * 6, 4 * pairs * 3
     )(w1, w2, dp, qg_all, tops, every)
     moved = swap(other, CORE)
-    own, own_slopes, turned = call(
-        functools.partial(key_side_and_turn, 0, 2 * AROUND),
-        half_out + (shape(BF16, 2, 2 * wide, 2 * rows),),
-        pairs * wide * 6,
-        4 * pairs * 3,
-    )(*kv_own, *kv_other, w1, w2, dp, qg_all, tops, every)
-    dq = call(query_side, shape(F32, columns, 2 * wide), 2 * pairs * wide * 6, 4 * pairs * 4)(
-        own_slopes, other_slopes, turned
-    )
+    own, dq = call(
+        functools.partial(own_half, 6),
+        (shape(F32, rows, 2 * wide), shape(F32, columns, 2 * wide)),
+        3 * pairs * wide * 6,
+        4 * pairs * 4,
+        scratch_shapes=[pltpu.VMEM((6, rows, columns), BF16), pltpu.VMEM((2, 2 * wide, 2 * rows), BF16)],
+    )(*kv_own, *kv_other, w1, w2, dp, qg_all, tops, every, other_slopes)
+    vmem, anywhere = pl.BlockSpec(memory_space=pltpu.VMEM), pl.BlockSpec(memory_space=pl.ANY)
+    mine, *away, dq = call(
+        add_moved,
+        (shape(F32, NEAR * own_keys, 2 * wide),) * AROUND + (shape(F32, columns, 2 * wide),),
+        0,
+        block,
+        in_specs=[vmem, vmem, anywhere],
+        out_specs=[vmem] * AROUND + [anywhere],
+        input_output_aliases={2: AROUND},
+    )(own, moved, dq)
     dq_parts = exchange(dq.reshape(QUERIES_IN, own_rows, 2 * wide), QUERY_GROUP)
-    attended, grad_queries = call(
-        add_blocks, (shape(F32, own_rows, wide),) * 2, 0, block // 2
-    )(dq_parts)
-    mine, *away = call(add_moved, (shape(F32, NEAR * own_keys, 2 * wide),) * AROUND, 0, block)(own, moved)
-    right, across, left = (around(x, n + 1) for n, x in enumerate(away))
-    mine = call(add_two, shape(F32, NEAR * own_keys, 2 * wide), 10**10, block)(mine, across)
+    across, right, left = (around(x, step) for x, step in zip(away, (2, 1, 3)))
+    mine = call(add_two, shape(F32, NEAR * own_keys, 2 * wide), 10**9, block)(mine, across)
     near, far = call(add_ring, (shape(F32, own_keys, 2 * wide),) * NEAR, 0, block)(mine, right, left)
-    grad_keys, grad_values = call(add_pair, (shape(F32, own_keys, wide),) * 2, 0, block // 4)(near, swap(far, PAIR))
+    grad_keys, grad_values, attended, grad_queries = call(
+        finish, (shape(F32, own_keys, wide),) * 2 + (shape(F32, own_rows, wide),) * 2, 0, block
+    )(near, swap(far, PAIR), dq_parts)
     return attended, grad_queries, grad_keys, grad_values
 
 

time: 109 us -> 106 us (0.972)
  the two profiles are of different devices: /device:TPU:8 before, /device:TPU:1 now
where the time goes in v5:
time: 106 us; the launch traced here: 105 us
  starting transfers between devices  61.4 us (58%)
  blocking collectives  22.8 us (22%)
  waiting for transfers between devices  11.9 us (11%)
  Pallas kernels  8 us (8%)
    all_to_all x1, blocking collectives, exchange(): return lax.all_to_all(x, axes, 0, 0, tiled=True)  22.8 us
    ppermute x6, starting transfers between devices, around(): lax.ppermute(x, RING, [(n, (n + step) % AROUND) for n in range(AROUND)])  22 us
    ppermute x6, starting transfers between devices, swap(): return lax.ppermute(x, axis, [(0, 1), (1, 0)])  20.7 us
    all_to_all x2, starting transfers between devices, exchange(): return lax.all_to_all(x, axes, 0, 0, tiled=True)  18.7 us
    ppermute x6, waiting for transfers between devices, around(): lax.ppermute(x, RING, [(n, (n + step) % AROUND) for n in range(AROUND)])  7.05 us
    ppermute x6, waiting for transfers between devices, swap(): return lax.ppermute(x, axis, [(0, 1), (1, 0)])  4.81 us
    pallas_call x1, Pallas kernels, per_device(): call(functools.partial(own_half, 6), (shape(F32, rows, 2 * wide), shape(F...  2.58 us
  transfers between devices with their start and end apart: 14, of which 5 were waited for; matrix products, arithmetic and copies ran while one was open for 0% of the time, Pallas kernels for 3%

profile of v5, /device:TPU:1, one launch (start us, length us, event | category | flops | bytes accessed | tf_op | source)
XLA Modules:
  0.0 104.9 jit_solution(478662142837289018)
XLA Ops:
  0.6 1.7 %shard_map.75 = (f32[64,512]{1,0:T(8,128)S(1)}, f32[32,8,512]{2,1,0:T(8,128)}) custom-call(f32[8,256]{1,0:T(8,128)} %queries_ref.1, f32[8,256]{1,0:T(8,128)} %grad_ref.1, f32[64,256]{1,0:T(8,128)} %key_ref.1, f32[64,256]{1,0:T(8,128)} %value_ref.1), custom_call_target="tpu_custom_call" | custom-call | bytes 524288 | tf_op jit(solution)/shard_map/pallas_call | solution.py:264
  2.4 4.0 %collective-permute-start = (f32[64,512]{1,0:T(8,128)S(1)}, f32[64,512]{1,0:T(8,128)S(1)}, u32[]{:S(2)}, u32[]{:S(2)}) collective-permute-start(f32[64,512]{1,0:T(8,128)S(1)} %get-tuple-element.26.refs_0_), channel_id=1, source_target_pairs={{0,2},{2,0},{1,3},{3,1},{4,6},{6,4},{5,7},{7,5},{8,10},{10,8},{9,1... | collective-permute-start | bytes 393224 | tf_op jit(solution)/shard_map/ppermute | solution.py:248
  6.4 14.8 %all-to-all-start = ((f32[32,8,512]{2,1,0:T(8,128)}), f32[32,8,512]{2,1,0:T(8,128)S(1)}, u32[]{:S(2)}, u32[]{:S(2)}) async-start(f32[32,8,512]{2,1,0:T(8,128)} %get-tuple-element.27), calls=%async_computation | async-start | bytes 1048576 | tf_op jit(solution)/shard_map/all_to_all | solution.py:256
  21.2 0.0 collective-permute-done.refs_1_
  21.3 4.7 %collective-permute-start.1 = (f32[128,512]{1,0:T(8,128)S(1)}, f32[128,512]{1,0:T(8,128)S(1)}, u32[]{:S(2)}, u32[]{:S(2)}) collective-permute-start(f32[128,512]{1,0:T(8,128)S(1)} %shard_map.76.refs_0_), channel_id=1, source_target_pairs={{0,32},{16,48},{32,0},{48,16},{1,33},{17,49},{33,1},{49,17},{2,34}... | collective-permute-start | bytes 786440 | tf_op jit(solution)/shard_map/ppermute | solution.py:252
  25.9 2.2 %collective-permute-start.3 = (f32[128,512]{1,0:T(8,128)S(1)}, f32[128,512]{1,0:T(8,128)S(1)}, u32[]{:S(2)}, u32[]{:S(2)}) collective-permute-start(f32[128,512]{1,0:T(8,128)S(1)} %shard_map.76.refs_0_), channel_id=1, source_target_pairs={{0,16},{16,32},{32,48},{48,0},{1,17},{17,33},{33,49},{49,1},{2,18}... | collective-permute-start | bytes 786440 | tf_op jit(solution)/shard_map/ppermute | solution.py:252
  28.2 4.3 %collective-permute-start.2 = (f32[128,512]{1,0:T(8,128)S(1)}, f32[128,512]{1,0:T(8,128)S(1)}, u32[]{:S(2)}, u32[]{:S(2)}) collective-permute-start(f32[128,512]{1,0:T(8,128)S(1)} %shard_map.76.refs_0_), channel_id=1, source_target_pairs={{0,48},{16,0},{32,16},{48,32},{1,49},{17,1},{33,17},{49,33},{2,50}... | collective-permute-start | bytes 786440 | tf_op jit(solution)/shard_map/ppermute | solution.py:252
  32.4 0.0 collective-permute-done.1.refs_1_
  32.5 4.6 %collective-permute-start.4 = (f32[256,512]{1,0:T(8,128)S(1)}, f32[256,512]{1,0:T(8,128)S(1)}, u32[]{:S(2)}, u32[]{:S(2)}) collective-permute-start(f32[256,512]{1,0:T(8,128)S(1)} %shard_map.77.refs_0_), channel_id=1, source_target_pairs={{0,1},{1,0},{2,3},{3,2},{4,5},{5,4},{6,7},{7,6},{8,9},{9,8},{10,11... | collective-permute-start | bytes 1572872 | tf_op jit(solution)/shard_map/ppermute | solution.py:248
  37.1 0.7 collective-permute-done.3.refs_2_
  37.8 3.4 %collective-permute-start.6 = (f32[128,512]{1,0:T(8,128)S(1)}, f32[128,512]{1,0:T(8,128)S(1)}, u32[]{:S(2)}, u32[]{:S(2)}) collective-permute-start(f32[128,512]{1,0:T(8,128)S(1)} %collective-permute-done.3.refs_2_), channel_id=1, source_target_pairs={{0,1},{1,0},{2,3},{3,2},{4,5},{5,4},{6,7},{7,6},{8,9},{9,8},{10,11... | collective-permute-start | bytes 786440 | tf_op jit(solution)/shard_map/ppermute | solution.py:248
  41.2 1.9 %collective-permute-start.5 = (f32[128,512]{1,0:T(8,128)S(1)}, f32[128,512]{1,0:T(8,128)S(1)}, u32[]{:S(2)}, u32[]{:S(2)}) collective-permute-start(f32[128,512]{1,0:T(8,128)S(1)} %collective-permute-done.2.refs_1_), channel_id=1, source_target_pairs={{0,1},{1,0},{2,3},{3,2},{4,5},{5,4},{6,7},{7,6},{8,9},{9,8},{10,11... | collective-permute-start | bytes 786440 | tf_op jit(solution)/shard_map/ppermute | solution.py:248
  43.1 0.0 collective-permute-done.6.refs_5_
  43.1 1.5 %collective-permute-done.5.refs_4_ = f32[128,512]{1,0:T(8,128)S(1)} collective-permute-done((f32[128,512]{1,0:T(8,128)S(1)}, f32[128,512]{1,0:T(8,128)S(1)}, u32[]{:S(2)}, u32[]{:S(2)}) %collective-permute-start.5) | collective-permute-done | bytes 262176 | tf_op jit(solution)/shard_map/ppermute | solution.py:248
  44.6 0.0 collective-permute-done.4.refs_3_
  44.6 0.0 all-to-all-done
  44.6 1.9 %shard_map.78 = (f32[1024,256]{1,0:T(8,128)S(1)}, f32[1024,256]{1,0:T(8,128)S(1)}, f32[1024,256]{1,0:T(8,128)S(1)}, f32[32,8,128]{2,1,0:T(8,128)S(1)}, f32[2,256]{1,0:T(2,128)S(1)}) custom-call(f32[256,512]{1,0:T(8,128)S(1)} %shard_map.77.refs_0_, f32[128,512]{1,0:T(8,128)S(1)} %collective-permute-done.2.refs_1_, ...), custom_call_target="tpu_custom_call" | custom-call | flops 1207959552 | bytes 3145728 | tf_op jit(solution)/shard_map/pallas_call | solution.py:281
  46.5 22.8 %all_to_all.15.every_ref.refs_11_ = f32[32,8,128]{2,1,0:T(8,128)S(1)} all-to-all(f32[32,8,128]{2,1,0:T(8,128)S(1)} %get-tuple-element.32), channel_id=1, replica_groups=mesh['z2'=2,'z1'=2,'z0'=2,'xh'=2,'xl'=2,'y2'=2,'y1'=2,'y0'=2,'c'=2] {'z2..., dimensions={0} | all-to-all | bytes 262144 | tf_op jit(solution)/shard_map/all_to_all | solution.py:256
  69.3 0.8 shard_map.79
  70.2 3.6 %collective-permute-start.7 = (f32[512,512]{1,0:T(8,128)S(1)}, f32[512,512]{1,0:T(8,128)S(1)}, u32[]{:S(2)}, u32[]{:S(2)}) collective-permute-start(f32[512,512]{1,0:T(8,128)S(1)} %get-tuple-element.35), channel_id=1, source_target_pairs={{0,1},{1,0},{2,3},{3,2},{4,5},{5,4},{6,7},{7,6},{8,9},{9,8},{10,11... | collective-permute-start | bytes 3145736 | tf_op jit(solution)/shard_map/ppermute | solution.py:248
  73.8 2.6 %shard_map.80 = (f32[512,512]{1,0:T(8,128)S(1)}, f32[256,512]{1,0:T(8,128)}) custom-call(f32[256,512]{1,0:T(8,128)S(1)} %shard_map.77.refs_0_, f32[128,512]{1,0:T(8,128)S(1)} %collective-permute-done.2.refs_1_, f32[128,512]{1,0:T(8,128)S(1)} %collective-permute-done.3.refs_2_, f32[256,512]{1,0:T(8,128)S(1)} %collective-permute-done.4.refs_3_, ...), custom_call_target="tpu_custom_call" | custom-call | flops 1207959552 | bytes 4194304 | tf_op jit(solution)/shard_map/pallas_call | solution.py:290
  76.4 0.0 collective-permute-done.7.moved_ref
  76.4 0.1 shard_map.81
  76.5 3.9 %all-to-all-start.2 = ((f32[32,8,512]{2,1,0:T(8,128)}), f32[32,8,512]{2,1,0:T(8,128)S(1)}, u32[]{:S(2)}, u32[]{:S(2)}) async-start(f32[32,8,512]{2,1,0:T(8,128)} %bitcast.1), calls=%async_computation.2 | async-start | bytes 1048576 | tf_op jit(solution)/shard_map/all_to_all | solution.py:256
  80.4 4.4 %collective-permute-start.8 = (f32[128,512]{1,0:T(8,128)S(1)}, f32[128,512]{1,0:T(8,128)S(1)}, u32[]{:S(2)}, u32[]{:S(2)}) collective-permute-start(f32[128,512]{1,0:T(8,128)S(1)} %get-tuple-element.38), channel_id=1, source_target_pairs={{0,32},{16,48},{32,0},{48,16},{1,33},{17,49},{33,1},{49,17},{2,34}... | collective-permute-start | bytes 786440 | tf_op jit(solution)/shard_map/ppermute | solution.py:252
  84.8 1.9 %collective-permute-start.9 = (f32[128,512]{1,0:T(8,128)S(1)}, f32[128,512]{1,0:T(8,128)S(1)}, u32[]{:S(2)}, u32[]{:S(2)}) collective-permute-start(f32[128,512]{1,0:T(8,128)S(1)} %get-tuple-element.39), channel_id=1, source_target_pairs={{0,16},{16,32},{32,48},{48,0},{1,17},{17,33},{33,49},{49,1},{2,18}... | collective-permute-start | bytes 786440 | tf_op jit(solution)/shard_map/ppermute | solution.py:252
  86.7 4.6 %collective-permute-start.10 = (f32[128,512]{1,0:T(8,128)S(1)}, f32[128,512]{1,0:T(8,128)S(1)}, u32[]{:S(2)}, u32[]{:S(2)}) collective-permute-start(f32[128,512]{1,0:T(8,128)S(1)} %get-tuple-element.40), channel_id=1, source_target_pairs={{0,48},{16,0},{32,16},{48,32},{1,49},{17,1},{33,17},{49,33},{2,50}... | collective-permute-start | bytes 786440 | tf_op jit(solution)/shard_map/ppermute | solution.py:252
  91.3 0.3 collective-permute-done.8.right_ref
  91.6 6.1 %collective-permute-done.9.refs_1_ = f32[128,512]{1,0:T(8,128)S(1)} collective-permute-done((f32[128,512]{1,0:T(8,128)S(1)}, f32[128,512]{1,0:T(8,128)S(1)}, u32[]{:S(2)}, u32[]{:S(2)}) %collective-permute-start.9) | collective-permute-done | bytes 262176 | tf_op jit(solution)/shard_map/ppermute | solution.py:252
  97.7 3.2 %collective-permute-start.11 = (f32[64,512]{1,0:T(8,128)S(1)}, f32[64,512]{1,0:T(8,128)S(1)}, u32[]{:S(2)}, u32[]{:S(2)}) collective-permute-start(f32[64,512]{1,0:T(8,128)S(1)} %get-tuple-element.42), channel_id=1, source_target_pairs={{0,2},{2,0},{1,3},{3,1},{4,6},{6,4},{5,7},{7,5},{8,10},{10,8},{9,1... | collective-permute-start | bytes 393224 | tf_op jit(solution)/shard_map/ppermute | solution.py:248
  100.9 3.3 %collective-permute-done.11.came_ref = f32[64,512]{1,0:T(8,128)S(1)} collective-permute-done((f32[64,512]{1,0:T(8,128)S(1)}, f32[64,512]{1,0:T(8,128)S(1)}, u32[]{:S(2)}, u32[]{:S(2)}) %collective-permute-start.11) | collective-permute-done | bytes 131104 | tf_op jit(solution)/shard_map/ppermute | solution.py:248
  104.2 0.7 shard_map.84
  (7 shorter events, 0.1 us)
Async XLA Ops:
  2.4 18.9 %collective-permute-start = (f32[64,512]{1,0:T(8,128)S(1)}, f32[64,512]{1,0:T(8,128)S(1)}, u32[]{:S(2)}, u32[]{:S(2)}) collective-permute-start(f32[64,512]{1,0:T(8,128)S(1)} %get-tuple-element.26.refs_0_), channel_id=1, source_target_pairs={{0,2},{2,0},{1,3},{3,1},{4,6},{6,4},{5,7},{7,5},{8,10},{10,8},{9,1... | collective-permute-start | bytes 393224 | tf_op jit(solution)/shard_map/ppermute | solution.py:248
  6.4 38.2 %all-to-all-start = ((f32[32,8,512]{2,1,0:T(8,128)}), f32[32,8,512]{2,1,0:T(8,128)S(1)}, u32[]{:S(2)}, u32[]{:S(2)}) async-start(f32[32,8,512]{2,1,0:T(8,128)} %get-tuple-element.27), calls=%async_computation | async-start | bytes 1048576 | tf_op jit(solution)/shard_map/all_to_all | solution.py:256
  21.3 11.2 %collective-permute-start.1 = (f32[128,512]{1,0:T(8,128)S(1)}, f32[128,512]{1,0:T(8,128)S(1)}, u32[]{:S(2)}, u32[]{:S(2)}) collective-permute-start(f32[128,512]{1,0:T(8,128)S(1)} %shard_map.76.refs_0_), channel_id=1, source_target_pairs={{0,32},{16,48},{32,0},{48,16},{1,33},{17,49},{33,1},{49,17},{2,34}... | collective-permute-start | bytes 786440 | tf_op jit(solution)/shard_map/ppermute | solution.py:252
  25.9 11.9 %collective-permute-start.3 = (f32[128,512]{1,0:T(8,128)S(1)}, f32[128,512]{1,0:T(8,128)S(1)}, u32[]{:S(2)}, u32[]{:S(2)}) collective-permute-start(f32[128,512]{1,0:T(8,128)S(1)} %shard_map.76.refs_0_), channel_id=1, source_target_pairs={{0,16},{16,32},{32,48},{48,0},{1,17},{17,33},{33,49},{49,1},{2,18}... | collective-permute-start | bytes 786440 | tf_op jit(solution)/shard_map/ppermute | solution.py:252
  28.2 13.0 %collective-permute-start.2 = (f32[128,512]{1,0:T(8,128)S(1)}, f32[128,512]{1,0:T(8,128)S(1)}, u32[]{:S(2)}, u32[]{:S(2)}) collective-permute-start(f32[128,512]{1,0:T(8,128)S(1)} %shard_map.76.refs_0_), channel_id=1, source_target_pairs={{0,48},{16,0},{32,16},{48,32},{1,49},{17,1},{33,17},{49,33},{2,50}... | collective-permute-start | bytes 786440 | tf_op jit(solution)/shard_map/ppermute | solution.py:252
  32.5 12.1 %collective-permute-start.4 = (f32[256,512]{1,0:T(8,128)S(1)}, f32[256,512]{1,0:T(8,128)S(1)}, u32[]{:S(2)}, u32[]{:S(2)}) collective-permute-start(f32[256,512]{1,0:T(8,128)S(1)} %shard_map.77.refs_0_), channel_id=1, source_target_pairs={{0,1},{1,0},{2,3},{3,2},{4,5},{5,4},{6,7},{7,6},{8,9},{9,8},{10,11... | collective-permute-start | bytes 1572872 | tf_op jit(solution)/shard_map/ppermute | solution.py:248
  37.8 5.3 %collective-permute-start.6 = (f32[128,512]{1,0:T(8,128)S(1)}, f32[128,512]{1,0:T(8,128)S(1)}, u32[]{:S(2)}, u32[]{:S(2)}) collective-permute-start(f32[128,512]{1,0:T(8,128)S(1)} %collective-permute-done.3.refs_2_), channel_id=1, source_target_pairs={{0,1},{1,0},{2,3},{3,2},{4,5},{5,4},{6,7},{7,6},{8,9},{9,8},{10,11... | collective-permute-start | bytes 786440 | tf_op jit(solution)/shard_map/ppermute | solution.py:248
  41.2 3.4 %collective-permute-start.5 = (f32[128,512]{1,0:T(8,128)S(1)}, f32[128,512]{1,0:T(8,128)S(1)}, u32[]{:S(2)}, u32[]{:S(2)}) collective-permute-start(f32[128,512]{1,0:T(8,128)S(1)} %collective-permute-done.2.refs_1_), channel_id=1, source_target_pairs={{0,1},{1,0},{2,3},{3,2},{4,5},{5,4},{6,7},{7,6},{8,9},{9,8},{10,11... | collective-permute-start | bytes 786440 | tf_op jit(solution)/shard_map/ppermute | solution.py:248
  70.2 6.2 %collective-permute-start.7 = (f32[512,512]{1,0:T(8,128)S(1)}, f32[512,512]{1,0:T(8,128)S(1)}, u32[]{:S(2)}, u32[]{:S(2)}) collective-permute-start(f32[512,512]{1,0:T(8,128)S(1)} %get-tuple-element.35), channel_id=1, source_target_pairs={{0,1},{1,0},{2,3},{3,2},{4,5},{5,4},{6,7},{7,6},{8,9},{9,8},{10,11... | collective-permute-start | bytes 3145736 | tf_op jit(solution)/shard_map/ppermute | solution.py:248
  76.5 27.7 %all-to-all-start.2 = ((f32[32,8,512]{2,1,0:T(8,128)}), f32[32,8,512]{2,1,0:T(8,128)S(1)}, u32[]{:S(2)}, u32[]{:S(2)}) async-start(f32[32,8,512]{2,1,0:T(8,128)} %bitcast.1), calls=%async_computation.2 | async-start | bytes 1048576 | tf_op jit(solution)/shard_map/all_to_all | solution.py:256
  80.4 11.2 %collective-permute-start.8 = (f32[128,512]{1,0:T(8,128)S(1)}, f32[128,512]{1,0:T(8,128)S(1)}, u32[]{:S(2)}, u32[]{:S(2)}) collective-permute-start(f32[128,512]{1,0:T(8,128)S(1)} %get-tuple-element.38), channel_id=1, source_target_pairs={{0,32},{16,48},{32,0},{48,16},{1,33},{17,49},{33,1},{49,17},{2,34}... | collective-permute-start | bytes 786440 | tf_op jit(solution)/shard_map/ppermute | solution.py:252
  84.8 12.9 %collective-permute-start.9 = (f32[128,512]{1,0:T(8,128)S(1)}, f32[128,512]{1,0:T(8,128)S(1)}, u32[]{:S(2)}, u32[]{:S(2)}) collective-permute-start(f32[128,512]{1,0:T(8,128)S(1)} %get-tuple-element.39), channel_id=1, source_target_pairs={{0,16},{16,32},{32,48},{48,0},{1,17},{17,33},{33,49},{49,1},{2,18}... | collective-permute-start | bytes 786440 | tf_op jit(solution)/shard_map/ppermute | solution.py:252
  86.7 11.0 %collective-permute-start.10 = (f32[128,512]{1,0:T(8,128)S(1)}, f32[128,512]{1,0:T(8,128)S(1)}, u32[]{:S(2)}, u32[]{:S(2)}) collective-permute-start(f32[128,512]{1,0:T(8,128)S(1)} %get-tuple-element.40), channel_id=1, source_target_pairs={{0,48},{16,0},{32,16},{48,32},{1,49},{17,1},{33,17},{49,33},{2,50}... | collective-permute-start | bytes 786440 | tf_op jit(solution)/shard_map/ppermute | solution.py:252
  97.7 6.5 %collective-permute-start.11 = (f32[64,512]{1,0:T(8,128)S(1)}, f32[64,512]{1,0:T(8,128)S(1)}, u32[]{:S(2)}, u32[]{:S(2)}) collective-permute-start(f32[64,512]{1,0:T(8,128)S(1)} %get-tuple-element.42), channel_id=1, source_target_pairs={{0,2},{2,0},{1,3},{3,1},{4,6},{6,4},{5,7},{7,5},{8,10},{10,8},{9,1... | collective-permute-start | bytes 393224 | tf_op jit(solution)/shard_map/ppermute | solution.py:248

commit v6 on v5

--- a/solution.py
+++ b/solution.py
@@ -110,11 +110,9 @@
         query.append((beside(hi, mid), beside(low, hi)))
     across = ((1,), (1,))
     tops = [None, None]
-    at = 0
-    for some in (in_refs[0:1], in_refs[1:3], in_refs[3:4], in_refs[4:6]):
-        both = jnp.concatenate([ref[...] for ref in some], axis=0)
-        there = pl.ds(at, both.shape[0])
-        at += both.shape[0]
+    for at, ref in enumerate(in_refs):
+        both = ref[...]
+        there = pl.ds(at * both.shape[0], both.shape[0])
         for head, w_ref in enumerate((w1_ref, w2_ref)):
             hi, mid, low = parts(both[:, head * half : (head + 1) * half], 3)
             main, rest = query[head]
@@ -248,8 +246,13 @@
     return lax.ppermute(x, axis, [(0, 1), (1, 0)])
 
 
-def around(x, step):
-    return lax.ppermute(x, RING, [(n, (n + step) % AROUND) for n in range(AROUND)])
+def across(x):
+    return lax.ppermute(x, RING, [(n, (n + AROUND // 2) % AROUND) for n in range(AROUND)])
+
+
+def toward(x, step):
+    pairs = [(2 * n + c, 2 * ((n + (step, -step)[c]) % AROUND) + c) for n in range(AROUND) for c in range(2)]
+    return lax.ppermute(x, RING + (CORE,), pairs)
 
 
 def exchange(x, axes):
@@ -270,9 +273,10 @@
         scratch_shapes=[pltpu.VMEM((own_rows, 2 * wide), F32), pltpu.SemaphoreType.DMA((4,))],
     )(*(in_hbm(x) for x in (queries, grad_out, key_pair, values)))
     kv_pair = call(stack, shape(F32, NEAR * own_keys, 2 * wide), 10**10, block // 2)(kv, swap(kv, PAIR))
-    right, across, left = (around(kv_pair, -n) for n in range(1, AROUND))
-    first = call(stack, shape(F32, 2 * NEAR * own_keys, 2 * wide), 10**9, block)(kv_pair, across)
-    kv_own = [first, right, left]
+    far, right, left = across(kv_pair), toward(kv_pair, -1), toward(kv_pair, 1)
+    first = call(stack, shape(F32, 2 * NEAR * own_keys, 2 * wide), 10**9, block)(kv_pair, far)
+    second = call(stack, shape(F32, 2 * NEAR * own_keys, 2 * wide), 0, block)(right, left)
+    kv_own = [first, second]
     kv_other = [swap(x, CORE) for x in kv_own]
     qg_all = exchange(qg, QUERY_GROUP).reshape(columns, 2 * wide)
     big = shape(F32, 2 * rows, columns)
@@ -288,7 +292,7 @@
     )(w1, w2, dp, qg_all, tops, every)
     moved = swap(other, CORE)
     own, dq = call(
-        functools.partial(own_half, 6),
+        functools.partial(own_half, 4),
         (shape(F32, rows, 2 * wide), shape(F32, columns, 2 * wide)),
         3 * pairs * wide * 6,
         4 * pairs * 4,
@@ -305,12 +309,12 @@
         input_output_aliases={2: AROUND},
     )(own, moved, dq)
     dq_parts = exchange(dq.reshape(QUERIES_IN, own_rows, 2 * wide), QUERY_GROUP)
-    across, right, left = (around(x, step) for x, step in zip(away, (2, 1, 3)))
-    mine = call(add_two, shape(F32, NEAR * own_keys, 2 * wide), 10**9, block)(mine, across)
-    near, far = call(add_ring, (shape(F32, own_keys, 2 * wide),) * NEAR, 0, block)(mine, right, left)
+    far, right, left = across(away[0]), toward(away[1], 1), toward(away[2], -1)
+    mine = call(add_two, shape(F32, NEAR * own_keys, 2 * wide), 10**9, block)(mine, far)
+    near, beyond = call(add_ring, (shape(F32, own_keys, 2 * wide),) * NEAR, 0, block)(mine, right, left)
     grad_keys, grad_values, attended, grad_queries = call(
         finish, (shape(F32, own_keys, wide),) * 2 + (shape(F32, own_rows, wide),) * 2, 0, block
-    )(near, swap(far, PAIR), dq_parts)
+    )(near, swap(beyond, PAIR), dq_parts)
     return attended, grad_queries, grad_keys, grad_values
 
 

time: 106 us -> 104 us (0.981)
  starting transfers between devices: 61.4 us -> 55.9 us
  waiting for transfers between devices: 11.9 us -> 15.6 us
    ppermute x6, waiting for transfers between devices: 7.05 us -> 10.5 us  [the longest x4 8.59 us: toward(): return lax.ppermute(x, RING + (CORE,), pairs)]
    ppermute x6, starting transfers between devices: 22 us -> 19.2 us  [the longest x4 10.6 us: toward(): return lax.ppermute(x, RING + (CORE,), pairs)]
    ppermute x6 -> x5, starting transfers between devices: 20.7 us -> 18 us  [swap(): return lax.ppermute(x, axis, [(0, 1), (1, 0)])]
    ppermute x6 -> x5, waiting for transfers between devices: 4.81 us -> 5.06 us  [swap(): return lax.ppermute(x, axis, [(0, 1), (1, 0)])]
    pallas_call x1 -> x2, Pallas kernels: 2.58 us -> 2.61 us  [the longest x1 2.58 us: per_device(): call(functools.partial(own_half, 4), (shape(F32, rows, 2 * wide), shape(F...]
  transfers between devices with their start and end apart: 14 -> 13, of which waited for: 5 -> 7; matrix products, arithmetic and copies ran while one was open for 0% -> 0% of each run, Pallas kernels for 3% -> 3%
where the time goes in v6:
time: 104 us; the launch traced here: 103 us
  starting transfers between devices  55.9 us (54%)
  blocking collectives  23.1 us (22%)
  waiting for transfers between devices  15.6 us (15%)
  Pallas kernels  8.03 us (8%)
    all_to_all x1, blocking collectives, exchange(): return lax.all_to_all(x, axes, 0, 0, tiled=True)  23.1 us
    all_to_all x2, starting transfers between devices, exchange(): return lax.all_to_all(x, axes, 0, 0, tiled=True)  18.7 us
    ppermute x5, starting transfers between devices, swap(): return lax.ppermute(x, axis, [(0, 1), (1, 0)])  18 us
    ppermute x4, starting transfers between devices, toward(): return lax.ppermute(x, RING + (CORE,), pairs)  10.6 us
    ppermute x2, starting transfers between devices, across(): lax.ppermute(x, RING, [(n, (n + AROUND // 2) % AROUND) for n in range(ARO...  8.66 us
    ppermute x4, waiting for transfers between devices, toward(): return lax.ppermute(x, RING + (CORE,), pairs)  8.59 us
    ppermute x5, waiting for transfers between devices, swap(): return lax.ppermute(x, axis, [(0, 1), (1, 0)])  5.06 us
    pallas_call x1, Pallas kernels, per_device(): call(functools.partial(own_half, 4), (shape(F32, rows, 2 * wide), shape(F...  2.58 us
  transfers between devices with their start and end apart: 13, of which 7 were waited for; matrix products, arithmetic and copies ran while one was open for 0% of the time, Pallas kernels for 3%

profile of v6, /device:TPU:1, one launch (start us, length us, event | category | flops | bytes accessed | tf_op | source)
XLA Modules:
  0.0 103.5 jit_solution(603502384303230250)
XLA Ops:
  0.6 1.7 %shard_map.75 = (f32[64,512]{1,0:T(8,128)S(1)}, f32[32,8,512]{2,1,0:T(8,128)}) custom-call(f32[8,256]{1,0:T(8,128)} %queries_ref.1, f32[8,256]{1,0:T(8,128)} %grad_ref.1, f32[64,256]{1,0:T(8,128)} %key_ref.1, f32[64,256]{1,0:T(8,128)} %value_ref.1), custom_call_target="tpu_custom_call" | custom-call | bytes 524288 | tf_op jit(solution)/shard_map/pallas_call | solution.py:267
  2.4 4.0 %collective-permute-start = (f32[64,512]{1,0:T(8,128)S(1)}, f32[64,512]{1,0:T(8,128)S(1)}, u32[]{:S(2)}, u32[]{:S(2)}) collective-permute-start(f32[64,512]{1,0:T(8,128)S(1)} %get-tuple-element.26.refs_0_), channel_id=1, source_target_pairs={{0,2},{2,0},{1,3},{3,1},{4,6},{6,4},{5,7},{7,5},{8,10},{10,8},{9,1... | collective-permute-start | bytes 393224 | tf_op jit(solution)/shard_map/ppermute | solution.py:246
  6.4 14.8 %all-to-all-start = ((f32[32,8,512]{2,1,0:T(8,128)}), f32[32,8,512]{2,1,0:T(8,128)S(1)}, u32[]{:S(2)}, u32[]{:S(2)}) async-start(f32[32,8,512]{2,1,0:T(8,128)} %get-tuple-element.27), calls=%async_computation | async-start | bytes 1048576 | tf_op jit(solution)/shard_map/all_to_all | solution.py:259
  21.2 0.0 collective-permute-done.refs_1_
  21.3 4.7 %collective-permute-start.1 = (f32[128,512]{1,0:T(8,128)S(1)}, f32[128,512]{1,0:T(8,128)S(1)}, u32[]{:S(2)}, u32[]{:S(2)}) collective-permute-start(f32[128,512]{1,0:T(8,128)S(1)} %shard_map.76.refs_0_), channel_id=1, source_target_pairs={{0,32},{16,48},{32,0},{48,16},{1,33},{17,49},{33,1},{49,17},{2,34}... | collective-permute-start | bytes 786440 | tf_op jit(solution)/shard_map/ppermute | solution.py:250
  25.9 2.8 %collective-permute-start.3 = (f32[128,512]{1,0:T(8,128)S(1)}, f32[128,512]{1,0:T(8,128)S(1)}, u32[]{:S(2)}, u32[]{:S(2)}) collective-permute-start(f32[128,512]{1,0:T(8,128)S(1)} %shard_map.76.refs_0_), channel_id=1, source_target_pairs={{0,16},{1,49},{16,32},{17,1},{32,48},{33,17},{48,0},{49,33},{2,18}... | collective-permute-start | bytes 786440 | tf_op jit(solution)/shard_map/ppermute | solution.py:255
  28.7 2.5 %collective-permute-start.2 = (f32[128,512]{1,0:T(8,128)S(1)}, f32[128,512]{1,0:T(8,128)S(1)}, u32[]{:S(2)}, u32[]{:S(2)}) collective-permute-start(f32[128,512]{1,0:T(8,128)S(1)} %shard_map.76.refs_0_), channel_id=1, source_target_pairs={{0,48},{1,17},{16,0},{17,33},{32,16},{33,49},{48,32},{49,1},{2,50}... | collective-permute-start | bytes 786440 | tf_op jit(solution)/shard_map/ppermute | solution.py:255
  31.2 0.0 collective-permute-done.1.refs_1_
  31.3 5.2 %collective-permute-start.4 = (f32[256,512]{1,0:T(8,128)S(1)}, f32[256,512]{1,0:T(8,128)S(1)}, u32[]{:S(2)}, u32[]{:S(2)}) collective-permute-start(f32[256,512]{1,0:T(8,128)S(1)} %shard_map.77.refs_0_), channel_id=1, source_target_pairs={{0,1},{1,0},{2,3},{3,2},{4,5},{5,4},{6,7},{7,6},{8,9},{9,8},{10,11... | collective-permute-start | bytes 1572872 | tf_op jit(solution)/shard_map/ppermute | solution.py:246
  36.5 0.2 collective-permute-done.3.refs_1_
  36.7 2.3 %collective-permute-done.2.refs_0_ = f32[128,512]{1,0:T(8,128)S(1)} collective-permute-done((f32[128,512]{1,0:T(8,128)S(1)}, f32[128,512]{1,0:T(8,128)S(1)}, u32[]{:S(2)}, u32[]{:S(2)}) %collective-permute-start.2) | collective-permute-done | bytes 262176 | tf_op jit(solution)/shard_map/ppermute | solution.py:255
  39.1 2.0 %collective-permute-start.5 = (f32[256,512]{1,0:T(8,128)S(1)}, f32[256,512]{1,0:T(8,128)S(1)}, u32[]{:S(2)}, u32[]{:S(2)}) collective-permute-start(f32[256,512]{1,0:T(8,128)S(1)} %shard_map.78.refs_1_), channel_id=1, source_target_pairs={{0,1},{1,0},{2,3},{3,2},{4,5},{5,4},{6,7},{7,6},{8,9},{9,8},{10,11... | collective-permute-start | bytes 1572872 | tf_op jit(solution)/shard_map/ppermute | solution.py:246
  41.0 0.0 collective-permute-done.4.refs_2_
  41.1 1.8 %collective-permute-done.5.refs_3_ = f32[256,512]{1,0:T(8,128)S(1)} collective-permute-done((f32[256,512]{1,0:T(8,128)S(1)}, f32[256,512]{1,0:T(8,128)S(1)}, u32[]{:S(2)}, u32[]{:S(2)}) %collective-permute-start.5) | collective-permute-done | bytes 524320 | tf_op jit(solution)/shard_map/ppermute | solution.py:246
  42.9 1.9 %shard_map.79 = (f32[1024,256]{1,0:T(8,128)S(1)}, f32[1024,256]{1,0:T(8,128)S(1)}, f32[1024,256]{1,0:T(8,128)S(1)}, f32[32,8,128]{2,1,0:T(8,128)S(1)}, f32[2,256]{1,0:T(2,128)S(1)}) custom-call(f32[256,512]{1,0:T(8,128)S(1)} %shard_map.77.refs_0_, f32[256,512]{1,0:T(8,128)S(1)} %shard_map.78.refs_1_, f32[256,512]{1,0:T(8,128)S(1)} %collective-permute-done.4.refs_2_, ...), custom_call_target="tpu_custom_call" | custom-call | flops 1207959552 | bytes 3145728 | tf_op jit(solution)/shard_map/pallas_call | solution.py:285
  44.8 23.1 %all_to_all.15.every_ref.refs_9_ = f32[32,8,128]{2,1,0:T(8,128)S(1)} all-to-all(f32[32,8,128]{2,1,0:T(8,128)S(1)} %get-tuple-element.32), channel_id=1, replica_groups=mesh['z2'=2,'z1'=2,'z0'=2,'xh'=2,'xl'=2,'y2'=2,'y1'=2,'y0'=2,'c'=2] {'z2..., dimensions={0} | all-to-all | bytes 262144 | tf_op jit(solution)/shard_map/all_to_all | solution.py:259
  67.9 0.8 shard_map.80
  68.7 3.7 %collective-permute-start.6 = (f32[512,512]{1,0:T(8,128)S(1)}, f32[512,512]{1,0:T(8,128)S(1)}, u32[]{:S(2)}, u32[]{:S(2)}) collective-permute-start(f32[512,512]{1,0:T(8,128)S(1)} %get-tuple-element.35), channel_id=1, source_target_pairs={{0,1},{1,0},{2,3},{3,2},{4,5},{5,4},{6,7},{7,6},{8,9},{9,8},{10,11... | collective-permute-start | bytes 3145736 | tf_op jit(solution)/shard_map/ppermute | solution.py:246
  72.4 2.6 %shard_map.81 = (f32[512,512]{1,0:T(8,128)S(1)}, f32[256,512]{1,0:T(8,128)}) custom-call(f32[256,512]{1,0:T(8,128)S(1)} %shard_map.77.refs_0_, f32[256,512]{1,0:T(8,128)S(1)} %shard_map.78.refs_1_, f32[256,512]{1,0:T(8,128)S(1)} %collective-permute-done.4.refs_2_, f32[256,512]{1,0:T(8,128)S(1)} %collective-permute-done.5.refs_3_, ...), custom_call_target="tpu_custom_call" | custom-call | flops 1207959552 | bytes 4194304 | tf_op jit(solution)/shard_map/pallas_call | solution.py:294
  75.0 0.0 collective-permute-done.6.moved_ref
  75.0 0.1 shard_map.82
  75.1 3.9 %all-to-all-start.2 = ((f32[32,8,512]{2,1,0:T(8,128)}), f32[32,8,512]{2,1,0:T(8,128)S(1)}, u32[]{:S(2)}, u32[]{:S(2)}) async-start(f32[32,8,512]{2,1,0:T(8,128)} %bitcast.1), calls=%async_computation.2 | async-start | bytes 1048576 | tf_op jit(solution)/shard_map/all_to_all | solution.py:259
  79.0 4.0 %collective-permute-start.7 = (f32[128,512]{1,0:T(8,128)S(1)}, f32[128,512]{1,0:T(8,128)S(1)}, u32[]{:S(2)}, u32[]{:S(2)}) collective-permute-start(f32[128,512]{1,0:T(8,128)S(1)} %get-tuple-element.38), channel_id=1, source_target_pairs={{0,32},{16,48},{32,0},{48,16},{1,33},{17,49},{33,1},{49,17},{2,34}... | collective-permute-start | bytes 786440 | tf_op jit(solution)/shard_map/ppermute | solution.py:250
  83.0 2.9 %collective-permute-start.8 = (f32[128,512]{1,0:T(8,128)S(1)}, f32[128,512]{1,0:T(8,128)S(1)}, u32[]{:S(2)}, u32[]{:S(2)}) collective-permute-start(f32[128,512]{1,0:T(8,128)S(1)} %get-tuple-element.39), channel_id=1, source_target_pairs={{0,16},{1,49},{16,32},{17,1},{32,48},{33,17},{48,0},{49,33},{2,18}... | collective-permute-start | bytes 786440 | tf_op jit(solution)/shard_map/ppermute | solution.py:255
  86.0 2.3 %collective-permute-start.9 = (f32[128,512]{1,0:T(8,128)S(1)}, f32[128,512]{1,0:T(8,128)S(1)}, u32[]{:S(2)}, u32[]{:S(2)}) collective-permute-start(f32[128,512]{1,0:T(8,128)S(1)} %get-tuple-element.40), channel_id=1, source_target_pairs={{0,48},{1,17},{16,0},{17,33},{32,16},{33,49},{48,32},{49,1},{2,50}... | collective-permute-start | bytes 786440 | tf_op jit(solution)/shard_map/ppermute | solution.py:255
  88.3 2.0 %collective-permute-done.7.right_ref = f32[128,512]{1,0:T(8,128)S(1)} collective-permute-done((f32[128,512]{1,0:T(8,128)S(1)}, f32[128,512]{1,0:T(8,128)S(1)}, u32[]{:S(2)}, u32[]{:S(2)}) %collective-permute-start.7) | collective-permute-done | bytes 262176 | tf_op jit(solution)/shard_map/ppermute | solution.py:250
  90.3 5.4 %collective-permute-done.8.refs_1_ = f32[128,512]{1,0:T(8,128)S(1)} collective-permute-done((f32[128,512]{1,0:T(8,128)S(1)}, f32[128,512]{1,0:T(8,128)S(1)}, u32[]{:S(2)}, u32[]{:S(2)}) %collective-permute-start.8) | collective-permute-done | bytes 262176 | tf_op jit(solution)/shard_map/ppermute | solution.py:255
  95.7 0.6 collective-permute-done.9.refs_2_
  96.4 3.1 %collective-permute-start.10 = (f32[64,512]{1,0:T(8,128)S(1)}, f32[64,512]{1,0:T(8,128)S(1)}, u32[]{:S(2)}, u32[]{:S(2)}) collective-permute-start(f32[64,512]{1,0:T(8,128)S(1)} %get-tuple-element.42), channel_id=1, source_target_pairs={{0,2},{2,0},{1,3},{3,1},{4,6},{6,4},{5,7},{7,5},{8,10},{10,8},{9,1... | collective-permute-start | bytes 393224 | tf_op jit(solution)/shard_map/ppermute | solution.py:246
  99.5 3.2 %collective-permute-done.10.came_ref = f32[64,512]{1,0:T(8,128)S(1)} collective-permute-done((f32[64,512]{1,0:T(8,128)S(1)}, f32[64,512]{1,0:T(8,128)S(1)}, u32[]{:S(2)}, u32[]{:S(2)}) %collective-permute-start.10) | collective-permute-done | bytes 131104 | tf_op jit(solution)/shard_map/ppermute | solution.py:246
  102.8 0.0 all-to-all-done.2.parts_ref
  102.8 0.7 shard_map.85
  (6 shorter events, 0.2 us)
Async XLA Ops:
  2.4 18.9 %collective-permute-start = (f32[64,512]{1,0:T(8,128)S(1)}, f32[64,512]{1,0:T(8,128)S(1)}, u32[]{:S(2)}, u32[]{:S(2)}) collective-permute-start(f32[64,512]{1,0:T(8,128)S(1)} %get-tuple-element.26.refs_0_), channel_id=1, source_target_pairs={{0,2},{2,0},{1,3},{3,1},{4,6},{6,4},{5,7},{7,5},{8,10},{10,8},{9,1... | collective-permute-start | bytes 393224 | tf_op jit(solution)/shard_map/ppermute | solution.py:246
  6.4 36.5 %all-to-all-start = ((f32[32,8,512]{2,1,0:T(8,128)}), f32[32,8,512]{2,1,0:T(8,128)S(1)}, u32[]{:S(2)}, u32[]{:S(2)}) async-start(f32[32,8,512]{2,1,0:T(8,128)} %get-tuple-element.27), calls=%async_computation | async-start | bytes 1048576 | tf_op jit(solution)/shard_map/all_to_all | solution.py:259
  21.3 10.0 %collective-permute-start.1 = (f32[128,512]{1,0:T(8,128)S(1)}, f32[128,512]{1,0:T(8,128)S(1)}, u32[]{:S(2)}, u32[]{:S(2)}) collective-permute-start(f32[128,512]{1,0:T(8,128)S(1)} %shard_map.76.refs_0_), channel_id=1, source_target_pairs={{0,32},{16,48},{32,0},{48,16},{1,33},{17,49},{33,1},{49,17},{2,34}... | collective-permute-start | bytes 786440 | tf_op jit(solution)/shard_map/ppermute | solution.py:250
  25.9 10.8 %collective-permute-start.3 = (f32[128,512]{1,0:T(8,128)S(1)}, f32[128,512]{1,0:T(8,128)S(1)}, u32[]{:S(2)}, u32[]{:S(2)}) collective-permute-start(f32[128,512]{1,0:T(8,128)S(1)} %shard_map.76.refs_0_), channel_id=1, source_target_pairs={{0,16},{1,49},{16,32},{17,1},{32,48},{33,17},{48,0},{49,33},{2,18}... | collective-permute-start | bytes 786440 | tf_op jit(solution)/shard_map/ppermute | solution.py:255
  28.7 10.3 %collective-permute-start.2 = (f32[128,512]{1,0:T(8,128)S(1)}, f32[128,512]{1,0:T(8,128)S(1)}, u32[]{:S(2)}, u32[]{:S(2)}) collective-permute-start(f32[128,512]{1,0:T(8,128)S(1)} %shard_map.76.refs_0_), channel_id=1, source_target_pairs={{0,48},{1,17},{16,0},{17,33},{32,16},{33,49},{48,32},{49,1},{2,50}... | collective-permute-start | bytes 786440 | tf_op jit(solution)/shard_map/ppermute | solution.py:255
  31.3 9.8 %collective-permute-start.4 = (f32[256,512]{1,0:T(8,128)S(1)}, f32[256,512]{1,0:T(8,128)S(1)}, u32[]{:S(2)}, u32[]{:S(2)}) collective-permute-start(f32[256,512]{1,0:T(8,128)S(1)} %shard_map.77.refs_0_), channel_id=1, source_target_pairs={{0,1},{1,0},{2,3},{3,2},{4,5},{5,4},{6,7},{7,6},{8,9},{9,8},{10,11... | collective-permute-start | bytes 1572872 | tf_op jit(solution)/shard_map/ppermute | solution.py:246
  39.1 3.8 %collective-permute-start.5 = (f32[256,512]{1,0:T(8,128)S(1)}, f32[256,512]{1,0:T(8,128)S(1)}, u32[]{:S(2)}, u32[]{:S(2)}) collective-permute-start(f32[256,512]{1,0:T(8,128)S(1)} %shard_map.78.refs_1_), channel_id=1, source_target_pairs={{0,1},{1,0},{2,3},{3,2},{4,5},{5,4},{6,7},{7,6},{8,9},{9,8},{10,11... | collective-permute-start | bytes 1572872 | tf_op jit(solution)/shard_map/ppermute | solution.py:246
  68.7 6.3 %collective-permute-start.6 = (f32[512,512]{1,0:T(8,128)S(1)}, f32[512,512]{1,0:T(8,128)S(1)}, u32[]{:S(2)}, u32[]{:S(2)}) collective-permute-start(f32[512,512]{1,0:T(8,128)S(1)} %get-tuple-element.35), channel_id=1, source_target_pairs={{0,1},{1,0},{2,3},{3,2},{4,5},{5,4},{6,7},{7,6},{8,9},{9,8},{10,11... | collective-permute-start | bytes 3145736 | tf_op jit(solution)/shard_map/ppermute | solution.py:246
  75.1 27.7 %all-to-all-start.2 = ((f32[32,8,512]{2,1,0:T(8,128)}), f32[32,8,512]{2,1,0:T(8,128)S(1)}, u32[]{:S(2)}, u32[]{:S(2)}) async-start(f32[32,8,512]{2,1,0:T(8,128)} %bitcast.1), calls=%async_computation.2 | async-start | bytes 1048576 | tf_op jit(solution)/shard_map/all_to_all | solution.py:259
  79.0 11.3 %collective-permute-start.7 = (f32[128,512]{1,0:T(8,128)S(1)}, f32[128,512]{1,0:T(8,128)S(1)}, u32[]{:S(2)}, u32[]{:S(2)}) collective-permute-start(f32[128,512]{1,0:T(8,128)S(1)} %get-tuple-element.38), channel_id=1, source_target_pairs={{0,32},{16,48},{32,0},{48,16},{1,33},{17,49},{33,1},{49,17},{2,34}... | collective-permute-start | bytes 786440 | tf_op jit(solution)/shard_map/ppermute | solution.py:250
  83.0 12.7 %collective-permute-start.8 = (f32[128,512]{1,0:T(8,128)S(1)}, f32[128,512]{1,0:T(8,128)S(1)}, u32[]{:S(2)}, u32[]{:S(2)}) collective-permute-start(f32[128,512]{1,0:T(8,128)S(1)} %get-tuple-element.39), channel_id=1, source_target_pairs={{0,16},{1,49},{16,32},{17,1},{32,48},{33,17},{48,0},{49,33},{2,18}... | collective-permute-start | bytes 786440 | tf_op jit(solution)/shard_map/ppermute | solution.py:255
  86.0 10.4 %collective-permute-start.9 = (f32[128,512]{1,0:T(8,128)S(1)}, f32[128,512]{1,0:T(8,128)S(1)}, u32[]{:S(2)}, u32[]{:S(2)}) collective-permute-start(f32[128,512]{1,0:T(8,128)S(1)} %get-tuple-element.40), channel_id=1, source_target_pairs={{0,48},{1,17},{16,0},{17,33},{32,16},{33,49},{48,32},{49,1},{2,50}... | collective-permute-start | bytes 786440 | tf_op jit(solution)/shard_map/ppermute | solution.py:255
  96.4 6.4 %collective-permute-start.10 = (f32[64,512]{1,0:T(8,128)S(1)}, f32[64,512]{1,0:T(8,128)S(1)}, u32[]{:S(2)}, u32[]{:S(2)}) collective-permute-start(f32[64,512]{1,0:T(8,128)S(1)} %get-tuple-element.42), channel_id=1, source_target_pairs={{0,2},{2,0},{1,3},{3,1},{4,6},{6,4},{5,7},{7,5},{8,10},{10,8},{9,1... | collective-permute-start | bytes 393224 | tf_op jit(solution)/shard_map/ppermute | solution.py:246

commit v7 on v6

--- a/solution.py
+++ b/solution.py
@@ -200,9 +200,10 @@
 
 def add_moved(own_ref, moved_ref, _, *refs):
     *out_refs, _ = refs
-    rows = out_refs[0].shape[0]
-    for n, out_ref in enumerate(out_refs):
-        here = pl.ds(n * rows, rows)
+    first = 0
+    for out_ref in out_refs:
+        here = pl.ds(first, out_ref.shape[0])
+        first += out_ref.shape[0]
         out_ref[...] = own_ref[here, :] + moved_ref[here, :]
 
 
@@ -228,9 +229,12 @@
     far_ref[...] = total[rows:]
 
 
-def finish(near_ref, came_ref, parts_ref, keys_ref, values_ref, attended_ref, queries_ref):
+def finish(*refs):
+    *in_refs, parts_ref, keys_ref, values_ref, attended_ref, queries_ref = refs
     wide = keys_ref.shape[1]
-    total = near_ref[...] + came_ref[...]
+    total = in_refs[0][...]
+    for ref in in_refs[1:]:
+        total = total + ref[...]
     keys_ref[...] = total[:, :wide]
     values_ref[...] = total[:, wide:]
     total = jnp.sum(parts_ref[...], axis=0)
@@ -253,6 +257,13 @@
 def toward(x, step):
     pairs = [(2 * n + c, 2 * ((n + (step, -step)[c]) % AROUND) + c) for n in range(AROUND) for c in range(2)]
     return lax.ppermute(x, RING + (CORE,), pairs)
+
+
+def past(x, step):
+    places = [(n, y, c) for n in range(AROUND) for y in range(NEAR) for c in range(2)]
+    at = {place: n for n, place in enumerate(places)}
+    pairs = [(at[n, y, c], at[(n + (step, -step)[c]) % AROUND, y ^ 1, c]) for n, y, c in places]
+    return lax.ppermute(x, RING + (PAIR, CORE), pairs)
 
 
 def exchange(x, axes):
@@ -299,22 +310,23 @@
         scratch_shapes=[pltpu.VMEM((6, rows, columns), BF16), pltpu.VMEM((2, 2 * wide, 2 * rows), BF16)],
     )(*kv_own, *kv_other, w1, w2, dp, qg_all, tops, every, other_slopes)
     vmem, anywhere = pl.BlockSpec(memory_space=pltpu.VMEM), pl.BlockSpec(memory_space=pl.ANY)
-    mine, *away, dq = call(
+    pair_sum, block_sum = shape(F32, NEAR * own_keys, 2 * wide), shape(F32, own_keys, 2 * wide)
+    mine, far, right, left, left_past, dq = call(
         add_moved,
-        (shape(F32, NEAR * own_keys, 2 * wide),) * AROUND + (shape(F32, columns, 2 * wide),),
+        (pair_sum,) * 3 + (block_sum,) * 2 + (shape(F32, columns, 2 * wide),),
         0,
         block,
         in_specs=[vmem, vmem, anywhere],
-        out_specs=[vmem] * AROUND + [anywhere],
-        input_output_aliases={2: AROUND},
+        out_specs=[vmem] * 5 + [anywhere],
+        input_output_aliases={2: 5},
     )(own, moved, dq)
     dq_parts = exchange(dq.reshape(QUERIES_IN, own_rows, 2 * wide), QUERY_GROUP)
-    far, right, left = across(away[0]), toward(away[1], 1), toward(away[2], -1)
-    mine = call(add_two, shape(F32, NEAR * own_keys, 2 * wide), 10**9, block)(mine, far)
-    near, beyond = call(add_ring, (shape(F32, own_keys, 2 * wide),) * NEAR, 0, block)(mine, right, left)
+    sides = (toward(left, -1), past(left_past, -1))
+    mine = call(add_two, pair_sum, 10**9, block)(mine, across(far))
+    near, beyond = call(add_ring, (block_sum,) * NEAR, 0, block)(mine, toward(right, 1))
     grad_keys, grad_values, attended, grad_queries = call(
         finish, (shape(F32, own_keys, wide),) * 2 + (shape(F32, own_rows, wide),) * 2, 0, block
-    )(near, swap(beyond, PAIR), dq_parts)
+    )(near, *sides, swap(beyond, PAIR), dq_parts)
     return attended, grad_queries, grad_keys, grad_values
 
 

time: 104 us -> 103 us (level)
  waiting for transfers between devices: 15.6 us -> 11.1 us
  starting transfers between devices: 55.9 us -> 59.6 us
    ppermute x0 -> x1, starting transfers between devices: none -> 3.77 us  [past(): return lax.ppermute(x, RING + (PAIR, CORE), pairs)]
    ppermute x4, waiting for transfers between devices: 8.59 us -> 5.53 us  [toward(): return lax.ppermute(x, RING + (CORE,), pairs)]
    ppermute x2, waiting for transfers between devices: 1.96 us -> 0.01 us  [across(): lax.ppermute(x, RING, [(n, (n + AROUND // 2) % AROUND) for n in range(ARO...]
  transfers between devices with their start and end apart: 13 -> 14, of which waited for: 7 -> 5; matrix products, arithmetic and copies ran while one was open for 0% -> 0% of each run, Pallas kernels for 3% -> 3%
where the time goes in v7:
time: 103 us
  starting transfers between devices  59.6 us (58%)
  blocking collectives  23.1 us (22%)
  waiting for transfers between devices  11.1 us (11%)
  Pallas kernels  8.05 us (8%)
    all_to_all x1, blocking collectives, exchange(): return lax.all_to_all(x, axes, 0, 0, tiled=True)  23.1 us
    all_to_all x2, starting transfers between devices, exchange(): return lax.all_to_all(x, axes, 0, 0, tiled=True)  18.7 us
    ppermute x5, starting transfers between devices, swap(): return lax.ppermute(x, axis, [(0, 1), (1, 0)])  17.9 us
    ppermute x4, starting transfers between devices, toward(): return lax.ppermute(x, RING + (CORE,), pairs)  10.6 us
    ppermute x2, starting transfers between devices, across(): lax.ppermute(x, RING, [(n, (n + AROUND // 2) % AROUND) for n in range(ARO...  8.66 us
    ppermute x4, waiting for transfers between devices, toward(): return lax.ppermute(x, RING + (CORE,), pairs)  5.53 us
    ppermute x5, waiting for transfers between devices, swap(): return lax.ppermute(x, axis, [(0, 1), (1, 0)])  5.53 us
    ppermute x1, starting transfers between devices, past(): return lax.ppermute(x, RING + (PAIR, CORE), pairs)  3.77 us
  transfers between devices with their start and end apart: 14, of which 5 were waited for; matrix products, arithmetic and copies ran while one was open for 0% of the time, Pallas kernels for 3%

profile of v7, /device:TPU:1, one launch (start us, length us, event | category | flops | bytes accessed | tf_op | source)
XLA Modules:
  0.0 102.6 jit_solution(11631340910385746006)
XLA Ops:
  0.6 1.7 %shard_map.75 = (f32[64,512]{1,0:T(8,128)S(1)}, f32[32,8,512]{2,1,0:T(8,128)}) custom-call(f32[8,256]{1,0:T(8,128)} %queries_ref.1, f32[8,256]{1,0:T(8,128)} %grad_ref.1, f32[64,256]{1,0:T(8,128)} %key_ref.1, f32[64,256]{1,0:T(8,128)} %value_ref.1), custom_call_target="tpu_custom_call" | custom-call | bytes 524288 | tf_op jit(solution)/shard_map/pallas_call | solution.py:278
  2.4 4.0 %collective-permute-start = (f32[64,512]{1,0:T(8,128)S(1)}, f32[64,512]{1,0:T(8,128)S(1)}, u32[]{:S(2)}, u32[]{:S(2)}) collective-permute-start(f32[64,512]{1,0:T(8,128)S(1)} %get-tuple-element.27.refs_0_), channel_id=1, source_target_pairs={{0,2},{2,0},{1,3},{3,1},{4,6},{6,4},{5,7},{7,5},{8,10},{10,8},{9,1... | collective-permute-start | bytes 393224 | tf_op jit(solution)/shard_map/ppermute | solution.py:250
  6.4 14.8 %all-to-all-start = ((f32[32,8,512]{2,1,0:T(8,128)}), f32[32,8,512]{2,1,0:T(8,128)S(1)}, u32[]{:S(2)}, u32[]{:S(2)}) async-start(f32[32,8,512]{2,1,0:T(8,128)} %get-tuple-element.28), calls=%async_computation | async-start | bytes 1048576 | tf_op jit(solution)/shard_map/all_to_all | solution.py:270
  21.2 0.0 collective-permute-done.refs_1_
  21.3 4.7 %collective-permute-start.1 = (f32[128,512]{1,0:T(8,128)S(1)}, f32[128,512]{1,0:T(8,128)S(1)}, u32[]{:S(2)}, u32[]{:S(2)}) collective-permute-start(f32[128,512]{1,0:T(8,128)S(1)} %shard_map.76.refs_0_), channel_id=1, source_target_pairs={{0,32},{16,48},{32,0},{48,16},{1,33},{17,49},{33,1},{49,17},{2,34}... | collective-permute-start | bytes 786440 | tf_op jit(solution)/shard_map/ppermute | solution.py:254
  25.9 2.8 %collective-permute-start.3 = (f32[128,512]{1,0:T(8,128)S(1)}, f32[128,512]{1,0:T(8,128)S(1)}, u32[]{:S(2)}, u32[]{:S(2)}) collective-permute-start(f32[128,512]{1,0:T(8,128)S(1)} %shard_map.76.refs_0_), channel_id=1, source_target_pairs={{0,16},{1,49},{16,32},{17,1},{32,48},{33,17},{48,0},{49,33},{2,18}... | collective-permute-start | bytes 786440 | tf_op jit(solution)/shard_map/ppermute | solution.py:259
  28.7 2.5 %collective-permute-start.2 = (f32[128,512]{1,0:T(8,128)S(1)}, f32[128,512]{1,0:T(8,128)S(1)}, u32[]{:S(2)}, u32[]{:S(2)}) collective-permute-start(f32[128,512]{1,0:T(8,128)S(1)} %shard_map.76.refs_0_), channel_id=1, source_target_pairs={{0,48},{1,17},{16,0},{17,33},{32,16},{33,49},{48,32},{49,1},{2,50}... | collective-permute-start | bytes 786440 | tf_op jit(solution)/shard_map/ppermute | solution.py:259
  31.2 0.0 collective-permute-done.1.refs_1_
  31.3 5.2 %collective-permute-start.4 = (f32[256,512]{1,0:T(8,128)S(1)}, f32[256,512]{1,0:T(8,128)S(1)}, u32[]{:S(2)}, u32[]{:S(2)}) collective-permute-start(f32[256,512]{1,0:T(8,128)S(1)} %shard_map.77.refs_0_), channel_id=1, source_target_pairs={{0,1},{1,0},{2,3},{3,2},{4,5},{5,4},{6,7},{7,6},{8,9},{9,8},{10,11... | collective-permute-start | bytes 1572872 | tf_op jit(solution)/shard_map/ppermute | solution.py:250
  36.5 0.2 collective-permute-done.3.refs_1_
  36.7 2.3 %collective-permute-done.2.refs_0_ = f32[128,512]{1,0:T(8,128)S(1)} collective-permute-done((f32[128,512]{1,0:T(8,128)S(1)}, f32[128,512]{1,0:T(8,128)S(1)}, u32[]{:S(2)}, u32[]{:S(2)}) %collective-permute-start.2) | collective-permute-done | bytes 262176 | tf_op jit(solution)/shard_map/ppermute | solution.py:259
  39.1 2.0 %collective-permute-start.5 = (f32[256,512]{1,0:T(8,128)S(1)}, f32[256,512]{1,0:T(8,128)S(1)}, u32[]{:S(2)}, u32[]{:S(2)}) collective-permute-start(f32[256,512]{1,0:T(8,128)S(1)} %shard_map.78.refs_1_), channel_id=1, source_target_pairs={{0,1},{1,0},{2,3},{3,2},{4,5},{5,4},{6,7},{7,6},{8,9},{9,8},{10,11... | collective-permute-start | bytes 1572872 | tf_op jit(solution)/shard_map/ppermute | solution.py:250
  41.0 0.0 collective-permute-done.4.refs_2_
  41.1 1.8 %collective-permute-done.5.refs_3_ = f32[256,512]{1,0:T(8,128)S(1)} collective-permute-done((f32[256,512]{1,0:T(8,128)S(1)}, f32[256,512]{1,0:T(8,128)S(1)}, u32[]{:S(2)}, u32[]{:S(2)}) %collective-permute-start.5) | collective-permute-done | bytes 524320 | tf_op jit(solution)/shard_map/ppermute | solution.py:250
  42.9 0.0 all-to-all-done
  42.9 1.9 %shard_map.79 = (f32[1024,256]{1,0:T(8,128)S(1)}, f32[1024,256]{1,0:T(8,128)S(1)}, f32[1024,256]{1,0:T(8,128)S(1)}, f32[32,8,128]{2,1,0:T(8,128)S(1)}, f32[2,256]{1,0:T(2,128)S(1)}) custom-call(f32[256,512]{1,0:T(8,128)S(1)} %shard_map.77.refs_0_, f32[256,512]{1,0:T(8,128)S(1)} %shard_map.78.refs_1_, f32[256,512]{1,0:T(8,128)S(1)} %collective-permute-done.4.refs_2_, ...), custom_call_target="tpu_custom_call" | custom-call | flops 1207959552 | bytes 3145728 | tf_op jit(solution)/shard_map/pallas_call | solution.py:296
  44.8 23.1 %all_to_all.15.every_ref.refs_9_ = f32[32,8,128]{2,1,0:T(8,128)S(1)} all-to-all(f32[32,8,128]{2,1,0:T(8,128)S(1)} %get-tuple-element.33), channel_id=1, replica_groups=mesh['z2'=2,'z1'=2,'z0'=2,'xh'=2,'xl'=2,'y2'=2,'y1'=2,'y0'=2,'c'=2] {'z2..., dimensions={0} | all-to-all | bytes 262144 | tf_op jit(solution)/shard_map/all_to_all | solution.py:270
  67.9 0.8 shard_map.80
  68.7 3.7 %collective-permute-start.6 = (f32[512,512]{1,0:T(8,128)S(1)}, f32[512,512]{1,0:T(8,128)S(1)}, u32[]{:S(2)}, u32[]{:S(2)}) collective-permute-start(f32[512,512]{1,0:T(8,128)S(1)} %get-tuple-element.36), channel_id=1, source_target_pairs={{0,1},{1,0},{2,3},{3,2},{4,5},{5,4},{6,7},{7,6},{8,9},{9,8},{10,11... | collective-permute-start | bytes 3145736 | tf_op jit(solution)/shard_map/ppermute | solution.py:250
  72.4 2.6 %shard_map.81 = (f32[512,512]{1,0:T(8,128)S(1)}, f32[256,512]{1,0:T(8,128)}) custom-call(f32[256,512]{1,0:T(8,128)S(1)} %shard_map.77.refs_0_, f32[256,512]{1,0:T(8,128)S(1)} %shard_map.78.refs_1_, f32[256,512]{1,0:T(8,128)S(1)} %collective-permute-done.4.refs_2_, f32[256,512]{1,0:T(8,128)S(1)} %collective-permute-done.5.refs_3_, ...), custom_call_target="tpu_custom_call" | custom-call | flops 1207959552 | bytes 4194304 | tf_op jit(solution)/shard_map/pallas_call | solution.py:305
  75.0 0.1 shard_map.82
  75.1 3.9 %all-to-all-start.2 = ((f32[32,8,512]{2,1,0:T(8,128)}), f32[32,8,512]{2,1,0:T(8,128)S(1)}, u32[]{:S(2)}, u32[]{:S(2)}) async-start(f32[32,8,512]{2,1,0:T(8,128)} %bitcast.1), calls=%async_computation.2 | async-start | bytes 1048576 | tf_op jit(solution)/shard_map/all_to_all | solution.py:270
  79.0 4.0 %collective-permute-start.7 = (f32[128,512]{1,0:T(8,128)S(1)}, f32[128,512]{1,0:T(8,128)S(1)}, u32[]{:S(2)}, u32[]{:S(2)}) collective-permute-start(f32[128,512]{1,0:T(8,128)S(1)} %get-tuple-element.39), channel_id=1, source_target_pairs={{0,32},{16,48},{32,0},{48,16},{1,33},{17,49},{33,1},{49,17},{2,34}... | collective-permute-start | bytes 786440 | tf_op jit(solution)/shard_map/ppermute | solution.py:254
  83.0 2.9 %collective-permute-start.8 = (f32[128,512]{1,0:T(8,128)S(1)}, f32[128,512]{1,0:T(8,128)S(1)}, u32[]{:S(2)}, u32[]{:S(2)}) collective-permute-start(f32[128,512]{1,0:T(8,128)S(1)} %get-tuple-element.40), channel_id=1, source_target_pairs={{0,16},{1,49},{16,32},{17,1},{32,48},{33,17},{48,0},{49,33},{2,18}... | collective-permute-start | bytes 786440 | tf_op jit(solution)/shard_map/ppermute | solution.py:259
  86.0 2.3 %collective-permute-start.9 = (f32[64,512]{1,0:T(8,128)S(1)}, f32[64,512]{1,0:T(8,128)S(1)}, u32[]{:S(2)}, u32[]{:S(2)}) collective-permute-start(f32[64,512]{1,0:T(8,128)S(1)} %get-tuple-element.42), channel_id=1, source_target_pairs={{0,48},{1,17},{16,0},{17,33},{32,16},{33,49},{48,32},{49,1},{2,50}... | collective-permute-start | bytes 393224 | tf_op jit(solution)/shard_map/ppermute | solution.py:259
  88.3 3.8 %collective-permute-start.10 = (f32[64,512]{1,0:T(8,128)S(1)}, f32[64,512]{1,0:T(8,128)S(1)}, u32[]{:S(2)}, u32[]{:S(2)}) collective-permute-start(f32[64,512]{1,0:T(8,128)S(1)} %get-tuple-element.43), channel_id=1, source_target_pairs={{0,50},{1,19},{2,48},{3,17},{16,2},{17,35},{18,0},{19,33},{32,18},... | collective-permute-start | bytes 393224 | tf_op jit(solution)/shard_map/ppermute | solution.py:266
  92.1 0.0 collective-permute-done.7.right_ref
  92.1 3.0 %collective-permute-done.8.refs_1_ = f32[128,512]{1,0:T(8,128)S(1)} collective-permute-done((f32[128,512]{1,0:T(8,128)S(1)}, f32[128,512]{1,0:T(8,128)S(1)}, u32[]{:S(2)}, u32[]{:S(2)}) %collective-permute-start.8) | collective-permute-done | bytes 262176 | tf_op jit(solution)/shard_map/ppermute | solution.py:259
  95.1 3.1 %collective-permute-start.11 = (f32[64,512]{1,0:T(8,128)S(1)}, f32[64,512]{1,0:T(8,128)S(1)}, u32[]{:S(2)}, u32[]{:S(2)}) collective-permute-start(f32[64,512]{1,0:T(8,128)S(1)} %get-tuple-element.44), channel_id=1, source_target_pairs={{0,2},{2,0},{1,3},{3,1},{4,6},{6,4},{5,7},{7,5},{8,10},{10,8},{9,1... | collective-permute-start | bytes 393224 | tf_op jit(solution)/shard_map/ppermute | solution.py:250
  98.2 3.7 %collective-permute-done.11.refs_3_ = f32[64,512]{1,0:T(8,128)S(1)} collective-permute-done((f32[64,512]{1,0:T(8,128)S(1)}, f32[64,512]{1,0:T(8,128)S(1)}, u32[]{:S(2)}, u32[]{:S(2)}) %collective-permute-start.11) | collective-permute-done | bytes 131104 | tf_op jit(solution)/shard_map/ppermute | solution.py:250
  101.9 0.0 all-to-all-done.2.refs_4_
  101.9 0.7 shard_map.85
  (8 shorter events, 0.2 us)
Async XLA Ops:
  2.4 18.9 %collective-permute-start = (f32[64,512]{1,0:T(8,128)S(1)}, f32[64,512]{1,0:T(8,128)S(1)}, u32[]{:S(2)}, u32[]{:S(2)}) collective-permute-start(f32[64,512]{1,0:T(8,128)S(1)} %get-tuple-element.27.refs_0_), channel_id=1, source_target_pairs={{0,2},{2,0},{1,3},{3,1},{4,6},{6,4},{5,7},{7,5},{8,10},{10,8},{9,1... | collective-permute-start | bytes 393224 | tf_op jit(solution)/shard_map/ppermute | solution.py:250
  6.4 36.5 %all-to-all-start = ((f32[32,8,512]{2,1,0:T(8,128)}), f32[32,8,512]{2,1,0:T(8,128)S(1)}, u32[]{:S(2)}, u32[]{:S(2)}) async-start(f32[32,8,512]{2,1,0:T(8,128)} %get-tuple-element.28), calls=%async_computation | async-start | bytes 1048576 | tf_op jit(solution)/shard_map/all_to_all | solution.py:270
  21.3 10.0 %collective-permute-start.1 = (f32[128,512]{1,0:T(8,128)S(1)}, f32[128,512]{1,0:T(8,128)S(1)}, u32[]{:S(2)}, u32[]{:S(2)}) collective-permute-start(f32[128,512]{1,0:T(8,128)S(1)} %shard_map.76.refs_0_), channel_id=1, source_target_pairs={{0,32},{16,48},{32,0},{48,16},{1,33},{17,49},{33,1},{49,17},{2,34}... | collective-permute-start | bytes 786440 | tf_op jit(solution)/shard_map/ppermute | solution.py:254
  25.9 10.8 %collective-permute-start.3 = (f32[128,512]{1,0:T(8,128)S(1)}, f32[128,512]{1,0:T(8,128)S(1)}, u32[]{:S(2)}, u32[]{:S(2)}) collective-permute-start(f32[128,512]{1,0:T(8,128)S(1)} %shard_map.76.refs_0_), channel_id=1, source_target_pairs={{0,16},{1,49},{16,32},{17,1},{32,48},{33,17},{48,0},{49,33},{2,18}... | collective-permute-start | bytes 786440 | tf_op jit(solution)/shard_map/ppermute | solution.py:259
  28.7 10.3 %collective-permute-start.2 = (f32[128,512]{1,0:T(8,128)S(1)}, f32[128,512]{1,0:T(8,128)S(1)}, u32[]{:S(2)}, u32[]{:S(2)}) collective-permute-start(f32[128,512]{1,0:T(8,128)S(1)} %shard_map.76.refs_0_), channel_id=1, source_target_pairs={{0,48},{1,17},{16,0},{17,33},{32,16},{33,49},{48,32},{49,1},{2,50}... | collective-permute-start | bytes 786440 | tf_op jit(solution)/shard_map/ppermute | solution.py:259
  31.3 9.8 %collective-permute-start.4 = (f32[256,512]{1,0:T(8,128)S(1)}, f32[256,512]{1,0:T(8,128)S(1)}, u32[]{:S(2)}, u32[]{:S(2)}) collective-permute-start(f32[256,512]{1,0:T(8,128)S(1)} %shard_map.77.refs_0_), channel_id=1, source_target_pairs={{0,1},{1,0},{2,3},{3,2},{4,5},{5,4},{6,7},{7,6},{8,9},{9,8},{10,11... | collective-permute-start | bytes 1572872 | tf_op jit(solution)/shard_map/ppermute | solution.py:250
  39.1 3.8 %collective-permute-start.5 = (f32[256,512]{1,0:T(8,128)S(1)}, f32[256,512]{1,0:T(8,128)S(1)}, u32[]{:S(2)}, u32[]{:S(2)}) collective-permute-start(f32[256,512]{1,0:T(8,128)S(1)} %shard_map.78.refs_1_), channel_id=1, source_target_pairs={{0,1},{1,0},{2,3},{3,2},{4,5},{5,4},{6,7},{7,6},{8,9},{9,8},{10,11... | collective-permute-start | bytes 1572872 | tf_op jit(solution)/shard_map/ppermute | solution.py:250
  68.7 6.3 %collective-permute-start.6 = (f32[512,512]{1,0:T(8,128)S(1)}, f32[512,512]{1,0:T(8,128)S(1)}, u32[]{:S(2)}, u32[]{:S(2)}) collective-permute-start(f32[512,512]{1,0:T(8,128)S(1)} %get-tuple-element.36), channel_id=1, source_target_pairs={{0,1},{1,0},{2,3},{3,2},{4,5},{5,4},{6,7},{7,6},{8,9},{9,8},{10,11... | collective-permute-start | bytes 3145736 | tf_op jit(solution)/shard_map/ppermute | solution.py:250
  75.1 26.8 %all-to-all-start.2 = ((f32[32,8,512]{2,1,0:T(8,128)}), f32[32,8,512]{2,1,0:T(8,128)S(1)}, u32[]{:S(2)}, u32[]{:S(2)}) async-start(f32[32,8,512]{2,1,0:T(8,128)} %bitcast.1), calls=%async_computation.2 | async-start | bytes 1048576 | tf_op jit(solution)/shard_map/all_to_all | solution.py:270
  79.0 13.1 %collective-permute-start.7 = (f32[128,512]{1,0:T(8,128)S(1)}, f32[128,512]{1,0:T(8,128)S(1)}, u32[]{:S(2)}, u32[]{:S(2)}) collective-permute-start(f32[128,512]{1,0:T(8,128)S(1)} %get-tuple-element.39), channel_id=1, source_target_pairs={{0,32},{16,48},{32,0},{48,16},{1,33},{17,49},{33,1},{49,17},{2,34}... | collective-permute-start | bytes 786440 | tf_op jit(solution)/shard_map/ppermute | solution.py:254
  83.0 12.1 %collective-permute-start.8 = (f32[128,512]{1,0:T(8,128)S(1)}, f32[128,512]{1,0:T(8,128)S(1)}, u32[]{:S(2)}, u32[]{:S(2)}) collective-permute-start(f32[128,512]{1,0:T(8,128)S(1)} %get-tuple-element.40), channel_id=1, source_target_pairs={{0,16},{1,49},{16,32},{17,1},{32,48},{33,17},{48,0},{49,33},{2,18}... | collective-permute-start | bytes 786440 | tf_op jit(solution)/shard_map/ppermute | solution.py:259
  86.0 12.2 %collective-permute-start.9 = (f32[64,512]{1,0:T(8,128)S(1)}, f32[64,512]{1,0:T(8,128)S(1)}, u32[]{:S(2)}, u32[]{:S(2)}) collective-permute-start(f32[64,512]{1,0:T(8,128)S(1)} %get-tuple-element.42), channel_id=1, source_target_pairs={{0,48},{1,17},{16,0},{17,33},{32,16},{33,49},{48,32},{49,1},{2,50}... | collective-permute-start | bytes 393224 | tf_op jit(solution)/shard_map/ppermute | solution.py:259
  88.3 9.9 %collective-permute-start.10 = (f32[64,512]{1,0:T(8,128)S(1)}, f32[64,512]{1,0:T(8,128)S(1)}, u32[]{:S(2)}, u32[]{:S(2)}) collective-permute-start(f32[64,512]{1,0:T(8,128)S(1)} %get-tuple-element.43), channel_id=1, source_target_pairs={{0,50},{1,19},{2,48},{3,17},{16,2},{17,35},{18,0},{19,33},{32,18},... | collective-permute-start | bytes 393224 | tf_op jit(solution)/shard_map/ppermute | solution.py:266
  95.1 6.8 %collective-permute-start.11 = (f32[64,512]{1,0:T(8,128)S(1)}, f32[64,512]{1,0:T(8,128)S(1)}, u32[]{:S(2)}, u32[]{:S(2)}) collective-permute-start(f32[64,512]{1,0:T(8,128)S(1)} %get-tuple-element.44), channel_id=1, source_target_pairs={{0,2},{2,0},{1,3},{3,1},{4,6},{6,4},{5,7},{7,5},{8,10},{10,8},{9,1... | collective-permute-start | bytes 393224 | tf_op jit(solution)/shard_map/ppermute | solution.py:250

commit v8 on v7

--- a/solution.py
+++ b/solution.py
@@ -213,10 +213,6 @@
     key_side(0, *given, out_ref, slopes)
     turn(*blocks, turned)
     query_side(slopes, other_slopes, turned, dq_ref)
-
-
-def add_two(left_ref, right_ref, out_ref):
-    out_ref[...] = left_ref[...] + right_ref[...]
 
 
 def add_ring(*refs):
@@ -322,8 +318,7 @@
     )(own, moved, dq)
     dq_parts = exchange(dq.reshape(QUERIES_IN, own_rows, 2 * wide), QUERY_GROUP)
     sides = (toward(left, -1), past(left_past, -1))
-    mine = call(add_two, pair_sum, 10**9, block)(mine, across(far))
-    near, beyond = call(add_ring, (block_sum,) * NEAR, 0, block)(mine, toward(right, 1))
+    near, beyond = call(add_ring, (block_sum,) * NEAR, 10**9, block)(mine, across(far), toward(right, 1))
     grad_keys, grad_values, attended, grad_queries = call(
         finish, (shape(F32, own_keys, wide),) * 2 + (shape(F32, own_rows, wide),) * 2, 0, block
     )(near, *sides, swap(beyond, PAIR), dq_parts)

time: 103 us -> 103 us (level)
  no operation moved by 1% of the time
where the time goes in v8:
time: 103 us
  starting transfers between devices  59.6 us (58%)
  blocking collectives  23.1 us (22%)
  waiting for transfers between devices  11.1 us (11%)
  Pallas kernels  8.03 us (8%)
    all_to_all x1, blocking collectives, exchange(): return lax.all_to_all(x, axes, 0, 0, tiled=True)  23.1 us
    all_to_all x2, starting transfers between devices, exchange(): return lax.all_to_all(x, axes, 0, 0, tiled=True)  18.7 us
    ppermute x5, starting transfers between devices, swap(): return lax.ppermute(x, axis, [(0, 1), (1, 0)])  17.9 us
    ppermute x4, starting transfers between devices, toward(): return lax.ppermute(x, RING + (CORE,), pairs)  10.6 us
    ppermute x2, starting transfers between devices, across(): lax.ppermute(x, RING, [(n, (n + AROUND // 2) % AROUND) for n in range(ARO...  8.66 us
    ppermute x4, waiting for transfers between devices, toward(): return lax.ppermute(x, RING + (CORE,), pairs)  5.57 us
    ppermute x5, waiting for transfers between devices, swap(): return lax.ppermute(x, axis, [(0, 1), (1, 0)])  5.53 us
    ppermute x1, starting transfers between devices, past(): return lax.ppermute(x, RING + (PAIR, CORE), pairs)  3.77 us
  transfers between devices with their start and end apart: 14, of which 5 were waited for; matrix products, arithmetic and copies ran while one was open for 0% of the time, Pallas kernels for 3%

profile of v8, /device:TPU:1, one launch (start us, length us, event | category | flops | bytes accessed | tf_op | source)
XLA Modules:
  0.0 102.6 jit_solution(15174032210639971253)
XLA Ops:
  0.6 1.7 %shard_map.75 = (f32[64,512]{1,0:T(8,128)S(1)}, f32[32,8,512]{2,1,0:T(8,128)}) custom-call(f32[8,256]{1,0:T(8,128)} %queries_ref.1, f32[8,256]{1,0:T(8,128)} %grad_ref.1, f32[64,256]{1,0:T(8,128)} %key_ref.1, f32[64,256]{1,0:T(8,128)} %value_ref.1), custom_call_target="tpu_custom_call" | custom-call | bytes 524288 | tf_op jit(solution)/shard_map/pallas_call | solution.py:274
  2.4 4.0 %collective-permute-start = (f32[64,512]{1,0:T(8,128)S(1)}, f32[64,512]{1,0:T(8,128)S(1)}, u32[]{:S(2)}, u32[]{:S(2)}) collective-permute-start(f32[64,512]{1,0:T(8,128)S(1)} %get-tuple-element.27.refs_0_), channel_id=1, source_target_pairs={{0,2},{2,0},{1,3},{3,1},{4,6},{6,4},{5,7},{7,5},{8,10},{10,8},{9,1... | collective-permute-start | bytes 393224 | tf_op jit(solution)/shard_map/ppermute | solution.py:246
  6.4 14.8 %all-to-all-start = ((f32[32,8,512]{2,1,0:T(8,128)}), f32[32,8,512]{2,1,0:T(8,128)S(1)}, u32[]{:S(2)}, u32[]{:S(2)}) async-start(f32[32,8,512]{2,1,0:T(8,128)} %get-tuple-element.28), calls=%async_computation | async-start | bytes 1048576 | tf_op jit(solution)/shard_map/all_to_all | solution.py:266
  21.3 4.7 %collective-permute-start.1 = (f32[128,512]{1,0:T(8,128)S(1)}, f32[128,512]{1,0:T(8,128)S(1)}, u32[]{:S(2)}, u32[]{:S(2)}) collective-permute-start(f32[128,512]{1,0:T(8,128)S(1)} %shard_map.76.refs_0_), channel_id=1, source_target_pairs={{0,32},{16,48},{32,0},{48,16},{1,33},{17,49},{33,1},{49,17},{2,34}... | collective-permute-start | bytes 786440 | tf_op jit(solution)/shard_map/ppermute | solution.py:250
  25.9 2.8 %collective-permute-start.3 = (f32[128,512]{1,0:T(8,128)S(1)}, f32[128,512]{1,0:T(8,128)S(1)}, u32[]{:S(2)}, u32[]{:S(2)}) collective-permute-start(f32[128,512]{1,0:T(8,128)S(1)} %shard_map.76.refs_0_), channel_id=1, source_target_pairs={{0,16},{1,49},{16,32},{17,1},{32,48},{33,17},{48,0},{49,33},{2,18}... | collective-permute-start | bytes 786440 | tf_op jit(solution)/shard_map/ppermute | solution.py:255
  28.7 2.5 %collective-permute-start.2 = (f32[128,512]{1,0:T(8,128)S(1)}, f32[128,512]{1,0:T(8,128)S(1)}, u32[]{:S(2)}, u32[]{:S(2)}) collective-permute-start(f32[128,512]{1,0:T(8,128)S(1)} %shard_map.76.refs_0_), channel_id=1, source_target_pairs={{0,48},{1,17},{16,0},{17,33},{32,16},{33,49},{48,32},{49,1},{2,50}... | collective-permute-start | bytes 786440 | tf_op jit(solution)/shard_map/ppermute | solution.py:255
  31.2 0.0 collective-permute-done.1.refs_1_
  31.3 5.2 %collective-permute-start.4 = (f32[256,512]{1,0:T(8,128)S(1)}, f32[256,512]{1,0:T(8,128)S(1)}, u32[]{:S(2)}, u32[]{:S(2)}) collective-permute-start(f32[256,512]{1,0:T(8,128)S(1)} %shard_map.77.refs_0_), channel_id=1, source_target_pairs={{0,1},{1,0},{2,3},{3,2},{4,5},{5,4},{6,7},{7,6},{8,9},{9,8},{10,11... | collective-permute-start | bytes 1572872 | tf_op jit(solution)/shard_map/ppermute | solution.py:246
  36.5 0.2 collective-permute-done.3.refs_1_
  36.7 2.3 %collective-permute-done.2.refs_0_ = f32[128,512]{1,0:T(8,128)S(1)} collective-permute-done((f32[128,512]{1,0:T(8,128)S(1)}, f32[128,512]{1,0:T(8,128)S(1)}, u32[]{:S(2)}, u32[]{:S(2)}) %collective-permute-start.2) | collective-permute-done | bytes 262176 | tf_op jit(solution)/shard_map/ppermute | solution.py:255
  39.1 2.0 %collective-permute-start.5 = (f32[256,512]{1,0:T(8,128)S(1)}, f32[256,512]{1,0:T(8,128)S(1)}, u32[]{:S(2)}, u32[]{:S(2)}) collective-permute-start(f32[256,512]{1,0:T(8,128)S(1)} %shard_map.78.refs_1_), channel_id=1, source_target_pairs={{0,1},{1,0},{2,3},{3,2},{4,5},{5,4},{6,7},{7,6},{8,9},{9,8},{10,11... | collective-permute-start | bytes 1572872 | tf_op jit(solution)/shard_map/ppermute | solution.py:246
  41.0 0.0 collective-permute-done.4.refs_2_
  41.1 1.8 %collective-permute-done.5.refs_3_ = f32[256,512]{1,0:T(8,128)S(1)} collective-permute-done((f32[256,512]{1,0:T(8,128)S(1)}, f32[256,512]{1,0:T(8,128)S(1)}, u32[]{:S(2)}, u32[]{:S(2)}) %collective-permute-start.5) | collective-permute-done | bytes 524320 | tf_op jit(solution)/shard_map/ppermute | solution.py:246
  42.9 0.0 all-to-all-done
  42.9 1.9 %shard_map.79 = (f32[1024,256]{1,0:T(8,128)S(1)}, f32[1024,256]{1,0:T(8,128)S(1)}, f32[1024,256]{1,0:T(8,128)S(1)}, f32[32,8,128]{2,1,0:T(8,128)S(1)}, f32[2,256]{1,0:T(2,128)S(1)}) custom-call(f32[256,512]{1,0:T(8,128)S(1)} %shard_map.77.refs_0_, f32[256,512]{1,0:T(8,128)S(1)} %shard_map.78.refs_1_, f32[256,512]{1,0:T(8,128)S(1)} %collective-permute-done.4.refs_2_, ...), custom_call_target="tpu_custom_call" | custom-call | flops 1207959552 | bytes 3145728 | tf_op jit(solution)/shard_map/pallas_call | solution.py:292
  44.8 23.1 %all_to_all.15.every_ref.refs_9_ = f32[32,8,128]{2,1,0:T(8,128)S(1)} all-to-all(f32[32,8,128]{2,1,0:T(8,128)S(1)} %get-tuple-element.33), channel_id=1, replica_groups=mesh['z2'=2,'z1'=2,'z0'=2,'xh'=2,'xl'=2,'y2'=2,'y1'=2,'y0'=2,'c'=2] {'z2..., dimensions={0} | all-to-all | bytes 262144 | tf_op jit(solution)/shard_map/all_to_all | solution.py:266
  67.9 0.8 shard_map.80
  68.7 3.7 %collective-permute-start.6 = (f32[512,512]{1,0:T(8,128)S(1)}, f32[512,512]{1,0:T(8,128)S(1)}, u32[]{:S(2)}, u32[]{:S(2)}) collective-permute-start(f32[512,512]{1,0:T(8,128)S(1)} %get-tuple-element.36), channel_id=1, source_target_pairs={{0,1},{1,0},{2,3},{3,2},{4,5},{5,4},{6,7},{7,6},{8,9},{9,8},{10,11... | collective-permute-start | bytes 3145736 | tf_op jit(solution)/shard_map/ppermute | solution.py:246
  72.4 2.6 %shard_map.81 = (f32[512,512]{1,0:T(8,128)S(1)}, f32[256,512]{1,0:T(8,128)}) custom-call(f32[256,512]{1,0:T(8,128)S(1)} %shard_map.77.refs_0_, f32[256,512]{1,0:T(8,128)S(1)} %shard_map.78.refs_1_, f32[256,512]{1,0:T(8,128)S(1)} %collective-permute-done.4.refs_2_, f32[256,512]{1,0:T(8,128)S(1)} %collective-permute-done.5.refs_3_, ...), custom_call_target="tpu_custom_call" | custom-call | flops 1207959552 | bytes 4194304 | tf_op jit(solution)/shard_map/pallas_call | solution.py:301
  75.0 0.1 shard_map.82
  75.1 3.9 %all-to-all-start.2 = ((f32[32,8,512]{2,1,0:T(8,128)}), f32[32,8,512]{2,1,0:T(8,128)S(1)}, u32[]{:S(2)}, u32[]{:S(2)}) async-start(f32[32,8,512]{2,1,0:T(8,128)} %bitcast.1), calls=%async_computation.2 | async-start | bytes 1048576 | tf_op jit(solution)/shard_map/all_to_all | solution.py:266
  79.0 4.0 %collective-permute-start.7 = (f32[128,512]{1,0:T(8,128)S(1)}, f32[128,512]{1,0:T(8,128)S(1)}, u32[]{:S(2)}, u32[]{:S(2)}) collective-permute-start(f32[128,512]{1,0:T(8,128)S(1)} %get-tuple-element.39), channel_id=1, source_target_pairs={{0,32},{16,48},{32,0},{48,16},{1,33},{17,49},{33,1},{49,17},{2,34}... | collective-permute-start | bytes 786440 | tf_op jit(solution)/shard_map/ppermute | solution.py:250
  83.0 2.9 %collective-permute-start.8 = (f32[128,512]{1,0:T(8,128)S(1)}, f32[128,512]{1,0:T(8,128)S(1)}, u32[]{:S(2)}, u32[]{:S(2)}) collective-permute-start(f32[128,512]{1,0:T(8,128)S(1)} %get-tuple-element.40), channel_id=1, source_target_pairs={{0,16},{1,49},{16,32},{17,1},{32,48},{33,17},{48,0},{49,33},{2,18}... | collective-permute-start | bytes 786440 | tf_op jit(solution)/shard_map/ppermute | solution.py:255
  86.0 2.3 %collective-permute-start.9 = (f32[64,512]{1,0:T(8,128)S(1)}, f32[64,512]{1,0:T(8,128)S(1)}, u32[]{:S(2)}, u32[]{:S(2)}) collective-permute-start(f32[64,512]{1,0:T(8,128)S(1)} %get-tuple-element.42), channel_id=1, source_target_pairs={{0,48},{1,17},{16,0},{17,33},{32,16},{33,49},{48,32},{49,1},{2,50}... | collective-permute-start | bytes 393224 | tf_op jit(solution)/shard_map/ppermute | solution.py:255
  88.3 3.8 %collective-permute-start.10 = (f32[64,512]{1,0:T(8,128)S(1)}, f32[64,512]{1,0:T(8,128)S(1)}, u32[]{:S(2)}, u32[]{:S(2)}) collective-permute-start(f32[64,512]{1,0:T(8,128)S(1)} %get-tuple-element.43), channel_id=1, source_target_pairs={{0,50},{1,19},{2,48},{3,17},{16,2},{17,35},{18,0},{19,33},{32,18},... | collective-permute-start | bytes 393224 | tf_op jit(solution)/shard_map/ppermute | solution.py:262
  92.1 0.0 collective-permute-done.7.refs_1_
  92.1 3.0 %collective-permute-done.8.refs_2_ = f32[128,512]{1,0:T(8,128)S(1)} collective-permute-done((f32[128,512]{1,0:T(8,128)S(1)}, f32[128,512]{1,0:T(8,128)S(1)}, u32[]{:S(2)}, u32[]{:S(2)}) %collective-permute-start.8) | collective-permute-done | bytes 262176 | tf_op jit(solution)/shard_map/ppermute | solution.py:255
  95.2 3.1 %collective-permute-start.11 = (f32[64,512]{1,0:T(8,128)S(1)}, f32[64,512]{1,0:T(8,128)S(1)}, u32[]{:S(2)}, u32[]{:S(2)}) collective-permute-start(f32[64,512]{1,0:T(8,128)S(1)} %get-tuple-element.44), channel_id=1, source_target_pairs={{0,2},{2,0},{1,3},{3,1},{4,6},{6,4},{5,7},{7,5},{8,10},{10,8},{9,1... | collective-permute-start | bytes 393224 | tf_op jit(solution)/shard_map/ppermute | solution.py:246
  98.2 0.0 collective-permute-done.9.refs_1_
  98.2 3.7 %collective-permute-done.11.refs_3_ = f32[64,512]{1,0:T(8,128)S(1)} collective-permute-done((f32[64,512]{1,0:T(8,128)S(1)}, f32[64,512]{1,0:T(8,128)S(1)}, u32[]{:S(2)}, u32[]{:S(2)}) %collective-permute-start.11) | collective-permute-done | bytes 131104 | tf_op jit(solution)/shard_map/ppermute | solution.py:246
  101.9 0.0 all-to-all-done.2.refs_4_
  101.9 0.7 shard_map.84
  (7 shorter events, 0.1 us)
Async XLA Ops:
  2.4 18.9 %collective-permute-start = (f32[64,512]{1,0:T(8,128)S(1)}, f32[64,512]{1,0:T(8,128)S(1)}, u32[]{:S(2)}, u32[]{:S(2)}) collective-permute-start(f32[64,512]{1,0:T(8,128)S(1)} %get-tuple-element.27.refs_0_), channel_id=1, source_target_pairs={{0,2},{2,0},{1,3},{3,1},{4,6},{6,4},{5,7},{7,5},{8,10},{10,8},{9,1... | collective-permute-start | bytes 393224 | tf_op jit(solution)/shard_map/ppermute | solution.py:246
  6.4 36.5 %all-to-all-start = ((f32[32,8,512]{2,1,0:T(8,128)}), f32[32,8,512]{2,1,0:T(8,128)S(1)}, u32[]{:S(2)}, u32[]{:S(2)}) async-start(f32[32,8,512]{2,1,0:T(8,128)} %get-tuple-element.28), calls=%async_computation | async-start | bytes 1048576 | tf_op jit(solution)/shard_map/all_to_all | solution.py:266
  21.3 10.0 %collective-permute-start.1 = (f32[128,512]{1,0:T(8,128)S(1)}, f32[128,512]{1,0:T(8,128)S(1)}, u32[]{:S(2)}, u32[]{:S(2)}) collective-permute-start(f32[128,512]{1,0:T(8,128)S(1)} %shard_map.76.refs_0_), channel_id=1, source_target_pairs={{0,32},{16,48},{32,0},{48,16},{1,33},{17,49},{33,1},{49,17},{2,34}... | collective-permute-start | bytes 786440 | tf_op jit(solution)/shard_map/ppermute | solution.py:250
  25.9 10.8 %collective-permute-start.3 = (f32[128,512]{1,0:T(8,128)S(1)}, f32[128,512]{1,0:T(8,128)S(1)}, u32[]{:S(2)}, u32[]{:S(2)}) collective-permute-start(f32[128,512]{1,0:T(8,128)S(1)} %shard_map.76.refs_0_), channel_id=1, source_target_pairs={{0,16},{1,49},{16,32},{17,1},{32,48},{33,17},{48,0},{49,33},{2,18}... | collective-permute-start | bytes 786440 | tf_op jit(solution)/shard_map/ppermute | solution.py:255
  28.7 10.3 %collective-permute-start.2 = (f32[128,512]{1,0:T(8,128)S(1)}, f32[128,512]{1,0:T(8,128)S(1)}, u32[]{:S(2)}, u32[]{:S(2)}) collective-permute-start(f32[128,512]{1,0:T(8,128)S(1)} %shard_map.76.refs_0_), channel_id=1, source_target_pairs={{0,48},{1,17},{16,0},{17,33},{32,16},{33,49},{48,32},{49,1},{2,50}... | collective-permute-start | bytes 786440 | tf_op jit(solution)/shard_map/ppermute | solution.py:255
  31.3 9.8 %collective-permute-start.4 = (f32[256,512]{1,0:T(8,128)S(1)}, f32[256,512]{1,0:T(8,128)S(1)}, u32[]{:S(2)}, u32[]{:S(2)}) collective-permute-start(f32[256,512]{1,0:T(8,128)S(1)} %shard_map.77.refs_0_), channel_id=1, source_target_pairs={{0,1},{1,0},{2,3},{3,2},{4,5},{5,4},{6,7},{7,6},{8,9},{9,8},{10,11... | collective-permute-start | bytes 1572872 | tf_op jit(solution)/shard_map/ppermute | solution.py:246
  39.1 3.8 %collective-permute-start.5 = (f32[256,512]{1,0:T(8,128)S(1)}, f32[256,512]{1,0:T(8,128)S(1)}, u32[]{:S(2)}, u32[]{:S(2)}) collective-permute-start(f32[256,512]{1,0:T(8,128)S(1)} %shard_map.78.refs_1_), channel_id=1, source_target_pairs={{0,1},{1,0},{2,3},{3,2},{4,5},{5,4},{6,7},{7,6},{8,9},{9,8},{10,11... | collective-permute-start | bytes 1572872 | tf_op jit(solution)/shard_map/ppermute | solution.py:246
  68.7 6.3 %collective-permute-start.6 = (f32[512,512]{1,0:T(8,128)S(1)}, f32[512,512]{1,0:T(8,128)S(1)}, u32[]{:S(2)}, u32[]{:S(2)}) collective-permute-start(f32[512,512]{1,0:T(8,128)S(1)} %get-tuple-element.36), channel_id=1, source_target_pairs={{0,1},{1,0},{2,3},{3,2},{4,5},{5,4},{6,7},{7,6},{8,9},{9,8},{10,11... | collective-permute-start | bytes 3145736 | tf_op jit(solution)/shard_map/ppermute | solution.py:246
  75.1 26.8 %all-to-all-start.2 = ((f32[32,8,512]{2,1,0:T(8,128)}), f32[32,8,512]{2,1,0:T(8,128)S(1)}, u32[]{:S(2)}, u32[]{:S(2)}) async-start(f32[32,8,512]{2,1,0:T(8,128)} %bitcast.1), calls=%async_computation.2 | async-start | bytes 1048576 | tf_op jit(solution)/shard_map/all_to_all | solution.py:266
  79.0 13.1 %collective-permute-start.7 = (f32[128,512]{1,0:T(8,128)S(1)}, f32[128,512]{1,0:T(8,128)S(1)}, u32[]{:S(2)}, u32[]{:S(2)}) collective-permute-start(f32[128,512]{1,0:T(8,128)S(1)} %get-tuple-element.39), channel_id=1, source_target_pairs={{0,32},{16,48},{32,0},{48,16},{1,33},{17,49},{33,1},{49,17},{2,34}... | collective-permute-start | bytes 786440 | tf_op jit(solution)/shard_map/ppermute | solution.py:250
  83.0 12.1 %collective-permute-start.8 = (f32[128,512]{1,0:T(8,128)S(1)}, f32[128,512]{1,0:T(8,128)S(1)}, u32[]{:S(2)}, u32[]{:S(2)}) collective-permute-start(f32[128,512]{1,0:T(8,128)S(1)} %get-tuple-element.40), channel_id=1, source_target_pairs={{0,16},{1,49},{16,32},{17,1},{32,48},{33,17},{48,0},{49,33},{2,18}... | collective-permute-start | bytes 786440 | tf_op jit(solution)/shard_map/ppermute | solution.py:255
  86.0 12.3 %collective-permute-start.9 = (f32[64,512]{1,0:T(8,128)S(1)}, f32[64,512]{1,0:T(8,128)S(1)}, u32[]{:S(2)}, u32[]{:S(2)}) collective-permute-start(f32[64,512]{1,0:T(8,128)S(1)} %get-tuple-element.42), channel_id=1, source_target_pairs={{0,48},{1,17},{16,0},{17,33},{32,16},{33,49},{48,32},{49,1},{2,50}... | collective-permute-start | bytes 393224 | tf_op jit(solution)/shard_map/ppermute | solution.py:255
  88.3 9.9 %collective-permute-start.10 = (f32[64,512]{1,0:T(8,128)S(1)}, f32[64,512]{1,0:T(8,128)S(1)}, u32[]{:S(2)}, u32[]{:S(2)}) collective-permute-start(f32[64,512]{1,0:T(8,128)S(1)} %get-tuple-element.43), channel_id=1, source_target_pairs={{0,50},{1,19},{2,48},{3,17},{16,2},{17,35},{18,0},{19,33},{32,18},... | collective-permute-start | bytes 393224 | tf_op jit(solution)/shard_map/ppermute | solution.py:262
  95.2 6.8 %collective-permute-start.11 = (f32[64,512]{1,0:T(8,128)S(1)}, f32[64,512]{1,0:T(8,128)S(1)}, u32[]{:S(2)}, u32[]{:S(2)}) collective-permute-start(f32[64,512]{1,0:T(8,128)S(1)} %get-tuple-element.44), channel_id=1, source_target_pairs={{0,2},{2,0},{1,3},{3,1},{4,6},{6,4},{5,7},{7,5},{8,10},{10,8},{9,1... | collective-permute-start | bytes 393224 | tf_op jit(solution)/shard_map/ppermute | solution.py:246
